TPU v7x, 256 devices: a whole 4x4x8 slice. The times are simulated.
256 devices in a mesh: dom: 32 (over z_lo, y, core), rows: 8 (over x, z_hi).
Axes of the slice: x: 4, y: 4, z: 8 (z_hi: 2, z_lo: 4; z = z_hi * 4 + z_lo), core: 2. Of those that a mesh axis runs over, the one named last changes fastest.
Arguments:
- depth: float32 [64, 128, 1536], P('dom', 'rows'), may hold values from 0.05 to 1.5
- x_flow: float32 [64, 128, 1536], P('dom', 'rows'), may hold values from -2 to 2
- y_flow: float32 [64, 128, 1536], P('dom', 'rows'), may hold values from -2 to 2
- elevation: float32 [128, 1536], P('rows'), may hold values from 0 to 0.5
- roughness: int32 [128, 1536], P('rows'), may hold values from 0 to 7
- wet: int32 [64, 128, 1536], P('dom', 'rows'), may hold values 0 or 1
- ancestors: int32 [64], P('dom'), may hold values from 0 to 63, as said below
Outputs:
- depth_out: float32 [64, 128, 1536], P('dom', 'rows')
- x_out: float32 [64, 128, 1536], P('dom', 'rows')
- y_out: float32 [64, 128, 1536], P('dom', 'rows')
Inputs may be any that keep to these rules, and one draw needn't show every extreme that they name: `ancestors`: duplicates allowed; some particle names ancestor 0 and some ancestor 64 - 1.
All inputs are finite; a program needn't handle non-finite values. No bound on the sum of `wet` on one device may be relied on, other than what follows from the above.
Results may differ from a plain program's by a relative error of at most 0.00002.
Values sent between devices are 32-bit elements; how exact they have to be, the bound alone decides.
No kernel may reach another device: no remote copies, remote signals or barrier semaphores. Data moves between devices by JAX's collectives and lax.ppermute only.
A program may use at most 128 MiB of HBM per device.

v0:
```python
import jax
import jax.numpy as jnp
from jax import lax
from jax.experimental import pallas as pl
from jax.experimental.pallas import tpu as pltpu
from jax.sharding import PartitionSpec as P

GDT = 9.81 * 1.0
SPACING = 10.0
RATIO = 1.0 / 10.0
MIN_DEPTH = 0.05
MANNING = (0.02, 0.025, 0.03, 0.035, 0.045, 0.06, 0.08, 0.1)
ROWS, COLS, HALF = 16, 1536, 8
NT = COLS // 128
F32 = jnp.float32

PER = 9
ITEMS = [(d, f, 3 * z + t) for z in range(4) for d in range(4) for f in range(3) for t in range(3)]
AT = {item: n for n, item in enumerate(ITEMS)}
STEP_Z = (0, 2, 3, 1)
STEP_Y = (0, 2, 1, 3)
VMEM = pl.BlockSpec(memory_space=pltpu.VMEM)
SMEM = pl.BlockSpec(memory_space=pltpu.SMEM)
HBM = pl.BlockSpec(memory_space=pltpu.HBM)


def place():
    dom = lax.axis_index("dom")
    return dom >> 3, (dom >> 1) & 3, dom & 1


def flux(q, eta_a, eta_b, bed, fric):
    he = jnp.maximum(jnp.maximum(eta_a, eta_b) - bed, MIN_DEPTH)
    numer = q - (GDT / SPACING) * he * (eta_b - eta_a)
    denom = 1.0 + fric * jnp.abs(q) * jnp.exp2((-7.0 / 3.0) * jnp.log2(he))
    return numer / denom


def friction(rough):
    total = jnp.zeros(rough.shape, F32)
    for klass, n in enumerate(MANNING):
        total = jnp.where(rough == klass, F32(GDT * (n * n)), total)
    return total


def right_of(v):
    return pltpu.roll(v, COLS - 1, 1)


def left_of(v):
    return pltpu.roll(v, 1, 1)


def below(v):
    return pltpu.roll(v, v.shape[0] - 1, 0)


def above(v):
    return pltpu.roll(v, 1, 0)


def x_faces(q, eta, bed_x, fric):
    last = lax.broadcasted_iota(jnp.int32, q.shape, 1) == COLS - 1
    return jnp.where(last, 0.0, flux(q, eta, right_of(eta), bed_x, fric))


def chunk_at(z, y, c, outer, inner):
    return jnp.where(
        c == 0,
        (z ^ STEP_Z[outer]) * 4 + (y ^ STEP_Y[inner]),
        (z ^ STEP_Z[inner]) * 4 + (y ^ STEP_Y[outer]),
    )


def step_of(steps, distance):
    found = jnp.int32(0)
    for k in range(1, 4):
        found = jnp.where(distance == steps[k], k, found)
    return found


def first_kernel(
    depth_in, xf_in, yf_in, wet_in, elev_in, rough_in, anc_in, keep, give, kept, given, terrain,
    depth, xf, yf, wet, elev, rough, anc, sems,
):
    pairs = zip(
        (elev_in, rough_in, depth_in, wet_in, xf_in, yf_in, anc_in), (elev, rough, depth, wet, xf, yf, anc)
    )
    copies = [pltpu.make_async_copy(src, dst, sems.at[n]) for n, (src, dst) in enumerate(pairs)]
    for copy in copies:
        copy.start()
    for copy in copies:
        copy.wait()
    _, _, c = place()
    top = c == 0
    bed = elev[...]
    fric = friction(rough[...])
    bed_x = jnp.maximum(bed, right_of(bed))
    bed_y = jnp.maximum(bed, below(bed))
    end = ROWS - 1
    last_row = lax.broadcasted_iota(jnp.int32, (ROWS, COLS), 0) == end
    terrain[0] = jnp.where(top, bed[:HALF], bed[HALF:])
    terrain[1] = jnp.where(top, fric[:HALF], fric[HALF:])
    terrain[2] = jnp.zeros((HALF, COLS), F32)
    terrain[2, 0:1, :] = jnp.where(top, bed[HALF : HALF + 1], bed[HALF - 1 : HALF])
    terrain[2, 1:2, :] = jnp.where(top, fric[HALF : HALF + 1], fric[HALF - 1 : HALF])
    lane = lax.broadcasted_iota(jnp.int32, (1, COLS), 1)
    at = 2 * lax.axis_index("dom")
    names = jnp.where(lane == at, anc[0].astype(F32), 0.0) + jnp.where(lane == at + 1, anc[1].astype(F32), 0.0)
    kept[6] = jnp.zeros((HALF, COLS), F32)
    given[6] = jnp.zeros((HALF, COLS), F32)
    kept[6, 4:5, :] = names
    given[6, 4:5, :] = names

    def edge(row, upper, lower):
        keep[row : row + 1, :] = jnp.where(top, upper, lower)
        give[row : row + 1, :] = jnp.where(top, lower, upper)

    zero = jnp.zeros((1, COLS), F32)
    edge(6, bed[:1], bed[end:])
    edge(7, fric[:1], fric[end:])
    for p in range(2):
        h0 = depth[p] * wet[p].astype(F32)
        qx, qy = xf[p], yf[p]
        edge(p, h0[:1], h0[end:])
        edge(4 + p, zero, qy[end:])
        eta = bed + h0
        qx = x_faces(qx, eta, bed_x, fric)
        qy = jnp.where(last_row, 0.0, flux(qy, eta, below(eta), bed_y, fric))
        h1 = h0 + RATIO * ((left_of(qx) - qx) + (above(qy) - qy))
        edge(2 + p, h1[:1], h1[end:])
        for f, v in enumerate((h1, qx, qy)):
            kept[3 * p + f] = jnp.where(top, v[:HALF], v[HALF:])
            given[3 * p + f] = jnp.where(top, v[HALF:], v[:HALF])
        kept[6, p : p + 1, :] = jnp.where(top, h1[HALF : HALF + 1], h1[HALF - 1 : HALF])
        given[6, p : p + 1, :] = jnp.where(top, h1[HALF - 1 : HALF], h1[HALF : HALF + 1])
        kept[6, 2 + p : 3 + p, :] = jnp.where(top, zero, qy[HALF - 1 : HALF])
        given[6, 2 + p : 3 + p, :] = jnp.where(top, qy[HALF - 1 : HALF], zero)


def second_kernel(own, far, terrain, mine, next_slab, o0, o1, o2, o3, rows, packed):
    z, y, c = place()
    top = c == 0
    slab = lax.axis_index("rows")
    bed, fric = terrain[0], terrain[1]
    bed_in, fric_in = terrain[2, 0:1, :], terrain[2, 1:2, :]
    row = lax.broadcasted_iota(jnp.int32, (HALF, COLS), 0)
    first, last = row == 0, row == HALF - 1
    at_edge = jnp.where(top, 0, HALF - 1)
    lower_edge = jnp.where(top, -1, HALF - 1)
    grid_end = jnp.where(slab == 7, lower_edge, -1)

    def rows_of(n, a, b):
        rows[n] = jnp.zeros((HALF, COLS), F32)
        rows[n, 0:2, :] = a
        rows[n, 2:4, :] = b
        return rows[n]

    in_h = rows_of(0, own[6, 0:2, :], far[6, 0:2, :])
    in_q = rows_of(1, own[6, 2:4, :], far[6, 2:4, :])
    out_h0 = rows_of(2, next_slab[8:10, :], next_slab[0:2, :])
    out_h1 = rows_of(3, next_slab[10:12, :], next_slab[2:4, :])
    out_q = rows_of(4, next_slab[12:14, :], next_slab[4:6, :])
    my_h = rows_of(5, mine[0:2, :], mine[8:10, :])
    my_q = rows_of(6, mine[4:6, :], mine[12:14, :])
    bed_out, fric_out = next_slab[6:7, :], next_slab[7:8, :]
    bed_mine = jnp.where(top, bed[:1], bed[HALF - 1 :])
    eta_mine, eta_out = bed_mine + my_h, bed_out + out_h0
    q1 = flux(
        jnp.where(top, out_q, my_q),
        jnp.where(top, eta_out, eta_mine),
        jnp.where(top, eta_mine, eta_out),
        jnp.maximum(bed_mine, bed_out),
        jnp.where(top, fric_out, fric[HALF - 1 :]),
    )
    q1 = jnp.where(jnp.where(top, slab, 7 - slab) == 0, 0.0, q1)
    out_h = out_h1 + jnp.where(top, -RATIO, RATIO) * q1
    bed_up, fric_up = jnp.where(top, bed_out, bed_in), jnp.where(top, fric_out, fric_in)
    bed_dn = jnp.where(top, bed_in, bed_out)
    eta_up = bed_up + jnp.where(top, out_h, in_h)
    eta_dn = bed_dn + jnp.where(top, in_h, out_h)
    q_up = jnp.where(top, q1, in_q)
    levels = []
    rows[7] = jnp.zeros((HALF, COLS), F32)
    for p in range(4):
        ref, n = (own, 3 * p) if p < 2 else (far, 3 * p - 6)
        q = q1[p : p + 1]
        h1 = ref[n] + jnp.where(row == at_edge, jnp.where(top, RATIO, -RATIO) * q, 0.0)
        qy1 = jnp.where(row == lower_edge, q, ref[n + 2])
        rows[7, p : p + 1, :] = bed[:1] + h1[:1]
        levels.append((h1, ref[n + 1], qy1))
    q2 = flux(q_up, eta_up, rows[7], jnp.maximum(bed_up, bed[:1]), fric_up)
    q2 = jnp.where(2 * slab + c == 0, 0.0, q2)
    bed_x = jnp.maximum(bed, right_of(bed))
    bed_y = jnp.maximum(bed, jnp.where(last, bed_dn, below(bed)))
    fields = []
    for p, (h1, qx, qy) in enumerate(levels):
        eta = bed + h1
        qx = x_faces(qx, eta, bed_x, fric)
        qy = flux(qy, eta, jnp.where(last, eta_dn[p : p + 1], below(eta)), bed_y, fric)
        qy = jnp.where(row == grid_end, 0.0, qy)
        over = jnp.where(first, q2[p : p + 1], above(qy))
        fields.append((h1 + RATIO * ((left_of(qx) - qx) + (over - qy)), qx, qy))
    low, even = masks()
    for f in range(3):
        for t in range(NT):
            a = [fields[p][f][:, 128 * t : 128 * t + 128] for p in range(4)]
            b0, b2 = jnp.where(low, a[0], pltpu.roll(a[2], 4, 0)), jnp.where(low, pltpu.roll(a[0], 4, 0), a[2])
            b1, b3 = jnp.where(low, a[1], pltpu.roll(a[3], 4, 0)), jnp.where(low, pltpu.roll(a[1], 4, 0), a[3])
            pair = [
                jnp.where(even, b0, pltpu.roll(b1, 2, 0)),
                jnp.where(even, pltpu.roll(b0, 6, 0), b1),
                jnp.where(even, b2, pltpu.roll(b3, 2, 0)),
                jnp.where(even, pltpu.roll(b2, 6, 0), b3),
            ]
            for d in range(4):
                n = AT[(d, f, t)]
                packed[n // PER, n % PER] = pair[d]
    names = own[6, 4:5, 0:128] + far[6, 4:5, 0:128]
    for k, out in enumerate((o0, o1, o2, o3)):
        for j in range(4):
            out[PER * j : PER * j + PER] = packed[chunk_at(z, y, c, k, j)]
        out[4 * PER] = jnp.zeros((8, 128), F32)
        out[4 * PER, 0:1, :] = names


def masks():
    sub = lax.broadcasted_iota(jnp.int32, (8, 128), 0)
    return sub < 4, (sub & 2) == 0


def select_kernel(anc, m0, m1, m2, m3, t0, t1, t2, t3, o0, o1, o2, o3, held):
    z, y, c = place()
    for n, refs in enumerate(((m0, m1, m2, m3), (t0, t1, t2, t3))):
        for j, ref in enumerate(refs):
            held[n, 4 * PER * j : 4 * PER * j + 4 * PER] = ref[: 4 * PER]
    for k, out in enumerate((o0, o1, o2, o3)):
        for j in range(4):
            at = chunk_at(z, y, c, k, j)
            dest = ((at >> 2) << 3) | ((at & 3) << 1) | c
            for u in range(2):
                name = anc[2 * dest + u]
                dz = step_of(STEP_Z, (name >> 4) ^ z)
                dy = step_of(STEP_Y, ((name >> 2) & 3) ^ y)
                for n in range(2):
                    core = c ^ n
                    base = jnp.where(core == 0, dy * 4 + dz, dz * 4 + dy) * PER
                    v = pl.multiple_of((((name >> 1) & 1) ^ core) * 4 + (name & 1) * 2, 2)
                    row = 4 * n + 2 * u
                    out[PER * j : PER * j + PER, row : row + 2, :] = held[n, pl.ds(base, PER), pl.ds(v, 2), :]


def last_kernel(f0, f1, f2, f3, ho, xo, yo, packed):
    z, y, c = place()
    low, even = masks()
    for j, ref in enumerate((f0, f1, f2, f3)):
        for k in range(4):
            packed[pl.ds(chunk_at(z, y, c, k, j) * PER, PER)] = ref[PER * k : PER * k + PER]
    for f, out in enumerate((ho, xo, yo)):
        for t in range(NT):
            cols = slice(128 * t, 128 * t + 128)
            pair = [packed[AT[(d, f, t)]] for d in range(4)]
            for n in range(2):
                rows = pl.ds(pl.multiple_of((c ^ n) * HALF, HALF), HALF)
                if n == 0:
                    b0 = jnp.where(low, pair[0], pltpu.roll(pair[2], 4, 0))
                    b1 = jnp.where(low, pair[1], pltpu.roll(pair[3], 4, 0))
                else:
                    b0 = jnp.where(low, pltpu.roll(pair[0], 4, 0), pair[2])
                    b1 = jnp.where(low, pltpu.roll(pair[1], 4, 0), pair[3])
                out[0, rows, cols] = jnp.where(even, b0, pltpu.roll(b1, 2, 0))
                out[1, rows, cols] = jnp.where(even, pltpu.roll(b0, 6, 0), b1)


def tiles(n):
    return jax.ShapeDtypeStruct((n, 8, 128), F32)


def params():
    return pltpu.CompilerParams(vmem_limit_bytes=32 * 1024 * 1024)


def outer_step(v, k):
    pairs = [(i, i ^ (STEP_Z[k] << 3 if i % 2 == 0 else STEP_Y[k] << 1)) for i in range(32)]
    return v if k == 0 else lax.ppermute(v, "dom", pairs)


def inner_step(v, k):
    pairs = [(i, i ^ (STEP_Y[k] << 1 if i % 2 == 0 else STEP_Z[k] << 3)) for i in range(32)]
    return v if k == 0 else lax.ppermute(v, "dom", pairs)


def other_core(v):
    return lax.ppermute(v, "dom", [(i, i ^ 1) for i in range(32)])


def next_slab(v):
    low = [((2 * chip + 1) * 8 + r, 2 * chip * 8 + r + 1) for chip in range(16) for r in range(7)]
    return lax.ppermute(v, ("dom", "rows"), low + [(b, a) for a, b in low])


def regroup(parts, count):
    return [jnp.concatenate([p[count * j : count * j + count] for p in parts]) for j in range(4)]


def shards(depth, x_flow, y_flow, elevation, roughness, wet, ancestors):
    state = jax.ShapeDtypeStruct((2, ROWS, COLS), F32)
    strip = jax.ShapeDtypeStruct((HALF, COLS), F32)
    halves = jax.ShapeDtypeStruct((7, HALF, COLS), F32)
    ground = jax.ShapeDtypeStruct((3, HALF, COLS), F32)
    args = (depth, x_flow, y_flow, wet, elevation, roughness, ancestors)
    keep, give, kept, given, terrain = pl.pallas_call(
        first_kernel,
        out_shape=[strip, strip, halves, halves, ground],
        in_specs=[HBM] * 7,
        out_specs=[VMEM] * 5,
        scratch_shapes=[pltpu.VMEM(v.shape, v.dtype) for v in args[:6]]
        + [pltpu.SMEM((2,), jnp.int32), pltpu.SemaphoreType.DMA((7,))],
        compiler_params=params(),
    )(*[pltpu.with_memory_space_constraint(v, pltpu.HBM) for v in args])
    mine = jnp.concatenate([keep, other_core(give)])
    far = other_core(given)
    arrived = next_slab(mine)
    parts = pl.pallas_call(
        second_kernel,
        out_shape=[tiles(4 * PER + 1)] * 4,
        in_specs=[VMEM] * 5,
        out_specs=[VMEM] * 4,
        scratch_shapes=[pltpu.VMEM((8, HALF, COLS), F32), pltpu.VMEM((16, PER, 8, 128), F32)],
        compiler_params=params(),
    )(kept, far, terrain, mine, arrived)
    parts = [outer_step(v, k) for k, v in enumerate(parts)]
    names = (parts[0][4 * PER] + parts[1][4 * PER]) + (parts[2][4 * PER] + parts[3][4 * PER])
    parts = [jnp.concatenate([v, names[None]]) for v in regroup(parts, PER)]
    parts = [inner_step(v, k) for k, v in enumerate(parts)]
    names = sum(v[4 * PER, 0, :64] for v in parts).astype(jnp.int32)
    others = [other_core(v) for v in parts]
    parts = pl.pallas_call(
        select_kernel,
        out_shape=[tiles(4 * PER)] * 4,
        in_specs=[SMEM] + [VMEM] * 8,
        out_specs=[VMEM] * 4,
        scratch_shapes=[pltpu.VMEM((2, 16 * PER, 8, 128), F32)],
        compiler_params=params(),
    )(names, *parts, *others)
    parts = [outer_step(v, k) for k, v in enumerate(parts)]
    parts = [inner_step(v, k) for k, v in enumerate(regroup(parts, PER))]
    return tuple(
        pl.pallas_call(
            last_kernel,
            out_shape=[state] * 3,
            in_specs=[VMEM] * 4,
            out_specs=[VMEM] * 3,
            scratch_shapes=[pltpu.VMEM((16 * PER, 8, 128), F32)],
            compiler_params=params(),
        )(*parts)
    )


def solution(mesh):
    wide = P("dom", "rows", None)
    in_specs = (wide, wide, wide, P("rows", None), P("rows", None), wide, P("dom"))
    return jax.shard_map(shards, mesh=mesh, in_specs=in_specs, out_specs=(wide, wide, wide), check_vma=False)
```

profile of v0, /device:TPU:6, one launch (start us, length us, event | category | flops | bytes accessed | tf_op | source)
XLA Modules:
  0.0 64.7 jit_solution(6198663743432021799)
XLA Ops:
  0.6 1.9 %shard_map.94 = (f32[8,1536]{1,0:T(8,128)S(1)}, f32[8,1536]{1,0:T(8,128)S(1)}, f32[7,8,1536]{2,1,0:T(8,128)S(1)}, f32[7,8,1536]{2,1,0:T(8,128)S(1)}, f32[3,8,1536]{2,1,0:T(8,128)S(1)}) custom-call(f32[2,16,1536]{2,1,0:T(8,128)} %depth_in.1, f32[2,16,1536]{2,1,0:T(8,128)} %xf_in.1, f32[2,16,1536]{2,1,0:T(8,128)} %yf_in.1, s32[2,16,1536]{2,1,0:T(8,128)} %wet_in.1, ...), custom_call_target="tpu_custom_call" | custom-call | tf_op jit(solution)/shard_map/pallas_call | solution.py:312
  2.7 0.5 collective-permute-start
  3.2 0.7 %collective-permute-done.1 = f32[8,1536]{1,0:T(8,128)S(1)} collective-permute-done((f32[8,1536]{1,0:T(8,128)S(1)}, f32[8,1536]{1,0:T(8,128)S(1)}, u32[]{:S(2)}, u32[]{:S(2)}) %collective-permute-start.1) | collective-permute-done | bytes 49184 | tf_op jit(solution)/shard_map/ppermute | solution.py:294
  3.9 9.1 %collective-permute-start.2 = (f32[16,1536]{1,0:T(8,128)S(1)}, f32[16,1536]{1,0:T(8,128)S(1)}, u32[]{:S(2)}, u32[]{:S(2)}) collective-permute-start(f32[16,1536]{1,0:T(8,128)S(1)} %constant_dynamic-update-slice_fusion.mine), channel_id=1, source_target_pairs={{8,1},{9,2},{10,3},{11,4},{12,5},{13,6},{14,7},{24,17},{25,18},{26... | collective-permute-start | bytes 294920 | tf_op jit(solution)/shard_map/ppermute | solution.py:299
  13.0 3.0 %collective-permute-done.2.next_slab = f32[16,1536]{1,0:T(8,128)S(1)} collective-permute-done((f32[16,1536]{1,0:T(8,128)S(1)}, f32[16,1536]{1,0:T(8,128)S(1)}, u32[]{:S(2)}, u32[]{:S(2)}) %collective-permute-start.2) | collective-permute-done | bytes 98336 | tf_op jit(solution)/shard_map/ppermute | solution.py:299
  16.1 0.7 %shard_map.95 = (f32[37,8,128]{2,1,0:T(8,128)S(1)}, f32[37,8,128]{2,1,0:T(8,128)S(1)}, f32[37,8,128]{2,1,0:T(8,128)S(1)}, f32[37,8,128]{2,1,0:T(8,128)S(1)}) custom-call(f32[7,8,1536]{2,1,0:T(8,128)S(1)} %get-tuple-element.16.own, f32[7,8,1536]{2,1,0:T(8,128)S(1)} %collective-permute-done.far, f32[3,8,1536]{2,1,0:T(8,128)S(1)} %get-tuple-element.18.terrain, ...), custom_call_target="tpu_custom_call" | custom-call | tf_op jit(solution)/shard_map/pallas_call | solution.py:324
  16.7 4.9 %collective-permute-start.3 = (f32[37,8,128]{2,1,0:T(8,128)S(1)}, f32[37,8,128]{2,1,0:T(8,128)S(1)}, u32[]{:S(2)}, u32[]{:S(2)}) collective-permute-start(f32[37,8,128]{2,1,0:T(8,128)S(1)} %get-tuple-element.22), channel_id=1, source_target_pairs={{0,128},{8,40},{16,144},{24,56},{32,160},{40,8},{48,176},{56,24},{... | collective-permute-start | bytes 454664 | tf_op jit(solution)/shard_map/ppermute | solution.py:285
  21.7 0.2 collective-permute-start.4
  21.8 0.5 collective-permute-start.5
  22.4 4.2 %collective-permute-done.3 = f32[37,8,128]{2,1,0:T(8,128)S(1)} collective-permute-done((f32[37,8,128]{2,1,0:T(8,128)S(1)}, f32[37,8,128]{2,1,0:T(8,128)S(1)}, u32[]{:S(2)}, u32[]{:S(2)}) %collective-permute-start.3) | collective-permute-done | bytes 151584 | tf_op jit(solution)/shard_map/ppermute | solution.py:285
  26.6 2.2 %collective-permute-done.4 = f32[37,8,128]{2,1,0:T(8,128)S(1)} collective-permute-done((f32[37,8,128]{2,1,0:T(8,128)S(1)}, f32[37,8,128]{2,1,0:T(8,128)S(1)}, u32[]{:S(2)}, u32[]{:S(2)}) %collective-permute-start.4) | collective-permute-done | bytes 151584 | tf_op jit(solution)/shard_map/ppermute | solution.py:285
  28.8 1.9 %collective-permute-done.5 = f32[37,8,128]{2,1,0:T(8,128)S(1)} collective-permute-done((f32[37,8,128]{2,1,0:T(8,128)S(1)}, f32[37,8,128]{2,1,0:T(8,128)S(1)}, u32[]{:S(2)}, u32[]{:S(2)}) %collective-permute-start.5) | collective-permute-done | bytes 151584 | tf_op jit(solution)/shard_map/ppermute | solution.py:285
  30.8 3.7 %collective-permute-start.6 = (f32[37,8,128]{2,1,0:T(8,128)S(1)}, f32[37,8,128]{2,1,0:T(8,128)S(1)}, u32[]{:S(2)}, u32[]{:S(2)}) collective-permute-start(f32[37,8,128]{2,1,0:T(8,128)S(1)} %get-tuple-element.63), channel_id=1, source_target_pairs={{0,32},{8,136},{16,48},{24,152},{32,0},{40,168},{48,16},{56,184},{... | collective-permute-start | bytes 454664 | tf_op jit(solution)/shard_map/ppermute | solution.py:290
  34.4 1.0 %collective-permute-start.8 = (f32[37,8,128]{2,1,0:T(8,128)S(1)}, f32[37,8,128]{2,1,0:T(8,128)S(1)}, u32[]{:S(2)}, u32[]{:S(2)}) collective-permute-start(f32[37,8,128]{2,1,0:T(8,128)S(1)} %get-tuple-element.64), channel_id=1, source_target_pairs={{0,48},{8,72},{16,32},{24,88},{32,16},{40,104},{48,0},{56,120},{64... | collective-permute-start | bytes 454664 | tf_op jit(solution)/shard_map/ppermute | solution.py:290
  35.5 2.2 %collective-permute-done.6.m1 = f32[37,8,128]{2,1,0:T(8,128)S(1)} collective-permute-done((f32[37,8,128]{2,1,0:T(8,128)S(1)}, f32[37,8,128]{2,1,0:T(8,128)S(1)}, u32[]{:S(2)}, u32[]{:S(2)}) %collective-permute-start.6) | collective-permute-done | bytes 151584 | tf_op jit(solution)/shard_map/ppermute | solution.py:290
  37.6 3.2 %collective-permute-done.8.m3 = f32[37,8,128]{2,1,0:T(8,128)S(1)} collective-permute-done((f32[37,8,128]{2,1,0:T(8,128)S(1)}, f32[37,8,128]{2,1,0:T(8,128)S(1)}, u32[]{:S(2)}, u32[]{:S(2)}) %collective-permute-start.8) | collective-permute-done | bytes 151584 | tf_op jit(solution)/shard_map/ppermute | solution.py:290
  40.8 0.5 collective-permute-start.11
  41.4 0.8 %collective-permute-done.12.t3 = f32[37,8,128]{2,1,0:T(8,128)S(1)} collective-permute-done((f32[37,8,128]{2,1,0:T(8,128)S(1)}, f32[37,8,128]{2,1,0:T(8,128)S(1)}, u32[]{:S(2)}, u32[]{:S(2)}) %collective-permute-start.12) | collective-permute-done | bytes 151584 | tf_op jit(solution)/shard_map/ppermute | solution.py:294
  42.2 0.2 collective-permute-done.11.t2
  42.4 1.1 %shard_map.96 = (f32[36,8,128]{2,1,0:T(8,128)S(1)}, f32[36,8,128]{2,1,0:T(8,128)S(1)}, f32[36,8,128]{2,1,0:T(8,128)S(1)}, f32[36,8,128]{2,1,0:T(8,128)S(1)}) custom-call(s32[64]{0:T(128)S(1)} %fusion.2.anc, f32[37,8,128]{2,1,0:T(8,128)S(1)} %get-tuple-element.29.m0, f32[37,8,128]{2,1,0:T(8,128)S(1)} %collective-permute-done.6.m1, ...), custom_call_target="tpu_custom_call" | custom-call | tf_op jit(solution)/shard_map/pallas_call | solution.py:338
  43.6 2.5 %collective-permute-start.13 = (f32[36,8,128]{2,1,0:T(8,128)S(1)}, f32[36,8,128]{2,1,0:T(8,128)S(1)}, u32[]{:S(2)}, u32[]{:S(2)}) collective-permute-start(f32[36,8,128]{2,1,0:T(8,128)S(1)} %get-tuple-element.26), channel_id=1, source_target_pairs={{0,128},{8,40},{16,144},{24,56},{32,160},{40,8},{48,176},{56,24},{... | collective-permute-start | bytes 442376 | tf_op jit(solution)/shard_map/ppermute | solution.py:285
  46.1 1.6 %collective-permute-start.14 = (f32[36,8,128]{2,1,0:T(8,128)S(1)}, f32[36,8,128]{2,1,0:T(8,128)S(1)}, u32[]{:S(2)}, u32[]{:S(2)}) collective-permute-start(f32[36,8,128]{2,1,0:T(8,128)S(1)} %get-tuple-element.27), channel_id=1, source_target_pairs={{0,192},{8,24},{16,208},{24,8},{32,224},{40,56},{48,240},{56,40},{... | collective-permute-start | bytes 442376 | tf_op jit(solution)/shard_map/ppermute | solution.py:285
  47.7 3.5 %collective-permute-done.13 = f32[36,8,128]{2,1,0:T(8,128)S(1)} collective-permute-done((f32[36,8,128]{2,1,0:T(8,128)S(1)}, f32[36,8,128]{2,1,0:T(8,128)S(1)}, u32[]{:S(2)}, u32[]{:S(2)}) %collective-permute-start.13) | collective-permute-done | bytes 147488 | tf_op jit(solution)/shard_map/ppermute | solution.py:285
  51.3 1.9 %collective-permute-done.14 = f32[36,8,128]{2,1,0:T(8,128)S(1)} collective-permute-done((f32[36,8,128]{2,1,0:T(8,128)S(1)}, f32[36,8,128]{2,1,0:T(8,128)S(1)}, u32[]{:S(2)}, u32[]{:S(2)}) %collective-permute-start.14) | collective-permute-done | bytes 147488 | tf_op jit(solution)/shard_map/ppermute | solution.py:285
  53.2 1.2 %collective-permute-done.15 = f32[36,8,128]{2,1,0:T(8,128)S(1)} collective-permute-done((f32[36,8,128]{2,1,0:T(8,128)S(1)}, f32[36,8,128]{2,1,0:T(8,128)S(1)}, u32[]{:S(2)}, u32[]{:S(2)}) %collective-permute-start.15) | collective-permute-done | bytes 147488 | tf_op jit(solution)/shard_map/ppermute | solution.py:285
  54.5 1.5 %collective-permute-start.16 = (f32[36,8,128]{2,1,0:T(8,128)S(1)}, f32[36,8,128]{2,1,0:T(8,128)S(1)}, u32[]{:S(2)}, u32[]{:S(2)}) collective-permute-start(f32[36,8,128]{2,1,0:T(8,128)S(1)} %pad_maximum_fusion.1), channel_id=1, source_target_pairs={{0,32},{8,136},{16,48},{24,152},{32,0},{40,168},{48,16},{56,184},{... | collective-permute-start | bytes 442376 | tf_op jit(solution)/shard_map/ppermute | solution.py:290
  56.0 1.4 %collective-permute-start.17 = (f32[36,8,128]{2,1,0:T(8,128)S(1)}, f32[36,8,128]{2,1,0:T(8,128)S(1)}, u32[]{:S(2)}, u32[]{:S(2)}) collective-permute-start(f32[36,8,128]{2,1,0:T(8,128)S(1)} %pad_maximum_fusion.2), channel_id=1, source_target_pairs={{0,16},{8,200},{16,0},{24,216},{32,48},{40,232},{48,32},{56,248},{... | collective-permute-start | bytes 442376 | tf_op jit(solution)/shard_map/ppermute | solution.py:290
  57.4 1.5 %collective-permute-start.18 = (f32[36,8,128]{2,1,0:T(8,128)S(1)}, f32[36,8,128]{2,1,0:T(8,128)S(1)}, u32[]{:S(2)}, u32[]{:S(2)}) collective-permute-start(f32[36,8,128]{2,1,0:T(8,128)S(1)} %pad_maximum_fusion.3), channel_id=1, source_target_pairs={{0,48},{8,72},{16,32},{24,88},{32,16},{40,104},{48,0},{56,120},{64... | collective-permute-start | bytes 442376 | tf_op jit(solution)/shard_map/ppermute | solution.py:290
  58.9 2.3 %collective-permute-done.16.f1 = f32[36,8,128]{2,1,0:T(8,128)S(1)} collective-permute-done((f32[36,8,128]{2,1,0:T(8,128)S(1)}, f32[36,8,128]{2,1,0:T(8,128)S(1)}, u32[]{:S(2)}, u32[]{:S(2)}) %collective-permute-start.16) | collective-permute-done | bytes 147488 | tf_op jit(solution)/shard_map/ppermute | solution.py:290
  61.2 0.7 %collective-permute-done.17.f2 = f32[36,8,128]{2,1,0:T(8,128)S(1)} collective-permute-done((f32[36,8,128]{2,1,0:T(8,128)S(1)}, f32[36,8,128]{2,1,0:T(8,128)S(1)}, u32[]{:S(2)}, u32[]{:S(2)}) %collective-permute-start.17) | collective-permute-done | bytes 147488 | tf_op jit(solution)/shard_map/ppermute | solution.py:290
  62.0 1.9 %collective-permute-done.18.f3 = f32[36,8,128]{2,1,0:T(8,128)S(1)} collective-permute-done((f32[36,8,128]{2,1,0:T(8,128)S(1)}, f32[36,8,128]{2,1,0:T(8,128)S(1)}, u32[]{:S(2)}, u32[]{:S(2)}) %collective-permute-start.18) | collective-permute-done | bytes 147488 | tf_op jit(solution)/shard_map/ppermute | solution.py:290
  63.8 0.9 %shard_map.97 = (f32[2,16,1536]{2,1,0:T(8,128)}, f32[2,16,1536]{2,1,0:T(8,128)}, f32[2,16,1536]{2,1,0:T(8,128)}) custom-call(f32[36,8,128]{2,1,0:T(8,128)S(1)} %pad_maximum_fusion.f0, f32[36,8,128]{2,1,0:T(8,128)S(1)} %collective-permute-done.16.f1, f32[36,8,128]{2,1,0:T(8,128)S(1)} %collective-permute-done.17.f2, f32[36,8,128]{2,1,0:T(8,128)S(1)} %collective-permute-done.18.f3), custom_call_target="tpu_custom_call" | custom-call | tf_op jit(solution)/shard_map/pallas_call | solution.py:349
  (27 shorter events, 0.3 us)
Async XLA Ops:
  2.6 1.3 %collective-permute-start.1 = (f32[8,1536]{1,0:T(8,128)S(1)}, f32[8,1536]{1,0:T(8,128)S(1)}, u32[]{:S(2)}, u32[]{:S(2)}) collective-permute-start(f32[8,1536]{1,0:T(8,128)S(1)} %get-tuple-element.20), channel_id=1, source_target_pairs={{0,8},{8,0},{16,24},{24,16},{32,40},{40,32},{48,56},{56,48},{64,72... | collective-permute-start | bytes 147464 | tf_op jit(solution)/shard_map/ppermute | solution.py:294
  2.7 13.4 %collective-permute-start = (f32[7,8,1536]{2,1,0:T(8,128)S(1)}, f32[7,8,1536]{2,1,0:T(8,128)S(1)}, u32[]{:S(2)}, u32[]{:S(2)}) collective-permute-start(f32[7,8,1536]{2,1,0:T(8,128)S(1)} %get-tuple-element.17), channel_id=1, source_target_pairs={{0,8},{8,0},{16,24},{24,16},{32,40},{40,32},{48,56},{56,48},{64,72... | collective-permute-start | bytes 1032200 | tf_op jit(solution)/shard_map/ppermute | solution.py:294
  3.9 12.2 %collective-permute-start.2 = (f32[16,1536]{1,0:T(8,128)S(1)}, f32[16,1536]{1,0:T(8,128)S(1)}, u32[]{:S(2)}, u32[]{:S(2)}) collective-permute-start(f32[16,1536]{1,0:T(8,128)S(1)} %constant_dynamic-update-slice_fusion.mine), channel_id=1, source_target_pairs={{8,1},{9,2},{10,3},{11,4},{12,5},{13,6},{14,7},{24,17},{25,18},{26... | collective-permute-start | bytes 294920 | tf_op jit(solution)/shard_map/ppermute | solution.py:299
  16.7 9.8 %collective-permute-start.3 = (f32[37,8,128]{2,1,0:T(8,128)S(1)}, f32[37,8,128]{2,1,0:T(8,128)S(1)}, u32[]{:S(2)}, u32[]{:S(2)}) collective-permute-start(f32[37,8,128]{2,1,0:T(8,128)S(1)} %get-tuple-element.22), channel_id=1, source_target_pairs={{0,128},{8,40},{16,144},{24,56},{32,160},{40,8},{48,176},{56,24},{... | collective-permute-start | bytes 454664 | tf_op jit(solution)/shard_map/ppermute | solution.py:285
  21.7 7.1 %collective-permute-start.4 = (f32[37,8,128]{2,1,0:T(8,128)S(1)}, f32[37,8,128]{2,1,0:T(8,128)S(1)}, u32[]{:S(2)}, u32[]{:S(2)}) collective-permute-start(f32[37,8,128]{2,1,0:T(8,128)S(1)} %get-tuple-element.23), channel_id=1, source_target_pairs={{0,192},{8,24},{16,208},{24,8},{32,224},{40,56},{48,240},{56,40},{... | collective-permute-start | bytes 454664 | tf_op jit(solution)/shard_map/ppermute | solution.py:285
  21.8 8.9 %collective-permute-start.5 = (f32[37,8,128]{2,1,0:T(8,128)S(1)}, f32[37,8,128]{2,1,0:T(8,128)S(1)}, u32[]{:S(2)}, u32[]{:S(2)}) collective-permute-start(f32[37,8,128]{2,1,0:T(8,128)S(1)} %get-tuple-element.24), channel_id=1, source_target_pairs={{0,64},{8,56},{16,80},{24,40},{32,96},{40,24},{48,112},{56,8},{64,... | collective-permute-start | bytes 454664 | tf_op jit(solution)/shard_map/ppermute | solution.py:285
  30.8 6.8 %collective-permute-start.6 = (f32[37,8,128]{2,1,0:T(8,128)S(1)}, f32[37,8,128]{2,1,0:T(8,128)S(1)}, u32[]{:S(2)}, u32[]{:S(2)}) collective-permute-start(f32[37,8,128]{2,1,0:T(8,128)S(1)} %get-tuple-element.63), channel_id=1, source_target_pairs={{0,32},{8,136},{16,48},{24,152},{32,0},{40,168},{48,16},{56,184},{... | collective-permute-start | bytes 454664 | tf_op jit(solution)/shard_map/ppermute | solution.py:290
  34.4 6.4 %collective-permute-start.8 = (f32[37,8,128]{2,1,0:T(8,128)S(1)}, f32[37,8,128]{2,1,0:T(8,128)S(1)}, u32[]{:S(2)}, u32[]{:S(2)}) collective-permute-start(f32[37,8,128]{2,1,0:T(8,128)S(1)} %get-tuple-element.64), channel_id=1, source_target_pairs={{0,48},{8,72},{16,32},{24,88},{32,16},{40,104},{48,0},{56,120},{64... | collective-permute-start | bytes 454664 | tf_op jit(solution)/shard_map/ppermute | solution.py:290
  35.5 5.4 %collective-permute-start.7 = (f32[37,8,128]{2,1,0:T(8,128)S(1)}, f32[37,8,128]{2,1,0:T(8,128)S(1)}, u32[]{:S(2)}, u32[]{:S(2)}) collective-permute-start(f32[37,8,128]{2,1,0:T(8,128)S(1)} %get-tuple-element.65), channel_id=1, source_target_pairs={{0,16},{8,200},{16,0},{24,216},{32,48},{40,232},{48,32},{56,248},{... | collective-permute-start | bytes 454664 | tf_op jit(solution)/shard_map/ppermute | solution.py:290
  35.5 5.9 %collective-permute-start.9 = (f32[37,8,128]{2,1,0:T(8,128)S(1)}, f32[37,8,128]{2,1,0:T(8,128)S(1)}, u32[]{:S(2)}, u32[]{:S(2)}) collective-permute-start(f32[37,8,128]{2,1,0:T(8,128)S(1)} %get-tuple-element.29.m0), channel_id=1, source_target_pairs={{0,8},{8,0},{16,24},{24,16},{32,40},{40,32},{48,56},{56,48},{64,72... | collective-permute-start | bytes 454664 | tf_op jit(solution)/shard_map/ppermute | solution.py:294
  37.6 3.8 %collective-permute-start.10 = (f32[37,8,128]{2,1,0:T(8,128)S(1)}, f32[37,8,128]{2,1,0:T(8,128)S(1)}, u32[]{:S(2)}, u32[]{:S(2)}) collective-permute-start(f32[37,8,128]{2,1,0:T(8,128)S(1)} %collective-permute-done.6.m1), channel_id=1, source_target_pairs={{0,8},{8,0},{16,24},{24,16},{32,40},{40,32},{48,56},{56,48},{64,72... | collective-permute-start | bytes 454664 | tf_op jit(solution)/shard_map/ppermute | solution.py:294
  40.8 1.4 %collective-permute-start.12 = (f32[37,8,128]{2,1,0:T(8,128)S(1)}, f32[37,8,128]{2,1,0:T(8,128)S(1)}, u32[]{:S(2)}, u32[]{:S(2)}) collective-permute-start(f32[37,8,128]{2,1,0:T(8,128)S(1)} %collective-permute-done.8.m3), channel_id=1, source_target_pairs={{0,8},{8,0},{16,24},{24,16},{32,40},{40,32},{48,56},{56,48},{64,72... | collective-permute-start | bytes 454664 | tf_op jit(solution)/shard_map/ppermute | solution.py:294
  40.8 1.6 %collective-permute-start.11 = (f32[37,8,128]{2,1,0:T(8,128)S(1)}, f32[37,8,128]{2,1,0:T(8,128)S(1)}, u32[]{:S(2)}, u32[]{:S(2)}) collective-permute-start(f32[37,8,128]{2,1,0:T(8,128)S(1)} %collective-permute-done.7.m2), channel_id=1, source_target_pairs={{0,8},{8,0},{16,24},{24,16},{32,40},{40,32},{48,56},{56,48},{64,72... | collective-permute-start | bytes 454664 | tf_op jit(solution)/shard_map/ppermute | solution.py:294
  43.6 7.7 %collective-permute-start.13 = (f32[36,8,128]{2,1,0:T(8,128)S(1)}, f32[36,8,128]{2,1,0:T(8,128)S(1)}, u32[]{:S(2)}, u32[]{:S(2)}) collective-permute-start(f32[36,8,128]{2,1,0:T(8,128)S(1)} %get-tuple-element.26), channel_id=1, source_target_pairs={{0,128},{8,40},{16,144},{24,56},{32,160},{40,8},{48,176},{56,24},{... | collective-permute-start | bytes 442376 | tf_op jit(solution)/shard_map/ppermute | solution.py:285
  46.1 7.1 %collective-permute-start.14 = (f32[36,8,128]{2,1,0:T(8,128)S(1)}, f32[36,8,128]{2,1,0:T(8,128)S(1)}, u32[]{:S(2)}, u32[]{:S(2)}) collective-permute-start(f32[36,8,128]{2,1,0:T(8,128)S(1)} %get-tuple-element.27), channel_id=1, source_target_pairs={{0,192},{8,24},{16,208},{24,8},{32,224},{40,56},{48,240},{56,40},{... | collective-permute-start | bytes 442376 | tf_op jit(solution)/shard_map/ppermute | solution.py:285
  47.7 6.7 %collective-permute-start.15 = (f32[36,8,128]{2,1,0:T(8,128)S(1)}, f32[36,8,128]{2,1,0:T(8,128)S(1)}, u32[]{:S(2)}, u32[]{:S(2)}) collective-permute-start(f32[36,8,128]{2,1,0:T(8,128)S(1)} %get-tuple-element.28), channel_id=1, source_target_pairs={{0,64},{8,56},{16,80},{24,40},{32,96},{40,24},{48,112},{56,8},{64,... | collective-permute-start | bytes 442376 | tf_op jit(solution)/shard_map/ppermute | solution.py:285
  54.5 6.7 %collective-permute-start.16 = (f32[36,8,128]{2,1,0:T(8,128)S(1)}, f32[36,8,128]{2,1,0:T(8,128)S(1)}, u32[]{:S(2)}, u32[]{:S(2)}) collective-permute-start(f32[36,8,128]{2,1,0:T(8,128)S(1)} %pad_maximum_fusion.1), channel_id=1, source_target_pairs={{0,32},{8,136},{16,48},{24,152},{32,0},{40,168},{48,16},{56,184},{... | collective-permute-start | bytes 442376 | tf_op jit(solution)/shard_map/ppermute | solution.py:290
  56.0 6.0 %collective-permute-start.17 = (f32[36,8,128]{2,1,0:T(8,128)S(1)}, f32[36,8,128]{2,1,0:T(8,128)S(1)}, u32[]{:S(2)}, u32[]{:S(2)}) collective-permute-start(f32[36,8,128]{2,1,0:T(8,128)S(1)} %pad_maximum_fusion.2), channel_id=1, source_target_pairs={{0,16},{8,200},{16,0},{24,216},{32,48},{40,232},{48,32},{56,248},{... | collective-permute-start | bytes 442376 | tf_op jit(solution)/shard_map/ppermute | solution.py:290
  57.4 6.4 %collective-permute-start.18 = (f32[36,8,128]{2,1,0:T(8,128)S(1)}, f32[36,8,128]{2,1,0:T(8,128)S(1)}, u32[]{:S(2)}, u32[]{:S(2)}) collective-permute-start(f32[36,8,128]{2,1,0:T(8,128)S(1)} %pad_maximum_fusion.3), channel_id=1, source_target_pairs={{0,48},{8,72},{16,32},{24,88},{32,16},{40,104},{48,0},{56,120},{64... | collective-permute-start | bytes 442376 | tf_op jit(solution)/shard_map/ppermute | solution.py:290
where the time goes:
time: 64.8 us; the launch traced here: 64.7 us
  waiting for transfers between devices  30.2 us (47%)
  starting transfers between devices  29 us (45%)
  Pallas kernels  4.63 us (7%)
  between operations  0.76 us (1%)
    ppermute x6, waiting for transfers between devices, outer_step(): return v if k == 0 else lax.ppermute(v, 'dom', pairs)  15 us
    ppermute x6, waiting for transfers between devices, inner_step(): return v if k == 0 else lax.ppermute(v, 'dom', pairs)  10.3 us
    ppermute x6, starting transfers between devices, outer_step(): return v if k == 0 else lax.ppermute(v, 'dom', pairs)  9.75 us
    ppermute x1, starting transfers between devices, next_slab(): return lax.ppermute(v, ('dom', 'rows'), low + [(b, a) for a, b in low])  9.12 us
    ppermute x6, starting transfers between devices, inner_step(): return v if k == 0 else lax.ppermute(v, 'dom', pairs)  9.02 us
    ppermute x1, waiting for transfers between devices, next_slab(): return lax.ppermute(v, ('dom', 'rows'), low + [(b, a) for a, b in low])  3.04 us
    pallas_call x1, Pallas kernels, shards(): pl.pallas_call(first_kernel, out_shape=[strip, strip, halves, halves, gro...  1.92 us
    ppermute x6, waiting for transfers between devices, other_core(): return lax.ppermute(v, 'dom', [(i, i ^ 1) for i in range(32)])  1.78 us
  transfers between devices with their start and end apart: 19, of which 15 were waited for; matrix products, arithmetic and copies ran while one was open for 0% of the time, Pallas kernels for 0%

commit v1 on v0

--- a/solution.py
+++ b/solution.py
@@ -19,6 +19,7 @@
 AT = {item: n for n, item in enumerate(ITEMS)}
 STEP_Z = (0, 2, 3, 1)
 STEP_Y = (0, 2, 1, 3)
+LATE_Z = (0, 2, 1, 3)
 VMEM = pl.BlockSpec(memory_space=pltpu.VMEM)
 SMEM = pl.BlockSpec(memory_space=pltpu.SMEM)
 HBM = pl.BlockSpec(memory_space=pltpu.HBM)
@@ -64,11 +65,11 @@
     return jnp.where(last, 0.0, flux(q, eta, right_of(eta), bed_x, fric))
 
 
-def chunk_at(z, y, c, outer, inner):
+def chunk_at(z, y, c, outer, inner, inner_z=STEP_Z):
     return jnp.where(
         c == 0,
         (z ^ STEP_Z[outer]) * 4 + (y ^ STEP_Y[inner]),
-        (z ^ STEP_Z[inner]) * 4 + (y ^ STEP_Y[outer]),
+        (z ^ inner_z[inner]) * 4 + (y ^ STEP_Y[outer]),
     )
 
 
@@ -219,7 +220,7 @@
     names = own[6, 4:5, 0:128] + far[6, 4:5, 0:128]
     for k, out in enumerate((o0, o1, o2, o3)):
         for j in range(4):
-            out[PER * j : PER * j + PER] = packed[chunk_at(z, y, c, k, j)]
+            out[PER * j : PER * j + PER] = packed[chunk_at(z, y, c, k, j, LATE_Z)]
         out[4 * PER] = jnp.zeros((8, 128), F32)
         out[4 * PER, 0:1, :] = names
 
@@ -240,11 +241,11 @@
             dest = ((at >> 2) << 3) | ((at & 3) << 1) | c
             for u in range(2):
                 name = anc[2 * dest + u]
-                dz = step_of(STEP_Z, (name >> 4) ^ z)
+                dz, late_dz = (step_of(steps, (name >> 4) ^ z) for steps in (STEP_Z, LATE_Z))
                 dy = step_of(STEP_Y, ((name >> 2) & 3) ^ y)
                 for n in range(2):
                     core = c ^ n
-                    base = jnp.where(core == 0, dy * 4 + dz, dz * 4 + dy) * PER
+                    base = jnp.where(core == 0, dy * 4 + dz, late_dz * 4 + dy) * PER
                     v = pl.multiple_of((((name >> 1) & 1) ^ core) * 4 + (name & 1) * 2, 2)
                     row = 4 * n + 2 * u
                     out[PER * j : PER * j + PER, row : row + 2, :] = held[n, pl.ds(base, PER), pl.ds(v, 2), :]
@@ -285,8 +286,8 @@
     return v if k == 0 else lax.ppermute(v, "dom", pairs)
 
 
-def inner_step(v, k):
-    pairs = [(i, i ^ (STEP_Y[k] << 1 if i % 2 == 0 else STEP_Z[k] << 3)) for i in range(32)]
+def inner_step(v, k, inner_z=STEP_Z):
+    pairs = [(i, i ^ (STEP_Y[k] << 1 if i % 2 == 0 else inner_z[k] << 3)) for i in range(32)]
     return v if k == 0 else lax.ppermute(v, "dom", pairs)
 
 
@@ -295,7 +296,7 @@
 
 
 def next_slab(v):
-    low = [((2 * chip + 1) * 8 + r, 2 * chip * 8 + r + 1) for chip in range(16) for r in range(7)]
+    low = [((2 * chip + 1) * 8 + r, 2 * chip * 8 + (r + 1) % 8) for chip in range(16) for r in range(8)]
     return lax.ppermute(v, ("dom", "rows"), low + [(b, a) for a, b in low])
 
 
@@ -332,7 +333,7 @@
     parts = [outer_step(v, k) for k, v in enumerate(parts)]
     names = (parts[0][4 * PER] + parts[1][4 * PER]) + (parts[2][4 * PER] + parts[3][4 * PER])
     parts = [jnp.concatenate([v, names[None]]) for v in regroup(parts, PER)]
-    parts = [inner_step(v, k) for k, v in enumerate(parts)]
+    parts = [inner_step(v, k, LATE_Z) for k, v in enumerate(parts)]
     names = sum(v[4 * PER, 0, :64] for v in parts).astype(jnp.int32)
     others = [other_core(v) for v in parts]
     parts = pl.pallas_call(

time: 64.8 us -> 64.8 us (level)
  the two profiles are of different devices: /device:TPU:6 before, /device:TPU:96 now
where the time goes in v1:
time: 64.8 us; the launch traced here: 64.7 us
  waiting for transfers between devices  32.2 us (50%)
  starting transfers between devices  27 us (42%)
  Pallas kernels  4.67 us (7%)
  between operations  0.75 us (1%)
    ppermute x6, waiting for transfers between devices, outer_step(): return v if k == 0 else lax.ppermute(v, 'dom', pairs)  15.9 us
    ppermute x6, starting transfers between devices, outer_step(): return v if k == 0 else lax.ppermute(v, 'dom', pairs)  11.3 us
    ppermute x6, waiting for transfers between devices, inner_step(): return v if k == 0 else lax.ppermute(v, 'dom', pairs)  10.2 us
    ppermute x6, starting transfers between devices, inner_step(): return v if k == 0 else lax.ppermute(v, 'dom', pairs)  8.13 us
    ppermute x1, starting transfers between devices, next_slab(): return lax.ppermute(v, ('dom', 'rows'), low + [(b, a) for a, b in low])  6.45 us
    ppermute x1, waiting for transfers between devices, next_slab(): return lax.ppermute(v, ('dom', 'rows'), low + [(b, a) for a, b in low])  4.31 us
    pallas_call x1, Pallas kernels, shards(): pl.pallas_call(first_kernel, out_shape=[strip, strip, halves, halves, gro...  1.92 us
    ppermute x6, waiting for transfers between devices, other_core(): return lax.ppermute(v, 'dom', [(i, i ^ 1) for i in range(32)])  1.78 us
  transfers between devices with their start and end apart: 19, of which 15 were waited for; matrix products, arithmetic and copies ran while one was open for 0% of the time, Pallas kernels for 0%

profile of v1, /device:TPU:96, one launch (start us, length us, event | category | flops | bytes accessed | tf_op | source)
XLA Modules:
  0.0 64.7 jit_solution(14752891681756365946)
XLA Ops:
  0.6 1.9 %shard_map.94 = (f32[8,1536]{1,0:T(8,128)S(1)}, f32[8,1536]{1,0:T(8,128)S(1)}, f32[7,8,1536]{2,1,0:T(8,128)S(1)}, f32[7,8,1536]{2,1,0:T(8,128)S(1)}, f32[3,8,1536]{2,1,0:T(8,128)S(1)}) custom-call(f32[2,16,1536]{2,1,0:T(8,128)} %depth_in.1, f32[2,16,1536]{2,1,0:T(8,128)} %xf_in.1, f32[2,16,1536]{2,1,0:T(8,128)} %yf_in.1, s32[2,16,1536]{2,1,0:T(8,128)} %wet_in.1, ...), custom_call_target="tpu_custom_call" | custom-call | tf_op jit(solution)/shard_map/pallas_call | solution.py:313
  2.6 0.1 collective-permute-start.1
  2.7 0.5 collective-permute-start
  3.2 0.7 %collective-permute-done.1 = f32[8,1536]{1,0:T(8,128)S(1)} collective-permute-done((f32[8,1536]{1,0:T(8,128)S(1)}, f32[8,1536]{1,0:T(8,128)S(1)}, u32[]{:S(2)}, u32[]{:S(2)}) %collective-permute-start.1) | collective-permute-done | bytes 49184 | tf_op jit(solution)/shard_map/ppermute | solution.py:295
  3.9 6.5 %collective-permute-start.2 = (f32[16,1536]{1,0:T(8,128)S(1)}, f32[16,1536]{1,0:T(8,128)S(1)}, u32[]{:S(2)}, u32[]{:S(2)}) collective-permute-start(f32[16,1536]{1,0:T(8,128)S(1)} %constant_dynamic-update-slice_fusion.mine), channel_id=1, source_target_pairs={{8,1},{9,2},{10,3},{11,4},{12,5},{13,6},{14,7},{15,0},{24,17},{25,... | collective-permute-start | bytes 294920 | tf_op jit(solution)/shard_map/ppermute | solution.py:300
  10.3 4.3 %collective-permute-done.2.next_slab = f32[16,1536]{1,0:T(8,128)S(1)} collective-permute-done((f32[16,1536]{1,0:T(8,128)S(1)}, f32[16,1536]{1,0:T(8,128)S(1)}, u32[]{:S(2)}, u32[]{:S(2)}) %collective-permute-start.2) | collective-permute-done | bytes 98336 | tf_op jit(solution)/shard_map/ppermute | solution.py:300
  14.7 0.7 %shard_map.95 = (f32[37,8,128]{2,1,0:T(8,128)S(1)}, f32[37,8,128]{2,1,0:T(8,128)S(1)}, f32[37,8,128]{2,1,0:T(8,128)S(1)}, f32[37,8,128]{2,1,0:T(8,128)S(1)}) custom-call(f32[7,8,1536]{2,1,0:T(8,128)S(1)} %get-tuple-element.16.own, f32[7,8,1536]{2,1,0:T(8,128)S(1)} %collective-permute-done.far, f32[3,8,1536]{2,1,0:T(8,128)S(1)} %get-tuple-element.18.terrain, ...), custom_call_target="tpu_custom_call" | custom-call | tf_op jit(solution)/shard_map/pallas_call | solution.py:325
  15.4 1.0 %collective-permute-start.3 = (f32[37,8,128]{2,1,0:T(8,128)S(1)}, f32[37,8,128]{2,1,0:T(8,128)S(1)}, u32[]{:S(2)}, u32[]{:S(2)}) collective-permute-start(f32[37,8,128]{2,1,0:T(8,128)S(1)} %get-tuple-element.22), channel_id=1, source_target_pairs={{0,128},{8,40},{16,144},{24,56},{32,160},{40,8},{48,176},{56,24},{... | collective-permute-start | bytes 454664 | tf_op jit(solution)/shard_map/ppermute | solution.py:286
  16.4 3.7 %collective-permute-start.4 = (f32[37,8,128]{2,1,0:T(8,128)S(1)}, f32[37,8,128]{2,1,0:T(8,128)S(1)}, u32[]{:S(2)}, u32[]{:S(2)}) collective-permute-start(f32[37,8,128]{2,1,0:T(8,128)S(1)} %get-tuple-element.23), channel_id=1, source_target_pairs={{0,192},{8,24},{16,208},{24,8},{32,224},{40,56},{48,240},{56,40},{... | collective-permute-start | bytes 454664 | tf_op jit(solution)/shard_map/ppermute | solution.py:286
  20.1 1.4 %collective-permute-done.3 = f32[37,8,128]{2,1,0:T(8,128)S(1)} collective-permute-done((f32[37,8,128]{2,1,0:T(8,128)S(1)}, f32[37,8,128]{2,1,0:T(8,128)S(1)}, u32[]{:S(2)}, u32[]{:S(2)}) %collective-permute-start.3) | collective-permute-done | bytes 151584 | tf_op jit(solution)/shard_map/ppermute | solution.py:286
  21.5 3.6 %collective-permute-done.4 = f32[37,8,128]{2,1,0:T(8,128)S(1)} collective-permute-done((f32[37,8,128]{2,1,0:T(8,128)S(1)}, f32[37,8,128]{2,1,0:T(8,128)S(1)}, u32[]{:S(2)}, u32[]{:S(2)}) %collective-permute-start.4) | collective-permute-done | bytes 151584 | tf_op jit(solution)/shard_map/ppermute | solution.py:286
  25.1 3.0 %collective-permute-done.5 = f32[37,8,128]{2,1,0:T(8,128)S(1)} collective-permute-done((f32[37,8,128]{2,1,0:T(8,128)S(1)}, f32[37,8,128]{2,1,0:T(8,128)S(1)}, u32[]{:S(2)}, u32[]{:S(2)}) %collective-permute-start.5) | collective-permute-done | bytes 151584 | tf_op jit(solution)/shard_map/ppermute | solution.py:286
  28.2 2.6 %collective-permute-start.6 = (f32[37,8,128]{2,1,0:T(8,128)S(1)}, f32[37,8,128]{2,1,0:T(8,128)S(1)}, u32[]{:S(2)}, u32[]{:S(2)}) collective-permute-start(f32[37,8,128]{2,1,0:T(8,128)S(1)} %get-tuple-element.63), channel_id=1, source_target_pairs={{0,32},{8,136},{16,48},{24,152},{32,0},{40,168},{48,16},{56,184},{... | collective-permute-start | bytes 454664 | tf_op jit(solution)/shard_map/ppermute | solution.py:291
  30.8 1.1 %collective-permute-start.8 = (f32[37,8,128]{2,1,0:T(8,128)S(1)}, f32[37,8,128]{2,1,0:T(8,128)S(1)}, u32[]{:S(2)}, u32[]{:S(2)}) collective-permute-start(f32[37,8,128]{2,1,0:T(8,128)S(1)} %get-tuple-element.64), channel_id=1, source_target_pairs={{0,48},{8,200},{16,32},{24,216},{32,16},{40,232},{48,0},{56,248},{... | collective-permute-start | bytes 454664 | tf_op jit(solution)/shard_map/ppermute | solution.py:291
  32.0 3.0 %collective-permute-done.6.m1 = f32[37,8,128]{2,1,0:T(8,128)S(1)} collective-permute-done((f32[37,8,128]{2,1,0:T(8,128)S(1)}, f32[37,8,128]{2,1,0:T(8,128)S(1)}, u32[]{:S(2)}, u32[]{:S(2)}) %collective-permute-start.6) | collective-permute-done | bytes 151584 | tf_op jit(solution)/shard_map/ppermute | solution.py:291
  35.0 2.3 %collective-permute-done.8.m3 = f32[37,8,128]{2,1,0:T(8,128)S(1)} collective-permute-done((f32[37,8,128]{2,1,0:T(8,128)S(1)}, f32[37,8,128]{2,1,0:T(8,128)S(1)}, u32[]{:S(2)}, u32[]{:S(2)}) %collective-permute-start.8) | collective-permute-done | bytes 151584 | tf_op jit(solution)/shard_map/ppermute | solution.py:291
  37.3 0.5 collective-permute-start.11
  37.8 0.8 %collective-permute-done.12.t3 = f32[37,8,128]{2,1,0:T(8,128)S(1)} collective-permute-done((f32[37,8,128]{2,1,0:T(8,128)S(1)}, f32[37,8,128]{2,1,0:T(8,128)S(1)}, u32[]{:S(2)}, u32[]{:S(2)}) %collective-permute-start.12) | collective-permute-done | bytes 151584 | tf_op jit(solution)/shard_map/ppermute | solution.py:295
  38.6 0.2 collective-permute-done.11.t2
  38.8 1.2 %shard_map.96 = (f32[36,8,128]{2,1,0:T(8,128)S(1)}, f32[36,8,128]{2,1,0:T(8,128)S(1)}, f32[36,8,128]{2,1,0:T(8,128)S(1)}, f32[36,8,128]{2,1,0:T(8,128)S(1)}) custom-call(s32[64]{0:T(128)S(1)} %fusion.2.anc, f32[37,8,128]{2,1,0:T(8,128)S(1)} %get-tuple-element.29.m0, f32[37,8,128]{2,1,0:T(8,128)S(1)} %collective-permute-done.6.m1, ...), custom_call_target="tpu_custom_call" | custom-call | tf_op jit(solution)/shard_map/pallas_call | solution.py:339
  40.0 4.0 %collective-permute-start.13 = (f32[36,8,128]{2,1,0:T(8,128)S(1)}, f32[36,8,128]{2,1,0:T(8,128)S(1)}, u32[]{:S(2)}, u32[]{:S(2)}) collective-permute-start(f32[36,8,128]{2,1,0:T(8,128)S(1)} %get-tuple-element.26), channel_id=1, source_target_pairs={{0,128},{8,40},{16,144},{24,56},{32,160},{40,8},{48,176},{56,24},{... | collective-permute-start | bytes 442376 | tf_op jit(solution)/shard_map/ppermute | solution.py:286
  44.0 2.5 %collective-permute-start.14 = (f32[36,8,128]{2,1,0:T(8,128)S(1)}, f32[36,8,128]{2,1,0:T(8,128)S(1)}, u32[]{:S(2)}, u32[]{:S(2)}) collective-permute-start(f32[36,8,128]{2,1,0:T(8,128)S(1)} %get-tuple-element.27), channel_id=1, source_target_pairs={{0,192},{8,24},{16,208},{24,8},{32,224},{40,56},{48,240},{56,40},{... | collective-permute-start | bytes 442376 | tf_op jit(solution)/shard_map/ppermute | solution.py:286
  46.5 0.6 %collective-permute-done.13 = f32[36,8,128]{2,1,0:T(8,128)S(1)} collective-permute-done((f32[36,8,128]{2,1,0:T(8,128)S(1)}, f32[36,8,128]{2,1,0:T(8,128)S(1)}, u32[]{:S(2)}, u32[]{:S(2)}) %collective-permute-start.13) | collective-permute-done | bytes 147488 | tf_op jit(solution)/shard_map/ppermute | solution.py:286
  47.2 4.2 %collective-permute-done.14 = f32[36,8,128]{2,1,0:T(8,128)S(1)} collective-permute-done((f32[36,8,128]{2,1,0:T(8,128)S(1)}, f32[36,8,128]{2,1,0:T(8,128)S(1)}, u32[]{:S(2)}, u32[]{:S(2)}) %collective-permute-start.14) | collective-permute-done | bytes 147488 | tf_op jit(solution)/shard_map/ppermute | solution.py:286
  51.4 3.0 %collective-permute-done.15 = f32[36,8,128]{2,1,0:T(8,128)S(1)} collective-permute-done((f32[36,8,128]{2,1,0:T(8,128)S(1)}, f32[36,8,128]{2,1,0:T(8,128)S(1)}, u32[]{:S(2)}, u32[]{:S(2)}) %collective-permute-start.15) | collective-permute-done | bytes 147488 | tf_op jit(solution)/shard_map/ppermute | solution.py:286
  54.5 1.4 %collective-permute-start.16 = (f32[36,8,128]{2,1,0:T(8,128)S(1)}, f32[36,8,128]{2,1,0:T(8,128)S(1)}, u32[]{:S(2)}, u32[]{:S(2)}) collective-permute-start(f32[36,8,128]{2,1,0:T(8,128)S(1)} %pad_maximum_fusion.1), channel_id=1, source_target_pairs={{0,32},{8,136},{16,48},{24,152},{32,0},{40,168},{48,16},{56,184},{... | collective-permute-start | bytes 442376 | tf_op jit(solution)/shard_map/ppermute | solution.py:291
  55.9 1.4 %collective-permute-start.17 = (f32[36,8,128]{2,1,0:T(8,128)S(1)}, f32[36,8,128]{2,1,0:T(8,128)S(1)}, u32[]{:S(2)}, u32[]{:S(2)}) collective-permute-start(f32[36,8,128]{2,1,0:T(8,128)S(1)} %pad_maximum_fusion.2), channel_id=1, source_target_pairs={{0,16},{8,200},{16,0},{24,216},{32,48},{40,232},{48,32},{56,248},{... | collective-permute-start | bytes 442376 | tf_op jit(solution)/shard_map/ppermute | solution.py:291
  57.4 1.5 %collective-permute-start.18 = (f32[36,8,128]{2,1,0:T(8,128)S(1)}, f32[36,8,128]{2,1,0:T(8,128)S(1)}, u32[]{:S(2)}, u32[]{:S(2)}) collective-permute-start(f32[36,8,128]{2,1,0:T(8,128)S(1)} %pad_maximum_fusion.3), channel_id=1, source_target_pairs={{0,48},{8,72},{16,32},{24,88},{32,16},{40,104},{48,0},{56,120},{64... | collective-permute-start | bytes 442376 | tf_op jit(solution)/shard_map/ppermute | solution.py:291
  58.9 2.3 %collective-permute-done.16.f1 = f32[36,8,128]{2,1,0:T(8,128)S(1)} collective-permute-done((f32[36,8,128]{2,1,0:T(8,128)S(1)}, f32[36,8,128]{2,1,0:T(8,128)S(1)}, u32[]{:S(2)}, u32[]{:S(2)}) %collective-permute-start.16) | collective-permute-done | bytes 147488 | tf_op jit(solution)/shard_map/ppermute | solution.py:291
  61.2 0.7 %collective-permute-done.17.f2 = f32[36,8,128]{2,1,0:T(8,128)S(1)} collective-permute-done((f32[36,8,128]{2,1,0:T(8,128)S(1)}, f32[36,8,128]{2,1,0:T(8,128)S(1)}, u32[]{:S(2)}, u32[]{:S(2)}) %collective-permute-start.17) | collective-permute-done | bytes 147488 | tf_op jit(solution)/shard_map/ppermute | solution.py:291
  62.0 1.9 %collective-permute-done.18.f3 = f32[36,8,128]{2,1,0:T(8,128)S(1)} collective-permute-done((f32[36,8,128]{2,1,0:T(8,128)S(1)}, f32[36,8,128]{2,1,0:T(8,128)S(1)}, u32[]{:S(2)}, u32[]{:S(2)}) %collective-permute-start.18) | collective-permute-done | bytes 147488 | tf_op jit(solution)/shard_map/ppermute | solution.py:291
  63.8 0.9 %shard_map.97 = (f32[2,16,1536]{2,1,0:T(8,128)}, f32[2,16,1536]{2,1,0:T(8,128)}, f32[2,16,1536]{2,1,0:T(8,128)}) custom-call(f32[36,8,128]{2,1,0:T(8,128)S(1)} %pad_maximum_fusion.f0, f32[36,8,128]{2,1,0:T(8,128)S(1)} %collective-permute-done.16.f1, f32[36,8,128]{2,1,0:T(8,128)S(1)} %collective-permute-done.17.f2, f32[36,8,128]{2,1,0:T(8,128)S(1)} %collective-permute-done.18.f3), custom_call_target="tpu_custom_call" | custom-call | tf_op jit(solution)/shard_map/pallas_call | solution.py:350
  (27 shorter events, 0.2 us)
Async XLA Ops:
  2.6 1.3 %collective-permute-start.1 = (f32[8,1536]{1,0:T(8,128)S(1)}, f32[8,1536]{1,0:T(8,128)S(1)}, u32[]{:S(2)}, u32[]{:S(2)}) collective-permute-start(f32[8,1536]{1,0:T(8,128)S(1)} %get-tuple-element.20), channel_id=1, source_target_pairs={{0,8},{8,0},{16,24},{24,16},{32,40},{40,32},{48,56},{56,48},{64,72... | collective-permute-start | bytes 147464 | tf_op jit(solution)/shard_map/ppermute | solution.py:295
  2.7 12.0 %collective-permute-start = (f32[7,8,1536]{2,1,0:T(8,128)S(1)}, f32[7,8,1536]{2,1,0:T(8,128)S(1)}, u32[]{:S(2)}, u32[]{:S(2)}) collective-permute-start(f32[7,8,1536]{2,1,0:T(8,128)S(1)} %get-tuple-element.17), channel_id=1, source_target_pairs={{0,8},{8,0},{16,24},{24,16},{32,40},{40,32},{48,56},{56,48},{64,72... | collective-permute-start | bytes 1032200 | tf_op jit(solution)/shard_map/ppermute | solution.py:295
  3.9 10.8 %collective-permute-start.2 = (f32[16,1536]{1,0:T(8,128)S(1)}, f32[16,1536]{1,0:T(8,128)S(1)}, u32[]{:S(2)}, u32[]{:S(2)}) collective-permute-start(f32[16,1536]{1,0:T(8,128)S(1)} %constant_dynamic-update-slice_fusion.mine), channel_id=1, source_target_pairs={{8,1},{9,2},{10,3},{11,4},{12,5},{13,6},{14,7},{15,0},{24,17},{25,... | collective-permute-start | bytes 294920 | tf_op jit(solution)/shard_map/ppermute | solution.py:300
  15.4 6.2 %collective-permute-start.3 = (f32[37,8,128]{2,1,0:T(8,128)S(1)}, f32[37,8,128]{2,1,0:T(8,128)S(1)}, u32[]{:S(2)}, u32[]{:S(2)}) collective-permute-start(f32[37,8,128]{2,1,0:T(8,128)S(1)} %get-tuple-element.22), channel_id=1, source_target_pairs={{0,128},{8,40},{16,144},{24,56},{32,160},{40,8},{48,176},{56,24},{... | collective-permute-start | bytes 454664 | tf_op jit(solution)/shard_map/ppermute | solution.py:286
  16.4 8.7 %collective-permute-start.4 = (f32[37,8,128]{2,1,0:T(8,128)S(1)}, f32[37,8,128]{2,1,0:T(8,128)S(1)}, u32[]{:S(2)}, u32[]{:S(2)}) collective-permute-start(f32[37,8,128]{2,1,0:T(8,128)S(1)} %get-tuple-element.23), channel_id=1, source_target_pairs={{0,192},{8,24},{16,208},{24,8},{32,224},{40,56},{48,240},{56,40},{... | collective-permute-start | bytes 454664 | tf_op jit(solution)/shard_map/ppermute | solution.py:286
  20.1 8.0 %collective-permute-start.5 = (f32[37,8,128]{2,1,0:T(8,128)S(1)}, f32[37,8,128]{2,1,0:T(8,128)S(1)}, u32[]{:S(2)}, u32[]{:S(2)}) collective-permute-start(f32[37,8,128]{2,1,0:T(8,128)S(1)} %get-tuple-element.24), channel_id=1, source_target_pairs={{0,64},{8,56},{16,80},{24,40},{32,96},{40,24},{48,112},{56,8},{64,... | collective-permute-start | bytes 454664 | tf_op jit(solution)/shard_map/ppermute | solution.py:286
  28.2 6.8 %collective-permute-start.6 = (f32[37,8,128]{2,1,0:T(8,128)S(1)}, f32[37,8,128]{2,1,0:T(8,128)S(1)}, u32[]{:S(2)}, u32[]{:S(2)}) collective-permute-start(f32[37,8,128]{2,1,0:T(8,128)S(1)} %get-tuple-element.63), channel_id=1, source_target_pairs={{0,32},{8,136},{16,48},{24,152},{32,0},{40,168},{48,16},{56,184},{... | collective-permute-start | bytes 454664 | tf_op jit(solution)/shard_map/ppermute | solution.py:291
  30.8 6.4 %collective-permute-start.8 = (f32[37,8,128]{2,1,0:T(8,128)S(1)}, f32[37,8,128]{2,1,0:T(8,128)S(1)}, u32[]{:S(2)}, u32[]{:S(2)}) collective-permute-start(f32[37,8,128]{2,1,0:T(8,128)S(1)} %get-tuple-element.64), channel_id=1, source_target_pairs={{0,48},{8,200},{16,32},{24,216},{32,16},{40,232},{48,0},{56,248},{... | collective-permute-start | bytes 454664 | tf_op jit(solution)/shard_map/ppermute | solution.py:291
  32.0 5.3 %collective-permute-start.7 = (f32[37,8,128]{2,1,0:T(8,128)S(1)}, f32[37,8,128]{2,1,0:T(8,128)S(1)}, u32[]{:S(2)}, u32[]{:S(2)}) collective-permute-start(f32[37,8,128]{2,1,0:T(8,128)S(1)} %get-tuple-element.65), channel_id=1, source_target_pairs={{0,16},{8,72},{16,0},{24,88},{32,48},{40,104},{48,32},{56,120},{64... | collective-permute-start | bytes 454664 | tf_op jit(solution)/shard_map/ppermute | solution.py:291
  32.0 5.8 %collective-permute-start.9 = (f32[37,8,128]{2,1,0:T(8,128)S(1)}, f32[37,8,128]{2,1,0:T(8,128)S(1)}, u32[]{:S(2)}, u32[]{:S(2)}) collective-permute-start(f32[37,8,128]{2,1,0:T(8,128)S(1)} %get-tuple-element.29.m0), channel_id=1, source_target_pairs={{0,8},{8,0},{16,24},{24,16},{32,40},{40,32},{48,56},{56,48},{64,72... | collective-permute-start | bytes 454664 | tf_op jit(solution)/shard_map/ppermute | solution.py:295
  35.0 2.8 %collective-permute-start.10 = (f32[37,8,128]{2,1,0:T(8,128)S(1)}, f32[37,8,128]{2,1,0:T(8,128)S(1)}, u32[]{:S(2)}, u32[]{:S(2)}) collective-permute-start(f32[37,8,128]{2,1,0:T(8,128)S(1)} %collective-permute-done.6.m1), channel_id=1, source_target_pairs={{0,8},{8,0},{16,24},{24,16},{32,40},{40,32},{48,56},{56,48},{64,72... | collective-permute-start | bytes 454664 | tf_op jit(solution)/shard_map/ppermute | solution.py:295
  37.2 1.4 %collective-permute-start.12 = (f32[37,8,128]{2,1,0:T(8,128)S(1)}, f32[37,8,128]{2,1,0:T(8,128)S(1)}, u32[]{:S(2)}, u32[]{:S(2)}) collective-permute-start(f32[37,8,128]{2,1,0:T(8,128)S(1)} %collective-permute-done.8.m3), channel_id=1, source_target_pairs={{0,8},{8,0},{16,24},{24,16},{32,40},{40,32},{48,56},{56,48},{64,72... | collective-permute-start | bytes 454664 | tf_op jit(solution)/shard_map/ppermute | solution.py:295
  37.3 1.6 %collective-permute-start.11 = (f32[37,8,128]{2,1,0:T(8,128)S(1)}, f32[37,8,128]{2,1,0:T(8,128)S(1)}, u32[]{:S(2)}, u32[]{:S(2)}) collective-permute-start(f32[37,8,128]{2,1,0:T(8,128)S(1)} %collective-permute-done.7.m2), channel_id=1, source_target_pairs={{0,8},{8,0},{16,24},{24,16},{32,40},{40,32},{48,56},{56,48},{64,72... | collective-permute-start | bytes 454664 | tf_op jit(solution)/shard_map/ppermute | solution.py:295
  40.0 7.2 %collective-permute-start.13 = (f32[36,8,128]{2,1,0:T(8,128)S(1)}, f32[36,8,128]{2,1,0:T(8,128)S(1)}, u32[]{:S(2)}, u32[]{:S(2)}) collective-permute-start(f32[36,8,128]{2,1,0:T(8,128)S(1)} %get-tuple-element.26), channel_id=1, source_target_pairs={{0,128},{8,40},{16,144},{24,56},{32,160},{40,8},{48,176},{56,24},{... | collective-permute-start | bytes 442376 | tf_op jit(solution)/shard_map/ppermute | solution.py:286
  44.0 7.4 %collective-permute-start.14 = (f32[36,8,128]{2,1,0:T(8,128)S(1)}, f32[36,8,128]{2,1,0:T(8,128)S(1)}, u32[]{:S(2)}, u32[]{:S(2)}) collective-permute-start(f32[36,8,128]{2,1,0:T(8,128)S(1)} %get-tuple-element.27), channel_id=1, source_target_pairs={{0,192},{8,24},{16,208},{24,8},{32,224},{40,56},{48,240},{56,40},{... | collective-permute-start | bytes 442376 | tf_op jit(solution)/shard_map/ppermute | solution.py:286
  46.5 8.0 %collective-permute-start.15 = (f32[36,8,128]{2,1,0:T(8,128)S(1)}, f32[36,8,128]{2,1,0:T(8,128)S(1)}, u32[]{:S(2)}, u32[]{:S(2)}) collective-permute-start(f32[36,8,128]{2,1,0:T(8,128)S(1)} %get-tuple-element.28), channel_id=1, source_target_pairs={{0,64},{8,56},{16,80},{24,40},{32,96},{40,24},{48,112},{56,8},{64,... | collective-permute-start | bytes 442376 | tf_op jit(solution)/shard_map/ppermute | solution.py:286
  54.5 6.7 %collective-permute-start.16 = (f32[36,8,128]{2,1,0:T(8,128)S(1)}, f32[36,8,128]{2,1,0:T(8,128)S(1)}, u32[]{:S(2)}, u32[]{:S(2)}) collective-permute-start(f32[36,8,128]{2,1,0:T(8,128)S(1)} %pad_maximum_fusion.1), channel_id=1, source_target_pairs={{0,32},{8,136},{16,48},{24,152},{32,0},{40,168},{48,16},{56,184},{... | collective-permute-start | bytes 442376 | tf_op jit(solution)/shard_map/ppermute | solution.py:291
  55.9 6.0 %collective-permute-start.17 = (f32[36,8,128]{2,1,0:T(8,128)S(1)}, f32[36,8,128]{2,1,0:T(8,128)S(1)}, u32[]{:S(2)}, u32[]{:S(2)}) collective-permute-start(f32[36,8,128]{2,1,0:T(8,128)S(1)} %pad_maximum_fusion.2), channel_id=1, source_target_pairs={{0,16},{8,200},{16,0},{24,216},{32,48},{40,232},{48,32},{56,248},{... | collective-permute-start | bytes 442376 | tf_op jit(solution)/shard_map/ppermute | solution.py:291
  57.4 6.4 %collective-permute-start.18 = (f32[36,8,128]{2,1,0:T(8,128)S(1)}, f32[36,8,128]{2,1,0:T(8,128)S(1)}, u32[]{:S(2)}, u32[]{:S(2)}) collective-permute-start(f32[36,8,128]{2,1,0:T(8,128)S(1)} %pad_maximum_fusion.3), channel_id=1, source_target_pairs={{0,48},{8,72},{16,32},{24,88},{32,16},{40,104},{48,0},{56,120},{64... | collective-permute-start | bytes 442376 | tf_op jit(solution)/shard_map/ppermute | solution.py:291

commit v2 on v1

--- a/solution.py
+++ b/solution.py
@@ -20,6 +20,7 @@
 STEP_Z = (0, 2, 3, 1)
 STEP_Y = (0, 2, 1, 3)
 LATE_Z = (0, 2, 1, 3)
+EARLY_Y = (0, 1, 3, 2)
 VMEM = pl.BlockSpec(memory_space=pltpu.VMEM)
 SMEM = pl.BlockSpec(memory_space=pltpu.SMEM)
 HBM = pl.BlockSpec(memory_space=pltpu.HBM)
@@ -65,11 +66,15 @@
     return jnp.where(last, 0.0, flux(q, eta, right_of(eta), bed_x, fric))
 
 
-def chunk_at(z, y, c, outer, inner, inner_z=STEP_Z):
+def role_of(core):
+    return core ^ (lax.axis_index("rows") & 1) ^ 1
+
+
+def chunk_at(z, y, role, outer, inner, inner_z=STEP_Z):
     return jnp.where(
-        c == 0,
+        role == 0,
         (z ^ STEP_Z[outer]) * 4 + (y ^ STEP_Y[inner]),
-        (z ^ inner_z[inner]) * 4 + (y ^ STEP_Y[outer]),
+        (z ^ inner_z[inner]) * 4 + (y ^ EARLY_Y[outer]),
     )
 
 
@@ -220,7 +225,7 @@
     names = own[6, 4:5, 0:128] + far[6, 4:5, 0:128]
     for k, out in enumerate((o0, o1, o2, o3)):
         for j in range(4):
-            out[PER * j : PER * j + PER] = packed[chunk_at(z, y, c, k, j, LATE_Z)]
+            out[PER * j : PER * j + PER] = packed[chunk_at(z, y, role_of(c), k, j, LATE_Z)]
         out[4 * PER] = jnp.zeros((8, 128), F32)
         out[4 * PER, 0:1, :] = names
 
@@ -237,15 +242,15 @@
             held[n, 4 * PER * j : 4 * PER * j + 4 * PER] = ref[: 4 * PER]
     for k, out in enumerate((o0, o1, o2, o3)):
         for j in range(4):
-            at = chunk_at(z, y, c, k, j)
+            at = chunk_at(z, y, role_of(c), k, j)
             dest = ((at >> 2) << 3) | ((at & 3) << 1) | c
             for u in range(2):
                 name = anc[2 * dest + u]
                 dz, late_dz = (step_of(steps, (name >> 4) ^ z) for steps in (STEP_Z, LATE_Z))
-                dy = step_of(STEP_Y, ((name >> 2) & 3) ^ y)
+                dy, early_dy = (step_of(steps, ((name >> 2) & 3) ^ y) for steps in (STEP_Y, EARLY_Y))
                 for n in range(2):
                     core = c ^ n
-                    base = jnp.where(core == 0, dy * 4 + dz, late_dz * 4 + dy) * PER
+                    base = jnp.where(role_of(core) == 0, dy * 4 + dz, late_dz * 4 + early_dy) * PER
                     v = pl.multiple_of((((name >> 1) & 1) ^ core) * 4 + (name & 1) * 2, 2)
                     row = 4 * n + 2 * u
                     out[PER * j : PER * j + PER, row : row + 2, :] = held[n, pl.ds(base, PER), pl.ds(v, 2), :]
@@ -256,7 +261,7 @@
     low, even = masks()
     for j, ref in enumerate((f0, f1, f2, f3)):
         for k in range(4):
-            packed[pl.ds(chunk_at(z, y, c, k, j) * PER, PER)] = ref[PER * k : PER * k + PER]
+            packed[pl.ds(chunk_at(z, y, role_of(c), k, j) * PER, PER)] = ref[PER * k : PER * k + PER]
     for f, out in enumerate((ho, xo, yo)):
         for t in range(NT):
             cols = slice(128 * t, 128 * t + 128)
@@ -281,14 +286,17 @@
     return pltpu.CompilerParams(vmem_limit_bytes=32 * 1024 * 1024)
 
 
+def swap(v, by_role):
+    pairs = [(8 * d + r, 8 * (d ^ by_role[(d ^ r ^ 1) & 1]) + r) for d in range(32) for r in range(8)]
+    return lax.ppermute(v, ("dom", "rows"), pairs)
+
+
 def outer_step(v, k):
-    pairs = [(i, i ^ (STEP_Z[k] << 3 if i % 2 == 0 else STEP_Y[k] << 1)) for i in range(32)]
-    return v if k == 0 else lax.ppermute(v, "dom", pairs)
+    return v if k == 0 else swap(v, (STEP_Z[k] << 3, EARLY_Y[k] << 1))
 
 
 def inner_step(v, k, inner_z=STEP_Z):
-    pairs = [(i, i ^ (STEP_Y[k] << 1 if i % 2 == 0 else inner_z[k] << 3)) for i in range(32)]
-    return v if k == 0 else lax.ppermute(v, "dom", pairs)
+    return v if k == 0 else swap(v, (STEP_Y[k] << 1, inner_z[k] << 3))
 
 
 def other_core(v):

time: 64.8 us -> 62 us (0.957)
  the two profiles are of different devices: /device:TPU:96 before, /device:TPU:6 now
where the time goes in v2:
time: 62 us; the launch traced here: 61.5 us
  waiting for transfers between devices  29.9 us (48%)
  starting transfers between devices  26 us (42%)
  Pallas kernels  4.68 us (8%)
  between operations  0.77 us (1%)
    ppermute x12, waiting for transfers between devices, swap(): return lax.ppermute(v, ('dom', 'rows'), pairs)  24.9 us
    ppermute x12, starting transfers between devices, swap(): return lax.ppermute(v, ('dom', 'rows'), pairs)  18.2 us
    ppermute x1, starting transfers between devices, next_slab(): return lax.ppermute(v, ('dom', 'rows'), low + [(b, a) for a, b in low])  7.22 us
    ppermute x1, waiting for transfers between devices, next_slab(): return lax.ppermute(v, ('dom', 'rows'), low + [(b, a) for a, b in low])  2.98 us
    ppermute x6, waiting for transfers between devices, other_core(): return lax.ppermute(v, 'dom', [(i, i ^ 1) for i in range(32)])  2.07 us
    pallas_call x1, Pallas kernels, shards(): pl.pallas_call(first_kernel, out_shape=[strip, strip, halves, halves, gro...  1.92 us
  transfers between devices with their start and end apart: 19, of which 14 were waited for; matrix products, arithmetic and copies ran while one was open for 0% of the time, Pallas kernels for 0%

profile of v2, /device:TPU:6, one launch (start us, length us, event | category | flops | bytes accessed | tf_op | source)
XLA Modules:
  0.0 61.5 jit_solution(18302320503851809719)
XLA Ops:
  0.6 1.9 %shard_map.94 = (f32[8,1536]{1,0:T(8,128)S(1)}, f32[8,1536]{1,0:T(8,128)S(1)}, f32[7,8,1536]{2,1,0:T(8,128)S(1)}, f32[7,8,1536]{2,1,0:T(8,128)S(1)}, f32[3,8,1536]{2,1,0:T(8,128)S(1)}) custom-call(f32[2,16,1536]{2,1,0:T(8,128)} %depth_in.1, f32[2,16,1536]{2,1,0:T(8,128)} %xf_in.1, f32[2,16,1536]{2,1,0:T(8,128)} %yf_in.1, s32[2,16,1536]{2,1,0:T(8,128)} %wet_in.1, ...), custom_call_target="tpu_custom_call" | custom-call | tf_op jit(solution)/shard_map/pallas_call | solution.py:321
  2.7 0.5 collective-permute-start
  3.2 0.7 %collective-permute-done.1 = f32[8,1536]{1,0:T(8,128)S(1)} collective-permute-done((f32[8,1536]{1,0:T(8,128)S(1)}, f32[8,1536]{1,0:T(8,128)S(1)}, u32[]{:S(2)}, u32[]{:S(2)}) %collective-permute-start.1) | collective-permute-done | bytes 49184 | tf_op jit(solution)/shard_map/ppermute | solution.py:303
  3.9 7.2 %collective-permute-start.2 = (f32[16,1536]{1,0:T(8,128)S(1)}, f32[16,1536]{1,0:T(8,128)S(1)}, u32[]{:S(2)}, u32[]{:S(2)}) collective-permute-start(f32[16,1536]{1,0:T(8,128)S(1)} %constant_dynamic-update-slice_fusion.mine), channel_id=1, source_target_pairs={{8,1},{9,2},{10,3},{11,4},{12,5},{13,6},{14,7},{15,0},{24,17},{25,... | collective-permute-start | bytes 294920 | tf_op jit(solution)/shard_map/ppermute | solution.py:308
  11.1 3.0 %collective-permute-done.2.next_slab = f32[16,1536]{1,0:T(8,128)S(1)} collective-permute-done((f32[16,1536]{1,0:T(8,128)S(1)}, f32[16,1536]{1,0:T(8,128)S(1)}, u32[]{:S(2)}, u32[]{:S(2)}) %collective-permute-start.2) | collective-permute-done | bytes 98336 | tf_op jit(solution)/shard_map/ppermute | solution.py:308
  14.1 0.7 %shard_map.95 = (f32[37,8,128]{2,1,0:T(8,128)S(1)}, f32[37,8,128]{2,1,0:T(8,128)S(1)}, f32[37,8,128]{2,1,0:T(8,128)S(1)}, f32[37,8,128]{2,1,0:T(8,128)S(1)}) custom-call(f32[7,8,1536]{2,1,0:T(8,128)S(1)} %get-tuple-element.16.own, f32[7,8,1536]{2,1,0:T(8,128)S(1)} %collective-permute-done.far, f32[3,8,1536]{2,1,0:T(8,128)S(1)} %get-tuple-element.18.terrain, ...), custom_call_target="tpu_custom_call" | custom-call | tf_op jit(solution)/shard_map/pallas_call | solution.py:333
  14.8 2.8 %collective-permute-start.3 = (f32[37,8,128]{2,1,0:T(8,128)S(1)}, f32[37,8,128]{2,1,0:T(8,128)S(1)}, u32[]{:S(2)}, u32[]{:S(2)}) collective-permute-start(f32[37,8,128]{2,1,0:T(8,128)S(1)} %get-tuple-element.22), channel_id=1, source_target_pairs={{0,16},{1,129},{2,18},{3,131},{4,20},{5,133},{6,22},{7,135},{8,136... | collective-permute-start | bytes 454664 | tf_op jit(solution)/shard_map/ppermute | solution.py:291
  17.6 2.2 %collective-permute-start.4 = (f32[37,8,128]{2,1,0:T(8,128)S(1)}, f32[37,8,128]{2,1,0:T(8,128)S(1)}, u32[]{:S(2)}, u32[]{:S(2)}) collective-permute-start(f32[37,8,128]{2,1,0:T(8,128)S(1)} %get-tuple-element.23), channel_id=1, source_target_pairs={{0,48},{1,193},{2,50},{3,195},{4,52},{5,197},{6,54},{7,199},{8,200... | collective-permute-start | bytes 454664 | tf_op jit(solution)/shard_map/ppermute | solution.py:291
  19.8 0.7 %collective-permute-start.5 = (f32[37,8,128]{2,1,0:T(8,128)S(1)}, f32[37,8,128]{2,1,0:T(8,128)S(1)}, u32[]{:S(2)}, u32[]{:S(2)}) collective-permute-start(f32[37,8,128]{2,1,0:T(8,128)S(1)} %get-tuple-element.24), channel_id=1, source_target_pairs={{0,32},{1,65},{2,34},{3,67},{4,36},{5,69},{6,38},{7,71},{8,72},{9,... | collective-permute-start | bytes 454664 | tf_op jit(solution)/shard_map/ppermute | solution.py:291
  20.5 0.2 collective-permute-done.3
  20.8 3.2 %collective-permute-done.4 = f32[37,8,128]{2,1,0:T(8,128)S(1)} collective-permute-done((f32[37,8,128]{2,1,0:T(8,128)S(1)}, f32[37,8,128]{2,1,0:T(8,128)S(1)}, u32[]{:S(2)}, u32[]{:S(2)}) %collective-permute-start.4) | collective-permute-done | bytes 151584 | tf_op jit(solution)/shard_map/ppermute | solution.py:291
  24.0 2.5 %collective-permute-done.5 = f32[37,8,128]{2,1,0:T(8,128)S(1)} collective-permute-done((f32[37,8,128]{2,1,0:T(8,128)S(1)}, f32[37,8,128]{2,1,0:T(8,128)S(1)}, u32[]{:S(2)}, u32[]{:S(2)}) %collective-permute-start.5) | collective-permute-done | bytes 151584 | tf_op jit(solution)/shard_map/ppermute | solution.py:291
  26.5 3.9 %collective-permute-start.6 = (f32[37,8,128]{2,1,0:T(8,128)S(1)}, f32[37,8,128]{2,1,0:T(8,128)S(1)}, u32[]{:S(2)}, u32[]{:S(2)}) collective-permute-start(f32[37,8,128]{2,1,0:T(8,128)S(1)} %get-tuple-element.63), channel_id=1, source_target_pairs={{0,128},{1,33},{2,130},{3,35},{4,132},{5,37},{6,134},{7,39},{8,40}... | collective-permute-start | bytes 454664 | tf_op jit(solution)/shard_map/ppermute | solution.py:291
  30.4 0.2 collective-permute-start.8
  30.6 0.5 collective-permute-start.7
  31.1 4.2 %collective-permute-done.6.m1 = f32[37,8,128]{2,1,0:T(8,128)S(1)} collective-permute-done((f32[37,8,128]{2,1,0:T(8,128)S(1)}, f32[37,8,128]{2,1,0:T(8,128)S(1)}, u32[]{:S(2)}, u32[]{:S(2)}) %collective-permute-start.6) | collective-permute-done | bytes 151584 | tf_op jit(solution)/shard_map/ppermute | solution.py:291
  35.3 2.3 %collective-permute-done.8.m3 = f32[37,8,128]{2,1,0:T(8,128)S(1)} collective-permute-done((f32[37,8,128]{2,1,0:T(8,128)S(1)}, f32[37,8,128]{2,1,0:T(8,128)S(1)}, u32[]{:S(2)}, u32[]{:S(2)}) %collective-permute-start.8) | collective-permute-done | bytes 151584 | tf_op jit(solution)/shard_map/ppermute | solution.py:291
  37.5 0.9 %collective-permute-done.7.m2 = f32[37,8,128]{2,1,0:T(8,128)S(1)} collective-permute-done((f32[37,8,128]{2,1,0:T(8,128)S(1)}, f32[37,8,128]{2,1,0:T(8,128)S(1)}, u32[]{:S(2)}, u32[]{:S(2)}) %collective-permute-start.7) | collective-permute-done | bytes 151584 | tf_op jit(solution)/shard_map/ppermute | solution.py:291
  38.5 0.5 collective-permute-done.12.t3
  38.9 0.9 %collective-permute-done.11.t2 = f32[37,8,128]{2,1,0:T(8,128)S(1)} collective-permute-done((f32[37,8,128]{2,1,0:T(8,128)S(1)}, f32[37,8,128]{2,1,0:T(8,128)S(1)}, u32[]{:S(2)}, u32[]{:S(2)}) %collective-permute-start.11) | collective-permute-done | bytes 151584 | tf_op jit(solution)/shard_map/ppermute | solution.py:303
  39.8 1.2 %shard_map.96 = (f32[36,8,128]{2,1,0:T(8,128)S(1)}, f32[36,8,128]{2,1,0:T(8,128)S(1)}, f32[36,8,128]{2,1,0:T(8,128)S(1)}, f32[36,8,128]{2,1,0:T(8,128)S(1)}) custom-call(s32[64]{0:T(128)S(1)} %fusion.2.anc, f32[37,8,128]{2,1,0:T(8,128)S(1)} %get-tuple-element.29.m0, f32[37,8,128]{2,1,0:T(8,128)S(1)} %collective-permute-done.6.m1, ...), custom_call_target="tpu_custom_call" | custom-call | tf_op jit(solution)/shard_map/pallas_call | solution.py:347
  41.0 0.8 %collective-permute-start.13 = (f32[36,8,128]{2,1,0:T(8,128)S(1)}, f32[36,8,128]{2,1,0:T(8,128)S(1)}, u32[]{:S(2)}, u32[]{:S(2)}) collective-permute-start(f32[36,8,128]{2,1,0:T(8,128)S(1)} %get-tuple-element.26), channel_id=1, source_target_pairs={{0,16},{1,129},{2,18},{3,131},{4,20},{5,133},{6,22},{7,135},{8,136... | collective-permute-start | bytes 442376 | tf_op jit(solution)/shard_map/ppermute | solution.py:291
  41.8 0.8 %collective-permute-start.14 = (f32[36,8,128]{2,1,0:T(8,128)S(1)}, f32[36,8,128]{2,1,0:T(8,128)S(1)}, u32[]{:S(2)}, u32[]{:S(2)}) collective-permute-start(f32[36,8,128]{2,1,0:T(8,128)S(1)} %get-tuple-element.27), channel_id=1, source_target_pairs={{0,48},{1,193},{2,50},{3,195},{4,52},{5,197},{6,54},{7,199},{8,200... | collective-permute-start | bytes 442376 | tf_op jit(solution)/shard_map/ppermute | solution.py:291
  42.5 2.6 %collective-permute-start.15 = (f32[36,8,128]{2,1,0:T(8,128)S(1)}, f32[36,8,128]{2,1,0:T(8,128)S(1)}, u32[]{:S(2)}, u32[]{:S(2)}) collective-permute-start(f32[36,8,128]{2,1,0:T(8,128)S(1)} %get-tuple-element.28), channel_id=1, source_target_pairs={{0,32},{1,65},{2,34},{3,67},{4,36},{5,69},{6,38},{7,71},{8,72},{9,... | collective-permute-start | bytes 442376 | tf_op jit(solution)/shard_map/ppermute | solution.py:291
  45.2 1.0 %collective-permute-done.13 = f32[36,8,128]{2,1,0:T(8,128)S(1)} collective-permute-done((f32[36,8,128]{2,1,0:T(8,128)S(1)}, f32[36,8,128]{2,1,0:T(8,128)S(1)}, u32[]{:S(2)}, u32[]{:S(2)}) %collective-permute-start.13) | collective-permute-done | bytes 147488 | tf_op jit(solution)/shard_map/ppermute | solution.py:291
  46.2 3.5 %collective-permute-done.14 = f32[36,8,128]{2,1,0:T(8,128)S(1)} collective-permute-done((f32[36,8,128]{2,1,0:T(8,128)S(1)}, f32[36,8,128]{2,1,0:T(8,128)S(1)}, u32[]{:S(2)}, u32[]{:S(2)}) %collective-permute-start.14) | collective-permute-done | bytes 147488 | tf_op jit(solution)/shard_map/ppermute | solution.py:291
  49.8 1.4 %collective-permute-start.16 = (f32[36,8,128]{2,1,0:T(8,128)S(1)}, f32[36,8,128]{2,1,0:T(8,128)S(1)}, u32[]{:S(2)}, u32[]{:S(2)}) collective-permute-start(f32[36,8,128]{2,1,0:T(8,128)S(1)} %pad_maximum_fusion.1), channel_id=1, source_target_pairs={{0,128},{1,33},{2,130},{3,35},{4,132},{5,37},{6,134},{7,39},{8,40}... | collective-permute-start | bytes 442376 | tf_op jit(solution)/shard_map/ppermute | solution.py:291
  51.2 1.9 %collective-permute-start.17 = (f32[36,8,128]{2,1,0:T(8,128)S(1)}, f32[36,8,128]{2,1,0:T(8,128)S(1)}, u32[]{:S(2)}, u32[]{:S(2)}) collective-permute-start(f32[36,8,128]{2,1,0:T(8,128)S(1)} %pad_maximum_fusion.2), channel_id=1, source_target_pairs={{0,192},{1,17},{2,194},{3,19},{4,196},{5,21},{6,198},{7,23},{8,24}... | collective-permute-start | bytes 442376 | tf_op jit(solution)/shard_map/ppermute | solution.py:291
  53.1 0.4 collective-permute-start.18
  53.6 5.6 %collective-permute-done.16.f1 = f32[36,8,128]{2,1,0:T(8,128)S(1)} collective-permute-done((f32[36,8,128]{2,1,0:T(8,128)S(1)}, f32[36,8,128]{2,1,0:T(8,128)S(1)}, u32[]{:S(2)}, u32[]{:S(2)}) %collective-permute-start.16) | collective-permute-done | bytes 147488 | tf_op jit(solution)/shard_map/ppermute | solution.py:291
  59.2 1.5 %collective-permute-done.18.f3 = f32[36,8,128]{2,1,0:T(8,128)S(1)} collective-permute-done((f32[36,8,128]{2,1,0:T(8,128)S(1)}, f32[36,8,128]{2,1,0:T(8,128)S(1)}, u32[]{:S(2)}, u32[]{:S(2)}) %collective-permute-start.18) | collective-permute-done | bytes 147488 | tf_op jit(solution)/shard_map/ppermute | solution.py:291
  60.6 0.9 %shard_map.97 = (f32[2,16,1536]{2,1,0:T(8,128)}, f32[2,16,1536]{2,1,0:T(8,128)}, f32[2,16,1536]{2,1,0:T(8,128)}) custom-call(f32[36,8,128]{2,1,0:T(8,128)S(1)} %pad_maximum_fusion.f0, f32[36,8,128]{2,1,0:T(8,128)S(1)} %collective-permute-done.16.f1, f32[36,8,128]{2,1,0:T(8,128)S(1)} %collective-permute-done.17.f2, f32[36,8,128]{2,1,0:T(8,128)S(1)} %collective-permute-done.18.f3), custom_call_target="tpu_custom_call" | custom-call | tf_op jit(solution)/shard_map/pallas_call | solution.py:358
  (27 shorter events, 0.3 us)
Async XLA Ops:
  2.6 1.3 %collective-permute-start.1 = (f32[8,1536]{1,0:T(8,128)S(1)}, f32[8,1536]{1,0:T(8,128)S(1)}, u32[]{:S(2)}, u32[]{:S(2)}) collective-permute-start(f32[8,1536]{1,0:T(8,128)S(1)} %get-tuple-element.20), channel_id=1, source_target_pairs={{0,8},{8,0},{16,24},{24,16},{32,40},{40,32},{48,56},{56,48},{64,72... | collective-permute-start | bytes 147464 | tf_op jit(solution)/shard_map/ppermute | solution.py:303
  2.7 11.4 %collective-permute-start = (f32[7,8,1536]{2,1,0:T(8,128)S(1)}, f32[7,8,1536]{2,1,0:T(8,128)S(1)}, u32[]{:S(2)}, u32[]{:S(2)}) collective-permute-start(f32[7,8,1536]{2,1,0:T(8,128)S(1)} %get-tuple-element.17), channel_id=1, source_target_pairs={{0,8},{8,0},{16,24},{24,16},{32,40},{40,32},{48,56},{56,48},{64,72... | collective-permute-start | bytes 1032200 | tf_op jit(solution)/shard_map/ppermute | solution.py:303
  3.9 10.2 %collective-permute-start.2 = (f32[16,1536]{1,0:T(8,128)S(1)}, f32[16,1536]{1,0:T(8,128)S(1)}, u32[]{:S(2)}, u32[]{:S(2)}) collective-permute-start(f32[16,1536]{1,0:T(8,128)S(1)} %constant_dynamic-update-slice_fusion.mine), channel_id=1, source_target_pairs={{8,1},{9,2},{10,3},{11,4},{12,5},{13,6},{14,7},{15,0},{24,17},{25,... | collective-permute-start | bytes 294920 | tf_op jit(solution)/shard_map/ppermute | solution.py:308
  14.8 6.0 %collective-permute-start.3 = (f32[37,8,128]{2,1,0:T(8,128)S(1)}, f32[37,8,128]{2,1,0:T(8,128)S(1)}, u32[]{:S(2)}, u32[]{:S(2)}) collective-permute-start(f32[37,8,128]{2,1,0:T(8,128)S(1)} %get-tuple-element.22), channel_id=1, source_target_pairs={{0,16},{1,129},{2,18},{3,131},{4,20},{5,133},{6,22},{7,135},{8,136... | collective-permute-start | bytes 454664 | tf_op jit(solution)/shard_map/ppermute | solution.py:291
  17.6 6.4 %collective-permute-start.4 = (f32[37,8,128]{2,1,0:T(8,128)S(1)}, f32[37,8,128]{2,1,0:T(8,128)S(1)}, u32[]{:S(2)}, u32[]{:S(2)}) collective-permute-start(f32[37,8,128]{2,1,0:T(8,128)S(1)} %get-tuple-element.23), channel_id=1, source_target_pairs={{0,48},{1,193},{2,50},{3,195},{4,52},{5,197},{6,54},{7,199},{8,200... | collective-permute-start | bytes 454664 | tf_op jit(solution)/shard_map/ppermute | solution.py:291
  19.8 6.7 %collective-permute-start.5 = (f32[37,8,128]{2,1,0:T(8,128)S(1)}, f32[37,8,128]{2,1,0:T(8,128)S(1)}, u32[]{:S(2)}, u32[]{:S(2)}) collective-permute-start(f32[37,8,128]{2,1,0:T(8,128)S(1)} %get-tuple-element.24), channel_id=1, source_target_pairs={{0,32},{1,65},{2,34},{3,67},{4,36},{5,69},{6,38},{7,71},{8,72},{9,... | collective-permute-start | bytes 454664 | tf_op jit(solution)/shard_map/ppermute | solution.py:291
  26.5 8.8 %collective-permute-start.6 = (f32[37,8,128]{2,1,0:T(8,128)S(1)}, f32[37,8,128]{2,1,0:T(8,128)S(1)}, u32[]{:S(2)}, u32[]{:S(2)}) collective-permute-start(f32[37,8,128]{2,1,0:T(8,128)S(1)} %get-tuple-element.63), channel_id=1, source_target_pairs={{0,128},{1,33},{2,130},{3,35},{4,132},{5,37},{6,134},{7,39},{8,40}... | collective-permute-start | bytes 454664 | tf_op jit(solution)/shard_map/ppermute | solution.py:291
  30.4 7.1 %collective-permute-start.8 = (f32[37,8,128]{2,1,0:T(8,128)S(1)}, f32[37,8,128]{2,1,0:T(8,128)S(1)}, u32[]{:S(2)}, u32[]{:S(2)}) collective-permute-start(f32[37,8,128]{2,1,0:T(8,128)S(1)} %get-tuple-element.64), channel_id=1, source_target_pairs={{0,192},{1,49},{2,194},{3,51},{4,196},{5,53},{6,198},{7,55},{8,56}... | collective-permute-start | bytes 454664 | tf_op jit(solution)/shard_map/ppermute | solution.py:291
  30.6 7.9 %collective-permute-start.7 = (f32[37,8,128]{2,1,0:T(8,128)S(1)}, f32[37,8,128]{2,1,0:T(8,128)S(1)}, u32[]{:S(2)}, u32[]{:S(2)}) collective-permute-start(f32[37,8,128]{2,1,0:T(8,128)S(1)} %get-tuple-element.65), channel_id=1, source_target_pairs={{0,64},{1,17},{2,66},{3,19},{4,68},{5,21},{6,70},{7,23},{8,24},{9,... | collective-permute-start | bytes 454664 | tf_op jit(solution)/shard_map/ppermute | solution.py:291
  31.0 7.4 %collective-permute-start.9 = (f32[37,8,128]{2,1,0:T(8,128)S(1)}, f32[37,8,128]{2,1,0:T(8,128)S(1)}, u32[]{:S(2)}, u32[]{:S(2)}) collective-permute-start(f32[37,8,128]{2,1,0:T(8,128)S(1)} %get-tuple-element.29.m0), channel_id=1, source_target_pairs={{0,8},{8,0},{16,24},{24,16},{32,40},{40,32},{48,56},{56,48},{64,72... | collective-permute-start | bytes 454664 | tf_op jit(solution)/shard_map/ppermute | solution.py:303
  35.3 3.2 %collective-permute-start.10 = (f32[37,8,128]{2,1,0:T(8,128)S(1)}, f32[37,8,128]{2,1,0:T(8,128)S(1)}, u32[]{:S(2)}, u32[]{:S(2)}) collective-permute-start(f32[37,8,128]{2,1,0:T(8,128)S(1)} %collective-permute-done.6.m1), channel_id=1, source_target_pairs={{0,8},{8,0},{16,24},{24,16},{32,40},{40,32},{48,56},{56,48},{64,72... | collective-permute-start | bytes 454664 | tf_op jit(solution)/shard_map/ppermute | solution.py:303
  37.5 1.4 %collective-permute-start.12 = (f32[37,8,128]{2,1,0:T(8,128)S(1)}, f32[37,8,128]{2,1,0:T(8,128)S(1)}, u32[]{:S(2)}, u32[]{:S(2)}) collective-permute-start(f32[37,8,128]{2,1,0:T(8,128)S(1)} %collective-permute-done.8.m3), channel_id=1, source_target_pairs={{0,8},{8,0},{16,24},{24,16},{32,40},{40,32},{48,56},{56,48},{64,72... | collective-permute-start | bytes 454664 | tf_op jit(solution)/shard_map/ppermute | solution.py:303
  38.4 1.4 %collective-permute-start.11 = (f32[37,8,128]{2,1,0:T(8,128)S(1)}, f32[37,8,128]{2,1,0:T(8,128)S(1)}, u32[]{:S(2)}, u32[]{:S(2)}) collective-permute-start(f32[37,8,128]{2,1,0:T(8,128)S(1)} %collective-permute-done.7.m2), channel_id=1, source_target_pairs={{0,8},{8,0},{16,24},{24,16},{32,40},{40,32},{48,56},{56,48},{64,72... | collective-permute-start | bytes 454664 | tf_op jit(solution)/shard_map/ppermute | solution.py:303
  41.0 5.2 %collective-permute-start.13 = (f32[36,8,128]{2,1,0:T(8,128)S(1)}, f32[36,8,128]{2,1,0:T(8,128)S(1)}, u32[]{:S(2)}, u32[]{:S(2)}) collective-permute-start(f32[36,8,128]{2,1,0:T(8,128)S(1)} %get-tuple-element.26), channel_id=1, source_target_pairs={{0,16},{1,129},{2,18},{3,131},{4,20},{5,133},{6,22},{7,135},{8,136... | collective-permute-start | bytes 442376 | tf_op jit(solution)/shard_map/ppermute | solution.py:291
  41.8 7.9 %collective-permute-start.14 = (f32[36,8,128]{2,1,0:T(8,128)S(1)}, f32[36,8,128]{2,1,0:T(8,128)S(1)}, u32[]{:S(2)}, u32[]{:S(2)}) collective-permute-start(f32[36,8,128]{2,1,0:T(8,128)S(1)} %get-tuple-element.27), channel_id=1, source_target_pairs={{0,48},{1,193},{2,50},{3,195},{4,52},{5,197},{6,54},{7,199},{8,200... | collective-permute-start | bytes 442376 | tf_op jit(solution)/shard_map/ppermute | solution.py:291
  42.5 7.2 %collective-permute-start.15 = (f32[36,8,128]{2,1,0:T(8,128)S(1)}, f32[36,8,128]{2,1,0:T(8,128)S(1)}, u32[]{:S(2)}, u32[]{:S(2)}) collective-permute-start(f32[36,8,128]{2,1,0:T(8,128)S(1)} %get-tuple-element.28), channel_id=1, source_target_pairs={{0,32},{1,65},{2,34},{3,67},{4,36},{5,69},{6,38},{7,71},{8,72},{9,... | collective-permute-start | bytes 442376 | tf_op jit(solution)/shard_map/ppermute | solution.py:291
  49.8 9.4 %collective-permute-start.16 = (f32[36,8,128]{2,1,0:T(8,128)S(1)}, f32[36,8,128]{2,1,0:T(8,128)S(1)}, u32[]{:S(2)}, u32[]{:S(2)}) collective-permute-start(f32[36,8,128]{2,1,0:T(8,128)S(1)} %pad_maximum_fusion.1), channel_id=1, source_target_pairs={{0,128},{1,33},{2,130},{3,35},{4,132},{5,37},{6,134},{7,39},{8,40}... | collective-permute-start | bytes 442376 | tf_op jit(solution)/shard_map/ppermute | solution.py:291
  51.2 8.0 %collective-permute-start.17 = (f32[36,8,128]{2,1,0:T(8,128)S(1)}, f32[36,8,128]{2,1,0:T(8,128)S(1)}, u32[]{:S(2)}, u32[]{:S(2)}) collective-permute-start(f32[36,8,128]{2,1,0:T(8,128)S(1)} %pad_maximum_fusion.2), channel_id=1, source_target_pairs={{0,192},{1,17},{2,194},{3,19},{4,196},{5,21},{6,198},{7,23},{8,24}... | collective-permute-start | bytes 442376 | tf_op jit(solution)/shard_map/ppermute | solution.py:291
  53.1 7.5 %collective-permute-start.18 = (f32[36,8,128]{2,1,0:T(8,128)S(1)}, f32[36,8,128]{2,1,0:T(8,128)S(1)}, u32[]{:S(2)}, u32[]{:S(2)}) collective-permute-start(f32[36,8,128]{2,1,0:T(8,128)S(1)} %pad_maximum_fusion.3), channel_id=1, source_target_pairs={{0,64},{1,49},{2,66},{3,51},{4,68},{5,53},{6,70},{7,55},{8,56},{9,... | collective-permute-start | bytes 442376 | tf_op jit(solution)/shard_map/ppermute | solution.py:291

commit v3 on v2

--- a/solution.py
+++ b/solution.py
@@ -20,7 +20,7 @@
 STEP_Z = (0, 2, 3, 1)
 STEP_Y = (0, 2, 1, 3)
 LATE_Z = (0, 2, 1, 3)
-EARLY_Y = (0, 1, 3, 2)
+EARLY_Y = (0, 2, 1, 3)
 VMEM = pl.BlockSpec(memory_space=pltpu.VMEM)
 SMEM = pl.BlockSpec(memory_space=pltpu.SMEM)
 HBM = pl.BlockSpec(memory_space=pltpu.HBM)

time: 62 us -> 61.4 us (level)
  no operation moved by 1% of the time
where the time goes in v3:
time: 61.4 us; the launch traced here: 61 us
  waiting for transfers between devices  29.6 us (48%)
  starting transfers between devices  25.8 us (42%)
  Pallas kernels  4.67 us (8%)
  between operations  0.77 us (1%)
    ppermute x12, waiting for transfers between devices, swap(): return lax.ppermute(v, ('dom', 'rows'), pairs)  24.5 us
    ppermute x12, starting transfers between devices, swap(): return lax.ppermute(v, ('dom', 'rows'), pairs)  18 us
    ppermute x1, starting transfers between devices, next_slab(): return lax.ppermute(v, ('dom', 'rows'), low + [(b, a) for a, b in low])  7.22 us
    ppermute x1, waiting for transfers between devices, next_slab(): return lax.ppermute(v, ('dom', 'rows'), low + [(b, a) for a, b in low])  2.98 us
    ppermute x6, waiting for transfers between devices, other_core(): return lax.ppermute(v, 'dom', [(i, i ^ 1) for i in range(32)])  2.07 us
    pallas_call x1, Pallas kernels, shards(): pl.pallas_call(first_kernel, out_shape=[strip, strip, halves, halves, gro...  1.92 us
  transfers between devices with their start and end apart: 19, of which 14 were waited for; matrix products, arithmetic and copies ran while one was open for 0% of the time, Pallas kernels for 0%

profile of v3, /device:TPU:6, one launch (start us, length us, event | category | flops | bytes accessed | tf_op | source)
XLA Modules:
  0.0 61.0 jit_solution(1164249621565454253)
XLA Ops:
  0.6 1.9 %shard_map.94 = (f32[8,1536]{1,0:T(8,128)S(1)}, f32[8,1536]{1,0:T(8,128)S(1)}, f32[7,8,1536]{2,1,0:T(8,128)S(1)}, f32[7,8,1536]{2,1,0:T(8,128)S(1)}, f32[3,8,1536]{2,1,0:T(8,128)S(1)}) custom-call(f32[2,16,1536]{2,1,0:T(8,128)} %depth_in.1, f32[2,16,1536]{2,1,0:T(8,128)} %xf_in.1, f32[2,16,1536]{2,1,0:T(8,128)} %yf_in.1, s32[2,16,1536]{2,1,0:T(8,128)} %wet_in.1, ...), custom_call_target="tpu_custom_call" | custom-call | tf_op jit(solution)/shard_map/pallas_call | solution.py:321
  2.7 0.5 collective-permute-start
  3.2 0.7 %collective-permute-done.1 = f32[8,1536]{1,0:T(8,128)S(1)} collective-permute-done((f32[8,1536]{1,0:T(8,128)S(1)}, f32[8,1536]{1,0:T(8,128)S(1)}, u32[]{:S(2)}, u32[]{:S(2)}) %collective-permute-start.1) | collective-permute-done | bytes 49184 | tf_op jit(solution)/shard_map/ppermute | solution.py:303
  3.9 7.2 %collective-permute-start.2 = (f32[16,1536]{1,0:T(8,128)S(1)}, f32[16,1536]{1,0:T(8,128)S(1)}, u32[]{:S(2)}, u32[]{:S(2)}) collective-permute-start(f32[16,1536]{1,0:T(8,128)S(1)} %constant_dynamic-update-slice_fusion.mine), channel_id=1, source_target_pairs={{8,1},{9,2},{10,3},{11,4},{12,5},{13,6},{14,7},{15,0},{24,17},{25,... | collective-permute-start | bytes 294920 | tf_op jit(solution)/shard_map/ppermute | solution.py:308
  11.1 3.0 %collective-permute-done.2.next_slab = f32[16,1536]{1,0:T(8,128)S(1)} collective-permute-done((f32[16,1536]{1,0:T(8,128)S(1)}, f32[16,1536]{1,0:T(8,128)S(1)}, u32[]{:S(2)}, u32[]{:S(2)}) %collective-permute-start.2) | collective-permute-done | bytes 98336 | tf_op jit(solution)/shard_map/ppermute | solution.py:308
  14.1 0.7 %shard_map.95 = (f32[37,8,128]{2,1,0:T(8,128)S(1)}, f32[37,8,128]{2,1,0:T(8,128)S(1)}, f32[37,8,128]{2,1,0:T(8,128)S(1)}, f32[37,8,128]{2,1,0:T(8,128)S(1)}) custom-call(f32[7,8,1536]{2,1,0:T(8,128)S(1)} %get-tuple-element.16.own, f32[7,8,1536]{2,1,0:T(8,128)S(1)} %collective-permute-done.far, f32[3,8,1536]{2,1,0:T(8,128)S(1)} %get-tuple-element.18.terrain, ...), custom_call_target="tpu_custom_call" | custom-call | tf_op jit(solution)/shard_map/pallas_call | solution.py:333
  14.8 4.4 %collective-permute-start.3 = (f32[37,8,128]{2,1,0:T(8,128)S(1)}, f32[37,8,128]{2,1,0:T(8,128)S(1)}, u32[]{:S(2)}, u32[]{:S(2)}) collective-permute-start(f32[37,8,128]{2,1,0:T(8,128)S(1)} %get-tuple-element.22), channel_id=1, source_target_pairs={{0,32},{1,129},{2,34},{3,131},{4,36},{5,133},{6,38},{7,135},{8,136... | collective-permute-start | bytes 454664 | tf_op jit(solution)/shard_map/ppermute | solution.py:291
  19.2 0.7 %collective-permute-start.4 = (f32[37,8,128]{2,1,0:T(8,128)S(1)}, f32[37,8,128]{2,1,0:T(8,128)S(1)}, u32[]{:S(2)}, u32[]{:S(2)}) collective-permute-start(f32[37,8,128]{2,1,0:T(8,128)S(1)} %get-tuple-element.23), channel_id=1, source_target_pairs={{0,16},{1,193},{2,18},{3,195},{4,20},{5,197},{6,22},{7,199},{8,200... | collective-permute-start | bytes 454664 | tf_op jit(solution)/shard_map/ppermute | solution.py:291
  19.9 0.4 collective-permute-start.5
  20.3 2.1 %collective-permute-done.3 = f32[37,8,128]{2,1,0:T(8,128)S(1)} collective-permute-done((f32[37,8,128]{2,1,0:T(8,128)S(1)}, f32[37,8,128]{2,1,0:T(8,128)S(1)}, u32[]{:S(2)}, u32[]{:S(2)}) %collective-permute-start.3) | collective-permute-done | bytes 151584 | tf_op jit(solution)/shard_map/ppermute | solution.py:291
  22.4 2.3 %collective-permute-done.4 = f32[37,8,128]{2,1,0:T(8,128)S(1)} collective-permute-done((f32[37,8,128]{2,1,0:T(8,128)S(1)}, f32[37,8,128]{2,1,0:T(8,128)S(1)}, u32[]{:S(2)}, u32[]{:S(2)}) %collective-permute-start.4) | collective-permute-done | bytes 151584 | tf_op jit(solution)/shard_map/ppermute | solution.py:291
  24.7 1.6 %collective-permute-done.5 = f32[37,8,128]{2,1,0:T(8,128)S(1)} collective-permute-done((f32[37,8,128]{2,1,0:T(8,128)S(1)}, f32[37,8,128]{2,1,0:T(8,128)S(1)}, u32[]{:S(2)}, u32[]{:S(2)}) %collective-permute-start.5) | collective-permute-done | bytes 151584 | tf_op jit(solution)/shard_map/ppermute | solution.py:291
  26.4 3.9 %collective-permute-start.6 = (f32[37,8,128]{2,1,0:T(8,128)S(1)}, f32[37,8,128]{2,1,0:T(8,128)S(1)}, u32[]{:S(2)}, u32[]{:S(2)}) collective-permute-start(f32[37,8,128]{2,1,0:T(8,128)S(1)} %get-tuple-element.63), channel_id=1, source_target_pairs={{0,128},{1,33},{2,130},{3,35},{4,132},{5,37},{6,134},{7,39},{8,40}... | collective-permute-start | bytes 454664 | tf_op jit(solution)/shard_map/ppermute | solution.py:291
  30.2 0.2 collective-permute-start.8
  30.4 0.5 collective-permute-start.7
  30.9 4.2 %collective-permute-done.6.m1 = f32[37,8,128]{2,1,0:T(8,128)S(1)} collective-permute-done((f32[37,8,128]{2,1,0:T(8,128)S(1)}, f32[37,8,128]{2,1,0:T(8,128)S(1)}, u32[]{:S(2)}, u32[]{:S(2)}) %collective-permute-start.6) | collective-permute-done | bytes 151584 | tf_op jit(solution)/shard_map/ppermute | solution.py:291
  35.1 2.3 %collective-permute-done.8.m3 = f32[37,8,128]{2,1,0:T(8,128)S(1)} collective-permute-done((f32[37,8,128]{2,1,0:T(8,128)S(1)}, f32[37,8,128]{2,1,0:T(8,128)S(1)}, u32[]{:S(2)}, u32[]{:S(2)}) %collective-permute-start.8) | collective-permute-done | bytes 151584 | tf_op jit(solution)/shard_map/ppermute | solution.py:291
  37.4 0.9 %collective-permute-done.7.m2 = f32[37,8,128]{2,1,0:T(8,128)S(1)} collective-permute-done((f32[37,8,128]{2,1,0:T(8,128)S(1)}, f32[37,8,128]{2,1,0:T(8,128)S(1)}, u32[]{:S(2)}, u32[]{:S(2)}) %collective-permute-start.7) | collective-permute-done | bytes 151584 | tf_op jit(solution)/shard_map/ppermute | solution.py:291
  38.3 0.5 collective-permute-done.12.t3
  38.7 0.9 %collective-permute-done.11.t2 = f32[37,8,128]{2,1,0:T(8,128)S(1)} collective-permute-done((f32[37,8,128]{2,1,0:T(8,128)S(1)}, f32[37,8,128]{2,1,0:T(8,128)S(1)}, u32[]{:S(2)}, u32[]{:S(2)}) %collective-permute-start.11) | collective-permute-done | bytes 151584 | tf_op jit(solution)/shard_map/ppermute | solution.py:303
  39.6 1.2 %shard_map.96 = (f32[36,8,128]{2,1,0:T(8,128)S(1)}, f32[36,8,128]{2,1,0:T(8,128)S(1)}, f32[36,8,128]{2,1,0:T(8,128)S(1)}, f32[36,8,128]{2,1,0:T(8,128)S(1)}) custom-call(s32[64]{0:T(128)S(1)} %fusion.2.anc, f32[37,8,128]{2,1,0:T(8,128)S(1)} %get-tuple-element.29.m0, f32[37,8,128]{2,1,0:T(8,128)S(1)} %collective-permute-done.6.m1, ...), custom_call_target="tpu_custom_call" | custom-call | tf_op jit(solution)/shard_map/pallas_call | solution.py:347
  40.8 1.3 %collective-permute-start.13 = (f32[36,8,128]{2,1,0:T(8,128)S(1)}, f32[36,8,128]{2,1,0:T(8,128)S(1)}, u32[]{:S(2)}, u32[]{:S(2)}) collective-permute-start(f32[36,8,128]{2,1,0:T(8,128)S(1)} %get-tuple-element.26), channel_id=1, source_target_pairs={{0,32},{1,129},{2,34},{3,131},{4,36},{5,133},{6,38},{7,135},{8,136... | collective-permute-start | bytes 442376 | tf_op jit(solution)/shard_map/ppermute | solution.py:291
  42.1 0.7 %collective-permute-start.14 = (f32[36,8,128]{2,1,0:T(8,128)S(1)}, f32[36,8,128]{2,1,0:T(8,128)S(1)}, u32[]{:S(2)}, u32[]{:S(2)}) collective-permute-start(f32[36,8,128]{2,1,0:T(8,128)S(1)} %get-tuple-element.27), channel_id=1, source_target_pairs={{0,16},{1,193},{2,18},{3,195},{4,20},{5,197},{6,22},{7,199},{8,200... | collective-permute-start | bytes 442376 | tf_op jit(solution)/shard_map/ppermute | solution.py:291
  42.8 2.2 %collective-permute-start.15 = (f32[36,8,128]{2,1,0:T(8,128)S(1)}, f32[36,8,128]{2,1,0:T(8,128)S(1)}, u32[]{:S(2)}, u32[]{:S(2)}) collective-permute-start(f32[36,8,128]{2,1,0:T(8,128)S(1)} %get-tuple-element.28), channel_id=1, source_target_pairs={{0,48},{1,65},{2,50},{3,67},{4,52},{5,69},{6,54},{7,71},{8,72},{9,... | collective-permute-start | bytes 442376 | tf_op jit(solution)/shard_map/ppermute | solution.py:291
  45.0 2.5 %collective-permute-done.13 = f32[36,8,128]{2,1,0:T(8,128)S(1)} collective-permute-done((f32[36,8,128]{2,1,0:T(8,128)S(1)}, f32[36,8,128]{2,1,0:T(8,128)S(1)}, u32[]{:S(2)}, u32[]{:S(2)}) %collective-permute-start.13) | collective-permute-done | bytes 147488 | tf_op jit(solution)/shard_map/ppermute | solution.py:291
  47.6 1.6 %collective-permute-done.15 = f32[36,8,128]{2,1,0:T(8,128)S(1)} collective-permute-done((f32[36,8,128]{2,1,0:T(8,128)S(1)}, f32[36,8,128]{2,1,0:T(8,128)S(1)}, u32[]{:S(2)}, u32[]{:S(2)}) %collective-permute-start.15) | collective-permute-done | bytes 147488 | tf_op jit(solution)/shard_map/ppermute | solution.py:291
  49.2 1.4 %collective-permute-start.16 = (f32[36,8,128]{2,1,0:T(8,128)S(1)}, f32[36,8,128]{2,1,0:T(8,128)S(1)}, u32[]{:S(2)}, u32[]{:S(2)}) collective-permute-start(f32[36,8,128]{2,1,0:T(8,128)S(1)} %pad_maximum_fusion.1), channel_id=1, source_target_pairs={{0,128},{1,33},{2,130},{3,35},{4,132},{5,37},{6,134},{7,39},{8,40}... | collective-permute-start | bytes 442376 | tf_op jit(solution)/shard_map/ppermute | solution.py:291
  50.6 1.9 %collective-permute-start.17 = (f32[36,8,128]{2,1,0:T(8,128)S(1)}, f32[36,8,128]{2,1,0:T(8,128)S(1)}, u32[]{:S(2)}, u32[]{:S(2)}) collective-permute-start(f32[36,8,128]{2,1,0:T(8,128)S(1)} %pad_maximum_fusion.2), channel_id=1, source_target_pairs={{0,192},{1,17},{2,194},{3,19},{4,196},{5,21},{6,198},{7,23},{8,24}... | collective-permute-start | bytes 442376 | tf_op jit(solution)/shard_map/ppermute | solution.py:291
  52.5 0.4 collective-permute-start.18
  53.0 5.6 %collective-permute-done.16.f1 = f32[36,8,128]{2,1,0:T(8,128)S(1)} collective-permute-done((f32[36,8,128]{2,1,0:T(8,128)S(1)}, f32[36,8,128]{2,1,0:T(8,128)S(1)}, u32[]{:S(2)}, u32[]{:S(2)}) %collective-permute-start.16) | collective-permute-done | bytes 147488 | tf_op jit(solution)/shard_map/ppermute | solution.py:291
  58.6 1.5 %collective-permute-done.18.f3 = f32[36,8,128]{2,1,0:T(8,128)S(1)} collective-permute-done((f32[36,8,128]{2,1,0:T(8,128)S(1)}, f32[36,8,128]{2,1,0:T(8,128)S(1)}, u32[]{:S(2)}, u32[]{:S(2)}) %collective-permute-start.18) | collective-permute-done | bytes 147488 | tf_op jit(solution)/shard_map/ppermute | solution.py:291
  60.1 0.9 %shard_map.97 = (f32[2,16,1536]{2,1,0:T(8,128)}, f32[2,16,1536]{2,1,0:T(8,128)}, f32[2,16,1536]{2,1,0:T(8,128)}) custom-call(f32[36,8,128]{2,1,0:T(8,128)S(1)} %pad_maximum_fusion.f0, f32[36,8,128]{2,1,0:T(8,128)S(1)} %collective-permute-done.16.f1, f32[36,8,128]{2,1,0:T(8,128)S(1)} %collective-permute-done.17.f2, f32[36,8,128]{2,1,0:T(8,128)S(1)} %collective-permute-done.18.f3), custom_call_target="tpu_custom_call" | custom-call | tf_op jit(solution)/shard_map/pallas_call | solution.py:358
  (27 shorter events, 0.3 us)
Async XLA Ops:
  2.6 1.3 %collective-permute-start.1 = (f32[8,1536]{1,0:T(8,128)S(1)}, f32[8,1536]{1,0:T(8,128)S(1)}, u32[]{:S(2)}, u32[]{:S(2)}) collective-permute-start(f32[8,1536]{1,0:T(8,128)S(1)} %get-tuple-element.20), channel_id=1, source_target_pairs={{0,8},{8,0},{16,24},{24,16},{32,40},{40,32},{48,56},{56,48},{64,72... | collective-permute-start | bytes 147464 | tf_op jit(solution)/shard_map/ppermute | solution.py:303
  2.7 11.4 %collective-permute-start = (f32[7,8,1536]{2,1,0:T(8,128)S(1)}, f32[7,8,1536]{2,1,0:T(8,128)S(1)}, u32[]{:S(2)}, u32[]{:S(2)}) collective-permute-start(f32[7,8,1536]{2,1,0:T(8,128)S(1)} %get-tuple-element.17), channel_id=1, source_target_pairs={{0,8},{8,0},{16,24},{24,16},{32,40},{40,32},{48,56},{56,48},{64,72... | collective-permute-start | bytes 1032200 | tf_op jit(solution)/shard_map/ppermute | solution.py:303
  3.9 10.2 %collective-permute-start.2 = (f32[16,1536]{1,0:T(8,128)S(1)}, f32[16,1536]{1,0:T(8,128)S(1)}, u32[]{:S(2)}, u32[]{:S(2)}) collective-permute-start(f32[16,1536]{1,0:T(8,128)S(1)} %constant_dynamic-update-slice_fusion.mine), channel_id=1, source_target_pairs={{8,1},{9,2},{10,3},{11,4},{12,5},{13,6},{14,7},{15,0},{24,17},{25,... | collective-permute-start | bytes 294920 | tf_op jit(solution)/shard_map/ppermute | solution.py:308
  14.8 7.6 %collective-permute-start.3 = (f32[37,8,128]{2,1,0:T(8,128)S(1)}, f32[37,8,128]{2,1,0:T(8,128)S(1)}, u32[]{:S(2)}, u32[]{:S(2)}) collective-permute-start(f32[37,8,128]{2,1,0:T(8,128)S(1)} %get-tuple-element.22), channel_id=1, source_target_pairs={{0,32},{1,129},{2,34},{3,131},{4,36},{5,133},{6,38},{7,135},{8,136... | collective-permute-start | bytes 454664 | tf_op jit(solution)/shard_map/ppermute | solution.py:291
  19.2 5.5 %collective-permute-start.4 = (f32[37,8,128]{2,1,0:T(8,128)S(1)}, f32[37,8,128]{2,1,0:T(8,128)S(1)}, u32[]{:S(2)}, u32[]{:S(2)}) collective-permute-start(f32[37,8,128]{2,1,0:T(8,128)S(1)} %get-tuple-element.23), channel_id=1, source_target_pairs={{0,16},{1,193},{2,18},{3,195},{4,20},{5,197},{6,22},{7,199},{8,200... | collective-permute-start | bytes 454664 | tf_op jit(solution)/shard_map/ppermute | solution.py:291
  19.9 6.4 %collective-permute-start.5 = (f32[37,8,128]{2,1,0:T(8,128)S(1)}, f32[37,8,128]{2,1,0:T(8,128)S(1)}, u32[]{:S(2)}, u32[]{:S(2)}) collective-permute-start(f32[37,8,128]{2,1,0:T(8,128)S(1)} %get-tuple-element.24), channel_id=1, source_target_pairs={{0,48},{1,65},{2,50},{3,67},{4,52},{5,69},{6,54},{7,71},{8,72},{9,... | collective-permute-start | bytes 454664 | tf_op jit(solution)/shard_map/ppermute | solution.py:291
  26.4 8.8 %collective-permute-start.6 = (f32[37,8,128]{2,1,0:T(8,128)S(1)}, f32[37,8,128]{2,1,0:T(8,128)S(1)}, u32[]{:S(2)}, u32[]{:S(2)}) collective-permute-start(f32[37,8,128]{2,1,0:T(8,128)S(1)} %get-tuple-element.63), channel_id=1, source_target_pairs={{0,128},{1,33},{2,130},{3,35},{4,132},{5,37},{6,134},{7,39},{8,40}... | collective-permute-start | bytes 454664 | tf_op jit(solution)/shard_map/ppermute | solution.py:291
  30.2 7.1 %collective-permute-start.8 = (f32[37,8,128]{2,1,0:T(8,128)S(1)}, f32[37,8,128]{2,1,0:T(8,128)S(1)}, u32[]{:S(2)}, u32[]{:S(2)}) collective-permute-start(f32[37,8,128]{2,1,0:T(8,128)S(1)} %get-tuple-element.64), channel_id=1, source_target_pairs={{0,192},{1,49},{2,194},{3,51},{4,196},{5,53},{6,198},{7,55},{8,56}... | collective-permute-start | bytes 454664 | tf_op jit(solution)/shard_map/ppermute | solution.py:291
  30.4 7.9 %collective-permute-start.7 = (f32[37,8,128]{2,1,0:T(8,128)S(1)}, f32[37,8,128]{2,1,0:T(8,128)S(1)}, u32[]{:S(2)}, u32[]{:S(2)}) collective-permute-start(f32[37,8,128]{2,1,0:T(8,128)S(1)} %get-tuple-element.65), channel_id=1, source_target_pairs={{0,64},{1,17},{2,66},{3,19},{4,68},{5,21},{6,70},{7,23},{8,24},{9,... | collective-permute-start | bytes 454664 | tf_op jit(solution)/shard_map/ppermute | solution.py:291
  30.9 7.4 %collective-permute-start.9 = (f32[37,8,128]{2,1,0:T(8,128)S(1)}, f32[37,8,128]{2,1,0:T(8,128)S(1)}, u32[]{:S(2)}, u32[]{:S(2)}) collective-permute-start(f32[37,8,128]{2,1,0:T(8,128)S(1)} %get-tuple-element.29.m0), channel_id=1, source_target_pairs={{0,8},{8,0},{16,24},{24,16},{32,40},{40,32},{48,56},{56,48},{64,72... | collective-permute-start | bytes 454664 | tf_op jit(solution)/shard_map/ppermute | solution.py:303
  35.1 3.2 %collective-permute-start.10 = (f32[37,8,128]{2,1,0:T(8,128)S(1)}, f32[37,8,128]{2,1,0:T(8,128)S(1)}, u32[]{:S(2)}, u32[]{:S(2)}) collective-permute-start(f32[37,8,128]{2,1,0:T(8,128)S(1)} %collective-permute-done.6.m1), channel_id=1, source_target_pairs={{0,8},{8,0},{16,24},{24,16},{32,40},{40,32},{48,56},{56,48},{64,72... | collective-permute-start | bytes 454664 | tf_op jit(solution)/shard_map/ppermute | solution.py:303
  37.4 1.4 %collective-permute-start.12 = (f32[37,8,128]{2,1,0:T(8,128)S(1)}, f32[37,8,128]{2,1,0:T(8,128)S(1)}, u32[]{:S(2)}, u32[]{:S(2)}) collective-permute-start(f32[37,8,128]{2,1,0:T(8,128)S(1)} %collective-permute-done.8.m3), channel_id=1, source_target_pairs={{0,8},{8,0},{16,24},{24,16},{32,40},{40,32},{48,56},{56,48},{64,72... | collective-permute-start | bytes 454664 | tf_op jit(solution)/shard_map/ppermute | solution.py:303
  38.3 1.4 %collective-permute-start.11 = (f32[37,8,128]{2,1,0:T(8,128)S(1)}, f32[37,8,128]{2,1,0:T(8,128)S(1)}, u32[]{:S(2)}, u32[]{:S(2)}) collective-permute-start(f32[37,8,128]{2,1,0:T(8,128)S(1)} %collective-permute-done.7.m2), channel_id=1, source_target_pairs={{0,8},{8,0},{16,24},{24,16},{32,40},{40,32},{48,56},{56,48},{64,72... | collective-permute-start | bytes 454664 | tf_op jit(solution)/shard_map/ppermute | solution.py:303
  40.8 6.7 %collective-permute-start.13 = (f32[36,8,128]{2,1,0:T(8,128)S(1)}, f32[36,8,128]{2,1,0:T(8,128)S(1)}, u32[]{:S(2)}, u32[]{:S(2)}) collective-permute-start(f32[36,8,128]{2,1,0:T(8,128)S(1)} %get-tuple-element.26), channel_id=1, source_target_pairs={{0,32},{1,129},{2,34},{3,131},{4,36},{5,133},{6,38},{7,135},{8,136... | collective-permute-start | bytes 442376 | tf_op jit(solution)/shard_map/ppermute | solution.py:291
  42.1 5.4 %collective-permute-start.14 = (f32[36,8,128]{2,1,0:T(8,128)S(1)}, f32[36,8,128]{2,1,0:T(8,128)S(1)}, u32[]{:S(2)}, u32[]{:S(2)}) collective-permute-start(f32[36,8,128]{2,1,0:T(8,128)S(1)} %get-tuple-element.27), channel_id=1, source_target_pairs={{0,16},{1,193},{2,18},{3,195},{4,20},{5,197},{6,22},{7,199},{8,200... | collective-permute-start | bytes 442376 | tf_op jit(solution)/shard_map/ppermute | solution.py:291
  42.8 6.4 %collective-permute-start.15 = (f32[36,8,128]{2,1,0:T(8,128)S(1)}, f32[36,8,128]{2,1,0:T(8,128)S(1)}, u32[]{:S(2)}, u32[]{:S(2)}) collective-permute-start(f32[36,8,128]{2,1,0:T(8,128)S(1)} %get-tuple-element.28), channel_id=1, source_target_pairs={{0,48},{1,65},{2,50},{3,67},{4,52},{5,69},{6,54},{7,71},{8,72},{9,... | collective-permute-start | bytes 442376 | tf_op jit(solution)/shard_map/ppermute | solution.py:291
  49.2 9.4 %collective-permute-start.16 = (f32[36,8,128]{2,1,0:T(8,128)S(1)}, f32[36,8,128]{2,1,0:T(8,128)S(1)}, u32[]{:S(2)}, u32[]{:S(2)}) collective-permute-start(f32[36,8,128]{2,1,0:T(8,128)S(1)} %pad_maximum_fusion.1), channel_id=1, source_target_pairs={{0,128},{1,33},{2,130},{3,35},{4,132},{5,37},{6,134},{7,39},{8,40}... | collective-permute-start | bytes 442376 | tf_op jit(solution)/shard_map/ppermute | solution.py:291
  50.6 8.0 %collective-permute-start.17 = (f32[36,8,128]{2,1,0:T(8,128)S(1)}, f32[36,8,128]{2,1,0:T(8,128)S(1)}, u32[]{:S(2)}, u32[]{:S(2)}) collective-permute-start(f32[36,8,128]{2,1,0:T(8,128)S(1)} %pad_maximum_fusion.2), channel_id=1, source_target_pairs={{0,192},{1,17},{2,194},{3,19},{4,196},{5,21},{6,198},{7,23},{8,24}... | collective-permute-start | bytes 442376 | tf_op jit(solution)/shard_map/ppermute | solution.py:291
  52.5 7.5 %collective-permute-start.18 = (f32[36,8,128]{2,1,0:T(8,128)S(1)}, f32[36,8,128]{2,1,0:T(8,128)S(1)}, u32[]{:S(2)}, u32[]{:S(2)}) collective-permute-start(f32[36,8,128]{2,1,0:T(8,128)S(1)} %pad_maximum_fusion.3), channel_id=1, source_target_pairs={{0,64},{1,49},{2,66},{3,51},{4,68},{5,53},{6,70},{7,55},{8,56},{9,... | collective-permute-start | bytes 442376 | tf_op jit(solution)/shard_map/ppermute | solution.py:291

commit v4 on v3

--- a/solution.py
+++ b/solution.py
@@ -17,9 +17,9 @@
 PER = 9
 ITEMS = [(d, f, 3 * z + t) for z in range(4) for d in range(4) for f in range(3) for t in range(3)]
 AT = {item: n for n, item in enumerate(ITEMS)}
-STEP_Z = (0, 2, 3, 1)
+STEP_Z = (0, 3, 2, 1)
 STEP_Y = (0, 2, 1, 3)
-LATE_Z = (0, 2, 1, 3)
+LATE_Z = (0, 3, 1, 2)
 EARLY_Y = (0, 2, 1, 3)
 VMEM = pl.BlockSpec(memory_space=pltpu.VMEM)
 SMEM = pl.BlockSpec(memory_space=pltpu.SMEM)

time: 61.4 us -> 61.2 us (level)
  waiting for transfers between devices: 29.6 us -> 27.8 us
  starting transfers between devices: 25.8 us -> 27.1 us
    ppermute x12, waiting for transfers between devices: 24.5 us -> 23 us  [swap(): return lax.ppermute(v, ('dom', 'rows'), pairs)]
    ppermute x12, starting transfers between devices: 18 us -> 18.8 us  [swap(): return lax.ppermute(v, ('dom', 'rows'), pairs)]
  transfers between devices with their start and end apart: 19 -> 19, of which waited for: 14 -> 13; matrix products, arithmetic and copies ran while one was open for 0% -> 0% of each run, Pallas kernels for 0% -> 0%
where the time goes in v4:
time: 61.2 us; the launch traced here: 60.5 us
  waiting for transfers between devices  27.8 us (45%)
  starting transfers between devices  27.1 us (44%)
  Pallas kernels  4.68 us (8%)
  between operations  0.78 us (1%)
    ppermute x12, waiting for transfers between devices, swap(): return lax.ppermute(v, ('dom', 'rows'), pairs)  23 us
    ppermute x12, starting transfers between devices, swap(): return lax.ppermute(v, ('dom', 'rows'), pairs)  18.8 us
    ppermute x1, starting transfers between devices, next_slab(): return lax.ppermute(v, ('dom', 'rows'), low + [(b, a) for a, b in low])  7.22 us
    ppermute x1, waiting for transfers between devices, next_slab(): return lax.ppermute(v, ('dom', 'rows'), low + [(b, a) for a, b in low])  2.98 us
    pallas_call x1, Pallas kernels, shards(): pl.pallas_call(first_kernel, out_shape=[strip, strip, halves, halves, gro...  1.92 us
    ppermute x6, waiting for transfers between devices, other_core(): return lax.ppermute(v, 'dom', [(i, i ^ 1) for i in range(32)])  1.78 us
  transfers between devices with their start and end apart: 19, of which 13 were waited for; matrix products, arithmetic and copies ran while one was open for 0% of the time, Pallas kernels for 0%

profile of v4, /device:TPU:6, one launch (start us, length us, event | category | flops | bytes accessed | tf_op | source)
XLA Modules:
  0.0 60.5 jit_solution(323705042423515713)
XLA Ops:
  0.6 1.9 %shard_map.94 = (f32[8,1536]{1,0:T(8,128)S(1)}, f32[8,1536]{1,0:T(8,128)S(1)}, f32[7,8,1536]{2,1,0:T(8,128)S(1)}, f32[7,8,1536]{2,1,0:T(8,128)S(1)}, f32[3,8,1536]{2,1,0:T(8,128)S(1)}) custom-call(f32[2,16,1536]{2,1,0:T(8,128)} %depth_in.1, f32[2,16,1536]{2,1,0:T(8,128)} %xf_in.1, f32[2,16,1536]{2,1,0:T(8,128)} %yf_in.1, s32[2,16,1536]{2,1,0:T(8,128)} %wet_in.1, ...), custom_call_target="tpu_custom_call" | custom-call | tf_op jit(solution)/shard_map/pallas_call | solution.py:321
  2.7 0.5 collective-permute-start
  3.2 0.7 %collective-permute-done.1 = f32[8,1536]{1,0:T(8,128)S(1)} collective-permute-done((f32[8,1536]{1,0:T(8,128)S(1)}, f32[8,1536]{1,0:T(8,128)S(1)}, u32[]{:S(2)}, u32[]{:S(2)}) %collective-permute-start.1) | collective-permute-done | bytes 49184 | tf_op jit(solution)/shard_map/ppermute | solution.py:303
  3.9 7.2 %collective-permute-start.2 = (f32[16,1536]{1,0:T(8,128)S(1)}, f32[16,1536]{1,0:T(8,128)S(1)}, u32[]{:S(2)}, u32[]{:S(2)}) collective-permute-start(f32[16,1536]{1,0:T(8,128)S(1)} %constant_dynamic-update-slice_fusion.mine), channel_id=1, source_target_pairs={{8,1},{9,2},{10,3},{11,4},{12,5},{13,6},{14,7},{15,0},{24,17},{25,... | collective-permute-start | bytes 294920 | tf_op jit(solution)/shard_map/ppermute | solution.py:308
  11.1 3.0 %collective-permute-done.2.next_slab = f32[16,1536]{1,0:T(8,128)S(1)} collective-permute-done((f32[16,1536]{1,0:T(8,128)S(1)}, f32[16,1536]{1,0:T(8,128)S(1)}, u32[]{:S(2)}, u32[]{:S(2)}) %collective-permute-start.2) | collective-permute-done | bytes 98336 | tf_op jit(solution)/shard_map/ppermute | solution.py:308
  14.1 0.7 %shard_map.95 = (f32[37,8,128]{2,1,0:T(8,128)S(1)}, f32[37,8,128]{2,1,0:T(8,128)S(1)}, f32[37,8,128]{2,1,0:T(8,128)S(1)}, f32[37,8,128]{2,1,0:T(8,128)S(1)}) custom-call(f32[7,8,1536]{2,1,0:T(8,128)S(1)} %get-tuple-element.16.own, f32[7,8,1536]{2,1,0:T(8,128)S(1)} %collective-permute-done.far, f32[3,8,1536]{2,1,0:T(8,128)S(1)} %get-tuple-element.18.terrain, ...), custom_call_target="tpu_custom_call" | custom-call | tf_op jit(solution)/shard_map/pallas_call | solution.py:333
  14.8 4.4 %collective-permute-start.3 = (f32[37,8,128]{2,1,0:T(8,128)S(1)}, f32[37,8,128]{2,1,0:T(8,128)S(1)}, u32[]{:S(2)}, u32[]{:S(2)}) collective-permute-start(f32[37,8,128]{2,1,0:T(8,128)S(1)} %get-tuple-element.22), channel_id=1, source_target_pairs={{0,32},{1,193},{2,34},{3,195},{4,36},{5,197},{6,38},{7,199},{8,200... | collective-permute-start | bytes 454664 | tf_op jit(solution)/shard_map/ppermute | solution.py:291
  19.2 0.7 %collective-permute-start.4 = (f32[37,8,128]{2,1,0:T(8,128)S(1)}, f32[37,8,128]{2,1,0:T(8,128)S(1)}, u32[]{:S(2)}, u32[]{:S(2)}) collective-permute-start(f32[37,8,128]{2,1,0:T(8,128)S(1)} %get-tuple-element.23), channel_id=1, source_target_pairs={{0,16},{1,129},{2,18},{3,131},{4,20},{5,133},{6,22},{7,135},{8,136... | collective-permute-start | bytes 454664 | tf_op jit(solution)/shard_map/ppermute | solution.py:291
  19.9 0.4 collective-permute-start.5
  20.3 2.1 %collective-permute-done.3 = f32[37,8,128]{2,1,0:T(8,128)S(1)} collective-permute-done((f32[37,8,128]{2,1,0:T(8,128)S(1)}, f32[37,8,128]{2,1,0:T(8,128)S(1)}, u32[]{:S(2)}, u32[]{:S(2)}) %collective-permute-start.3) | collective-permute-done | bytes 151584 | tf_op jit(solution)/shard_map/ppermute | solution.py:291
  22.4 2.3 %collective-permute-done.4 = f32[37,8,128]{2,1,0:T(8,128)S(1)} collective-permute-done((f32[37,8,128]{2,1,0:T(8,128)S(1)}, f32[37,8,128]{2,1,0:T(8,128)S(1)}, u32[]{:S(2)}, u32[]{:S(2)}) %collective-permute-start.4) | collective-permute-done | bytes 151584 | tf_op jit(solution)/shard_map/ppermute | solution.py:291
  24.7 1.6 %collective-permute-done.5 = f32[37,8,128]{2,1,0:T(8,128)S(1)} collective-permute-done((f32[37,8,128]{2,1,0:T(8,128)S(1)}, f32[37,8,128]{2,1,0:T(8,128)S(1)}, u32[]{:S(2)}, u32[]{:S(2)}) %collective-permute-start.5) | collective-permute-done | bytes 151584 | tf_op jit(solution)/shard_map/ppermute | solution.py:291
  26.4 3.0 %collective-permute-start.6 = (f32[37,8,128]{2,1,0:T(8,128)S(1)}, f32[37,8,128]{2,1,0:T(8,128)S(1)}, u32[]{:S(2)}, u32[]{:S(2)}) collective-permute-start(f32[37,8,128]{2,1,0:T(8,128)S(1)} %get-tuple-element.63), channel_id=1, source_target_pairs={{0,192},{1,33},{2,194},{3,35},{4,196},{5,37},{6,198},{7,39},{8,40}... | collective-permute-start | bytes 454664 | tf_op jit(solution)/shard_map/ppermute | solution.py:291
  29.3 1.0 %collective-permute-start.8 = (f32[37,8,128]{2,1,0:T(8,128)S(1)}, f32[37,8,128]{2,1,0:T(8,128)S(1)}, u32[]{:S(2)}, u32[]{:S(2)}) collective-permute-start(f32[37,8,128]{2,1,0:T(8,128)S(1)} %get-tuple-element.64), channel_id=1, source_target_pairs={{0,128},{1,49},{2,130},{3,51},{4,132},{5,53},{6,134},{7,55},{8,56}... | collective-permute-start | bytes 454664 | tf_op jit(solution)/shard_map/ppermute | solution.py:291
  30.3 0.5 collective-permute-start.7
  30.8 2.7 %collective-permute-done.6.m1 = f32[37,8,128]{2,1,0:T(8,128)S(1)} collective-permute-done((f32[37,8,128]{2,1,0:T(8,128)S(1)}, f32[37,8,128]{2,1,0:T(8,128)S(1)}, u32[]{:S(2)}, u32[]{:S(2)}) %collective-permute-start.6) | collective-permute-done | bytes 151584 | tf_op jit(solution)/shard_map/ppermute | solution.py:291
  33.5 4.7 %collective-permute-done.8.m3 = f32[37,8,128]{2,1,0:T(8,128)S(1)} collective-permute-done((f32[37,8,128]{2,1,0:T(8,128)S(1)}, f32[37,8,128]{2,1,0:T(8,128)S(1)}, u32[]{:S(2)}, u32[]{:S(2)}) %collective-permute-start.8) | collective-permute-done | bytes 151584 | tf_op jit(solution)/shard_map/ppermute | solution.py:291
  38.3 0.5 collective-permute-start.11
  38.8 0.8 %collective-permute-done.12.t3 = f32[37,8,128]{2,1,0:T(8,128)S(1)} collective-permute-done((f32[37,8,128]{2,1,0:T(8,128)S(1)}, f32[37,8,128]{2,1,0:T(8,128)S(1)}, u32[]{:S(2)}, u32[]{:S(2)}) %collective-permute-start.12) | collective-permute-done | bytes 151584 | tf_op jit(solution)/shard_map/ppermute | solution.py:303
  39.6 0.2 collective-permute-done.11.t2
  39.8 1.2 %shard_map.96 = (f32[36,8,128]{2,1,0:T(8,128)S(1)}, f32[36,8,128]{2,1,0:T(8,128)S(1)}, f32[36,8,128]{2,1,0:T(8,128)S(1)}, f32[36,8,128]{2,1,0:T(8,128)S(1)}) custom-call(s32[64]{0:T(128)S(1)} %fusion.2.anc, f32[37,8,128]{2,1,0:T(8,128)S(1)} %get-tuple-element.29.m0, f32[37,8,128]{2,1,0:T(8,128)S(1)} %collective-permute-done.6.m1, ...), custom_call_target="tpu_custom_call" | custom-call | tf_op jit(solution)/shard_map/pallas_call | solution.py:347
  41.0 1.3 %collective-permute-start.13 = (f32[36,8,128]{2,1,0:T(8,128)S(1)}, f32[36,8,128]{2,1,0:T(8,128)S(1)}, u32[]{:S(2)}, u32[]{:S(2)}) collective-permute-start(f32[36,8,128]{2,1,0:T(8,128)S(1)} %get-tuple-element.26), channel_id=1, source_target_pairs={{0,32},{1,193},{2,34},{3,195},{4,36},{5,197},{6,38},{7,199},{8,200... | collective-permute-start | bytes 442376 | tf_op jit(solution)/shard_map/ppermute | solution.py:291
  42.4 0.7 %collective-permute-start.14 = (f32[36,8,128]{2,1,0:T(8,128)S(1)}, f32[36,8,128]{2,1,0:T(8,128)S(1)}, u32[]{:S(2)}, u32[]{:S(2)}) collective-permute-start(f32[36,8,128]{2,1,0:T(8,128)S(1)} %get-tuple-element.27), channel_id=1, source_target_pairs={{0,16},{1,129},{2,18},{3,131},{4,20},{5,133},{6,22},{7,135},{8,136... | collective-permute-start | bytes 442376 | tf_op jit(solution)/shard_map/ppermute | solution.py:291
  43.0 2.2 %collective-permute-start.15 = (f32[36,8,128]{2,1,0:T(8,128)S(1)}, f32[36,8,128]{2,1,0:T(8,128)S(1)}, u32[]{:S(2)}, u32[]{:S(2)}) collective-permute-start(f32[36,8,128]{2,1,0:T(8,128)S(1)} %get-tuple-element.28), channel_id=1, source_target_pairs={{0,48},{1,65},{2,50},{3,67},{4,52},{5,69},{6,54},{7,71},{8,72},{9,... | collective-permute-start | bytes 442376 | tf_op jit(solution)/shard_map/ppermute | solution.py:291
  45.2 2.5 %collective-permute-done.13 = f32[36,8,128]{2,1,0:T(8,128)S(1)} collective-permute-done((f32[36,8,128]{2,1,0:T(8,128)S(1)}, f32[36,8,128]{2,1,0:T(8,128)S(1)}, u32[]{:S(2)}, u32[]{:S(2)}) %collective-permute-start.13) | collective-permute-done | bytes 147488 | tf_op jit(solution)/shard_map/ppermute | solution.py:291
  47.8 1.6 %collective-permute-done.15 = f32[36,8,128]{2,1,0:T(8,128)S(1)} collective-permute-done((f32[36,8,128]{2,1,0:T(8,128)S(1)}, f32[36,8,128]{2,1,0:T(8,128)S(1)}, u32[]{:S(2)}, u32[]{:S(2)}) %collective-permute-start.15) | collective-permute-done | bytes 147488 | tf_op jit(solution)/shard_map/ppermute | solution.py:291
  49.4 3.0 %collective-permute-start.16 = (f32[36,8,128]{2,1,0:T(8,128)S(1)}, f32[36,8,128]{2,1,0:T(8,128)S(1)}, u32[]{:S(2)}, u32[]{:S(2)}) collective-permute-start(f32[36,8,128]{2,1,0:T(8,128)S(1)} %pad_maximum_fusion.1), channel_id=1, source_target_pairs={{0,192},{1,33},{2,194},{3,35},{4,196},{5,37},{6,198},{7,39},{8,40}... | collective-permute-start | bytes 442376 | tf_op jit(solution)/shard_map/ppermute | solution.py:291
  52.4 0.1 collective-permute-start.17
  52.6 1.5 %collective-permute-start.18 = (f32[36,8,128]{2,1,0:T(8,128)S(1)}, f32[36,8,128]{2,1,0:T(8,128)S(1)}, u32[]{:S(2)}, u32[]{:S(2)}) collective-permute-start(f32[36,8,128]{2,1,0:T(8,128)S(1)} %pad_maximum_fusion.3), channel_id=1, source_target_pairs={{0,64},{1,49},{2,66},{3,51},{4,68},{5,53},{6,70},{7,55},{8,56},{9,... | collective-permute-start | bytes 442376 | tf_op jit(solution)/shard_map/ppermute | solution.py:291
  54.1 2.4 %collective-permute-done.16.f1 = f32[36,8,128]{2,1,0:T(8,128)S(1)} collective-permute-done((f32[36,8,128]{2,1,0:T(8,128)S(1)}, f32[36,8,128]{2,1,0:T(8,128)S(1)}, u32[]{:S(2)}, u32[]{:S(2)}) %collective-permute-start.16) | collective-permute-done | bytes 147488 | tf_op jit(solution)/shard_map/ppermute | solution.py:291
  56.5 3.1 %collective-permute-done.17.f2 = f32[36,8,128]{2,1,0:T(8,128)S(1)} collective-permute-done((f32[36,8,128]{2,1,0:T(8,128)S(1)}, f32[36,8,128]{2,1,0:T(8,128)S(1)}, u32[]{:S(2)}, u32[]{:S(2)}) %collective-permute-start.17) | collective-permute-done | bytes 147488 | tf_op jit(solution)/shard_map/ppermute | solution.py:291
  59.6 0.9 %shard_map.97 = (f32[2,16,1536]{2,1,0:T(8,128)}, f32[2,16,1536]{2,1,0:T(8,128)}, f32[2,16,1536]{2,1,0:T(8,128)}) custom-call(f32[36,8,128]{2,1,0:T(8,128)S(1)} %pad_maximum_fusion.f0, f32[36,8,128]{2,1,0:T(8,128)S(1)} %collective-permute-done.16.f1, f32[36,8,128]{2,1,0:T(8,128)S(1)} %collective-permute-done.17.f2, f32[36,8,128]{2,1,0:T(8,128)S(1)} %collective-permute-done.18.f3), custom_call_target="tpu_custom_call" | custom-call | tf_op jit(solution)/shard_map/pallas_call | solution.py:358
  (27 shorter events, 0.3 us)
Async XLA Ops:
  2.6 1.3 %collective-permute-start.1 = (f32[8,1536]{1,0:T(8,128)S(1)}, f32[8,1536]{1,0:T(8,128)S(1)}, u32[]{:S(2)}, u32[]{:S(2)}) collective-permute-start(f32[8,1536]{1,0:T(8,128)S(1)} %get-tuple-element.20), channel_id=1, source_target_pairs={{0,8},{8,0},{16,24},{24,16},{32,40},{40,32},{48,56},{56,48},{64,72... | collective-permute-start | bytes 147464 | tf_op jit(solution)/shard_map/ppermute | solution.py:303
  2.7 11.4 %collective-permute-start = (f32[7,8,1536]{2,1,0:T(8,128)S(1)}, f32[7,8,1536]{2,1,0:T(8,128)S(1)}, u32[]{:S(2)}, u32[]{:S(2)}) collective-permute-start(f32[7,8,1536]{2,1,0:T(8,128)S(1)} %get-tuple-element.17), channel_id=1, source_target_pairs={{0,8},{8,0},{16,24},{24,16},{32,40},{40,32},{48,56},{56,48},{64,72... | collective-permute-start | bytes 1032200 | tf_op jit(solution)/shard_map/ppermute | solution.py:303
  3.9 10.2 %collective-permute-start.2 = (f32[16,1536]{1,0:T(8,128)S(1)}, f32[16,1536]{1,0:T(8,128)S(1)}, u32[]{:S(2)}, u32[]{:S(2)}) collective-permute-start(f32[16,1536]{1,0:T(8,128)S(1)} %constant_dynamic-update-slice_fusion.mine), channel_id=1, source_target_pairs={{8,1},{9,2},{10,3},{11,4},{12,5},{13,6},{14,7},{15,0},{24,17},{25,... | collective-permute-start | bytes 294920 | tf_op jit(solution)/shard_map/ppermute | solution.py:308
  14.8 7.6 %collective-permute-start.3 = (f32[37,8,128]{2,1,0:T(8,128)S(1)}, f32[37,8,128]{2,1,0:T(8,128)S(1)}, u32[]{:S(2)}, u32[]{:S(2)}) collective-permute-start(f32[37,8,128]{2,1,0:T(8,128)S(1)} %get-tuple-element.22), channel_id=1, source_target_pairs={{0,32},{1,193},{2,34},{3,195},{4,36},{5,197},{6,38},{7,199},{8,200... | collective-permute-start | bytes 454664 | tf_op jit(solution)/shard_map/ppermute | solution.py:291
  19.2 5.5 %collective-permute-start.4 = (f32[37,8,128]{2,1,0:T(8,128)S(1)}, f32[37,8,128]{2,1,0:T(8,128)S(1)}, u32[]{:S(2)}, u32[]{:S(2)}) collective-permute-start(f32[37,8,128]{2,1,0:T(8,128)S(1)} %get-tuple-element.23), channel_id=1, source_target_pairs={{0,16},{1,129},{2,18},{3,131},{4,20},{5,133},{6,22},{7,135},{8,136... | collective-permute-start | bytes 454664 | tf_op jit(solution)/shard_map/ppermute | solution.py:291
  19.9 6.4 %collective-permute-start.5 = (f32[37,8,128]{2,1,0:T(8,128)S(1)}, f32[37,8,128]{2,1,0:T(8,128)S(1)}, u32[]{:S(2)}, u32[]{:S(2)}) collective-permute-start(f32[37,8,128]{2,1,0:T(8,128)S(1)} %get-tuple-element.24), channel_id=1, source_target_pairs={{0,48},{1,65},{2,50},{3,67},{4,52},{5,69},{6,54},{7,71},{8,72},{9,... | collective-permute-start | bytes 454664 | tf_op jit(solution)/shard_map/ppermute | solution.py:291
  26.4 7.2 %collective-permute-start.6 = (f32[37,8,128]{2,1,0:T(8,128)S(1)}, f32[37,8,128]{2,1,0:T(8,128)S(1)}, u32[]{:S(2)}, u32[]{:S(2)}) collective-permute-start(f32[37,8,128]{2,1,0:T(8,128)S(1)} %get-tuple-element.63), channel_id=1, source_target_pairs={{0,192},{1,33},{2,194},{3,35},{4,196},{5,37},{6,198},{7,39},{8,40}... | collective-permute-start | bytes 454664 | tf_op jit(solution)/shard_map/ppermute | solution.py:291
  29.3 8.9 %collective-permute-start.8 = (f32[37,8,128]{2,1,0:T(8,128)S(1)}, f32[37,8,128]{2,1,0:T(8,128)S(1)}, u32[]{:S(2)}, u32[]{:S(2)}) collective-permute-start(f32[37,8,128]{2,1,0:T(8,128)S(1)} %get-tuple-element.64), channel_id=1, source_target_pairs={{0,128},{1,49},{2,130},{3,51},{4,132},{5,53},{6,134},{7,55},{8,56}... | collective-permute-start | bytes 454664 | tf_op jit(solution)/shard_map/ppermute | solution.py:291
  30.3 7.9 %collective-permute-start.7 = (f32[37,8,128]{2,1,0:T(8,128)S(1)}, f32[37,8,128]{2,1,0:T(8,128)S(1)}, u32[]{:S(2)}, u32[]{:S(2)}) collective-permute-start(f32[37,8,128]{2,1,0:T(8,128)S(1)} %get-tuple-element.65), channel_id=1, source_target_pairs={{0,64},{1,17},{2,66},{3,19},{4,68},{5,21},{6,70},{7,23},{8,24},{9,... | collective-permute-start | bytes 454664 | tf_op jit(solution)/shard_map/ppermute | solution.py:291
  30.8 8.0 %collective-permute-start.9 = (f32[37,8,128]{2,1,0:T(8,128)S(1)}, f32[37,8,128]{2,1,0:T(8,128)S(1)}, u32[]{:S(2)}, u32[]{:S(2)}) collective-permute-start(f32[37,8,128]{2,1,0:T(8,128)S(1)} %get-tuple-element.29.m0), channel_id=1, source_target_pairs={{0,8},{8,0},{16,24},{24,16},{32,40},{40,32},{48,56},{56,48},{64,72... | collective-permute-start | bytes 454664 | tf_op jit(solution)/shard_map/ppermute | solution.py:303
  33.5 5.3 %collective-permute-start.10 = (f32[37,8,128]{2,1,0:T(8,128)S(1)}, f32[37,8,128]{2,1,0:T(8,128)S(1)}, u32[]{:S(2)}, u32[]{:S(2)}) collective-permute-start(f32[37,8,128]{2,1,0:T(8,128)S(1)} %collective-permute-done.6.m1), channel_id=1, source_target_pairs={{0,8},{8,0},{16,24},{24,16},{32,40},{40,32},{48,56},{56,48},{64,72... | collective-permute-start | bytes 454664 | tf_op jit(solution)/shard_map/ppermute | solution.py:303
  38.3 1.4 %collective-permute-start.12 = (f32[37,8,128]{2,1,0:T(8,128)S(1)}, f32[37,8,128]{2,1,0:T(8,128)S(1)}, u32[]{:S(2)}, u32[]{:S(2)}) collective-permute-start(f32[37,8,128]{2,1,0:T(8,128)S(1)} %collective-permute-done.8.m3), channel_id=1, source_target_pairs={{0,8},{8,0},{16,24},{24,16},{32,40},{40,32},{48,56},{56,48},{64,72... | collective-permute-start | bytes 454664 | tf_op jit(solution)/shard_map/ppermute | solution.py:303
  38.3 1.6 %collective-permute-start.11 = (f32[37,8,128]{2,1,0:T(8,128)S(1)}, f32[37,8,128]{2,1,0:T(8,128)S(1)}, u32[]{:S(2)}, u32[]{:S(2)}) collective-permute-start(f32[37,8,128]{2,1,0:T(8,128)S(1)} %collective-permute-done.7.m2), channel_id=1, source_target_pairs={{0,8},{8,0},{16,24},{24,16},{32,40},{40,32},{48,56},{56,48},{64,72... | collective-permute-start | bytes 454664 | tf_op jit(solution)/shard_map/ppermute | solution.py:303
  41.0 6.7 %collective-permute-start.13 = (f32[36,8,128]{2,1,0:T(8,128)S(1)}, f32[36,8,128]{2,1,0:T(8,128)S(1)}, u32[]{:S(2)}, u32[]{:S(2)}) collective-permute-start(f32[36,8,128]{2,1,0:T(8,128)S(1)} %get-tuple-element.26), channel_id=1, source_target_pairs={{0,32},{1,193},{2,34},{3,195},{4,36},{5,197},{6,38},{7,199},{8,200... | collective-permute-start | bytes 442376 | tf_op jit(solution)/shard_map/ppermute | solution.py:291
  42.4 5.4 %collective-permute-start.14 = (f32[36,8,128]{2,1,0:T(8,128)S(1)}, f32[36,8,128]{2,1,0:T(8,128)S(1)}, u32[]{:S(2)}, u32[]{:S(2)}) collective-permute-start(f32[36,8,128]{2,1,0:T(8,128)S(1)} %get-tuple-element.27), channel_id=1, source_target_pairs={{0,16},{1,129},{2,18},{3,131},{4,20},{5,133},{6,22},{7,135},{8,136... | collective-permute-start | bytes 442376 | tf_op jit(solution)/shard_map/ppermute | solution.py:291
  43.0 6.4 %collective-permute-start.15 = (f32[36,8,128]{2,1,0:T(8,128)S(1)}, f32[36,8,128]{2,1,0:T(8,128)S(1)}, u32[]{:S(2)}, u32[]{:S(2)}) collective-permute-start(f32[36,8,128]{2,1,0:T(8,128)S(1)} %get-tuple-element.28), channel_id=1, source_target_pairs={{0,48},{1,65},{2,50},{3,67},{4,52},{5,69},{6,54},{7,71},{8,72},{9,... | collective-permute-start | bytes 442376 | tf_op jit(solution)/shard_map/ppermute | solution.py:291
  49.4 7.1 %collective-permute-start.16 = (f32[36,8,128]{2,1,0:T(8,128)S(1)}, f32[36,8,128]{2,1,0:T(8,128)S(1)}, u32[]{:S(2)}, u32[]{:S(2)}) collective-permute-start(f32[36,8,128]{2,1,0:T(8,128)S(1)} %pad_maximum_fusion.1), channel_id=1, source_target_pairs={{0,192},{1,33},{2,194},{3,35},{4,196},{5,37},{6,198},{7,39},{8,40}... | collective-permute-start | bytes 442376 | tf_op jit(solution)/shard_map/ppermute | solution.py:291
  52.4 7.2 %collective-permute-start.17 = (f32[36,8,128]{2,1,0:T(8,128)S(1)}, f32[36,8,128]{2,1,0:T(8,128)S(1)}, u32[]{:S(2)}, u32[]{:S(2)}) collective-permute-start(f32[36,8,128]{2,1,0:T(8,128)S(1)} %pad_maximum_fusion.2), channel_id=1, source_target_pairs={{0,128},{1,17},{2,130},{3,19},{4,132},{5,21},{6,134},{7,23},{8,24}... | collective-permute-start | bytes 442376 | tf_op jit(solution)/shard_map/ppermute | solution.py:291
  52.6 7.1 %collective-permute-start.18 = (f32[36,8,128]{2,1,0:T(8,128)S(1)}, f32[36,8,128]{2,1,0:T(8,128)S(1)}, u32[]{:S(2)}, u32[]{:S(2)}) collective-permute-start(f32[36,8,128]{2,1,0:T(8,128)S(1)} %pad_maximum_fusion.3), channel_id=1, source_target_pairs={{0,64},{1,49},{2,66},{3,51},{4,68},{5,53},{6,70},{7,55},{8,56},{9,... | collective-permute-start | bytes 442376 | tf_op jit(solution)/shard_map/ppermute | solution.py:291

commit v5 on v4

--- a/solution.py
+++ b/solution.py
@@ -19,8 +19,10 @@
 AT = {item: n for n, item in enumerate(ITEMS)}
 STEP_Z = (0, 3, 2, 1)
 STEP_Y = (0, 2, 1, 3)
-LATE_Z = (0, 3, 1, 2)
+LATE_Z = (0, 3, 2, 1)
 EARLY_Y = (0, 2, 1, 3)
+LAST_Z = (0, 1, 2, 3)
+LAST_Y = (0, 1, 3, 2)
 VMEM = pl.BlockSpec(memory_space=pltpu.VMEM)
 SMEM = pl.BlockSpec(memory_space=pltpu.SMEM)
 HBM = pl.BlockSpec(memory_space=pltpu.HBM)
@@ -70,10 +72,10 @@
     return core ^ (lax.axis_index("rows") & 1) ^ 1
 
 
-def chunk_at(z, y, role, outer, inner, inner_z=STEP_Z):
+def chunk_at(z, y, role, outer, inner, inner_z=LAST_Z, inner_y=LAST_Y):
     return jnp.where(
         role == 0,
-        (z ^ STEP_Z[outer]) * 4 + (y ^ STEP_Y[inner]),
+        (z ^ STEP_Z[outer]) * 4 + (y ^ inner_y[inner]),
         (z ^ inner_z[inner]) * 4 + (y ^ EARLY_Y[outer]),
     )
 
@@ -119,8 +121,8 @@
     given[6, 4:5, :] = names
 
     def edge(row, upper, lower):
-        keep[row : row + 1, :] = jnp.where(top, upper, lower)
-        give[row : row + 1, :] = jnp.where(top, lower, upper)
+        keep[row // 2, row % 2 : row % 2 + 1, :] = jnp.where(top, upper, lower)
+        give[row // 2, row % 2 : row % 2 + 1, :] = jnp.where(top, lower, upper)
 
     zero = jnp.zeros((1, COLS), F32)
     edge(6, bed[:1], bed[end:])
@@ -164,12 +166,12 @@
 
     in_h = rows_of(0, own[6, 0:2, :], far[6, 0:2, :])
     in_q = rows_of(1, own[6, 2:4, :], far[6, 2:4, :])
-    out_h0 = rows_of(2, next_slab[8:10, :], next_slab[0:2, :])
-    out_h1 = rows_of(3, next_slab[10:12, :], next_slab[2:4, :])
-    out_q = rows_of(4, next_slab[12:14, :], next_slab[4:6, :])
-    my_h = rows_of(5, mine[0:2, :], mine[8:10, :])
-    my_q = rows_of(6, mine[4:6, :], mine[12:14, :])
-    bed_out, fric_out = next_slab[6:7, :], next_slab[7:8, :]
+    out_h0 = rows_of(2, next_slab[4], next_slab[0])
+    out_h1 = rows_of(3, next_slab[5], next_slab[1])
+    out_q = rows_of(4, next_slab[6], next_slab[2])
+    my_h = rows_of(5, mine[0], mine[4])
+    my_q = rows_of(6, mine[2], mine[6])
+    bed_out, fric_out = next_slab[3, 0:1, :], next_slab[3, 1:2, :]
     bed_mine = jnp.where(top, bed[:1], bed[HALF - 1 :])
     eta_mine, eta_out = bed_mine + my_h, bed_out + out_h0
     q1 = flux(
@@ -225,7 +227,7 @@
     names = own[6, 4:5, 0:128] + far[6, 4:5, 0:128]
     for k, out in enumerate((o0, o1, o2, o3)):
         for j in range(4):
-            out[PER * j : PER * j + PER] = packed[chunk_at(z, y, role_of(c), k, j, LATE_Z)]
+            out[PER * j : PER * j + PER] = packed[chunk_at(z, y, role_of(c), k, j, LATE_Z, STEP_Y)]
         out[4 * PER] = jnp.zeros((8, 128), F32)
         out[4 * PER, 0:1, :] = names
 
@@ -235,7 +237,7 @@
     return sub < 4, (sub & 2) == 0
 
 
-def select_kernel(anc, m0, m1, m2, m3, t0, t1, t2, t3, o0, o1, o2, o3, held):
+def select_kernel(codes, m0, m1, m2, m3, t0, t1, t2, t3, o0, o1, o2, o3, held):
     z, y, c = place()
     for n, refs in enumerate(((m0, m1, m2, m3), (t0, t1, t2, t3))):
         for j, ref in enumerate(refs):
@@ -245,15 +247,23 @@
             at = chunk_at(z, y, role_of(c), k, j)
             dest = ((at >> 2) << 3) | ((at & 3) << 1) | c
             for u in range(2):
-                name = anc[2 * dest + u]
-                dz, late_dz = (step_of(steps, (name >> 4) ^ z) for steps in (STEP_Z, LATE_Z))
-                dy, early_dy = (step_of(steps, ((name >> 2) & 3) ^ y) for steps in (STEP_Y, EARLY_Y))
                 for n in range(2):
-                    core = c ^ n
-                    base = jnp.where(role_of(core) == 0, dy * 4 + dz, late_dz * 4 + early_dy) * PER
-                    v = pl.multiple_of((((name >> 1) & 1) ^ core) * 4 + (name & 1) * 2, 2)
+                    code = codes[64 * n + 2 * dest + u]
+                    v = pl.multiple_of(code & 6, 2)
                     row = 4 * n + 2 * u
-                    out[PER * j : PER * j + PER, row : row + 2, :] = held[n, pl.ds(base, PER), pl.ds(v, 2), :]
+                    out[PER * j : PER * j + PER, row : row + 2, :] = held[n, pl.ds(code >> 3, PER), pl.ds(v, 2), :]
+
+
+def codes_of(names):
+    z, y, c = place()
+    dz, late_dz = (step_of(steps, (names >> 4) ^ z) for steps in (STEP_Z, LATE_Z))
+    dy, early_dy = (step_of(steps, ((names >> 2) & 3) ^ y) for steps in (STEP_Y, EARLY_Y))
+    codes = []
+    for n in range(2):
+        core = c ^ n
+        base = jnp.where(role_of(core) == 0, dy * 4 + dz, late_dz * 4 + early_dy) * PER
+        codes.append(base * 8 + (((names >> 1) & 1) ^ core) * 4 + (names & 1) * 2)
+    return jnp.concatenate(codes)
 
 
 def last_kernel(f0, f1, f2, f3, ho, xo, yo, packed):
@@ -295,8 +305,8 @@
     return v if k == 0 else swap(v, (STEP_Z[k] << 3, EARLY_Y[k] << 1))
 
 
-def inner_step(v, k, inner_z=STEP_Z):
-    return v if k == 0 else swap(v, (STEP_Y[k] << 1, inner_z[k] << 3))
+def inner_step(v, k, inner_z=LAST_Z, inner_y=LAST_Y):
+    return v if k == 0 else swap(v, (inner_y[k] << 1, inner_z[k] << 3))
 
 
 def other_core(v):
@@ -314,7 +324,7 @@
 
 def shards(depth, x_flow, y_flow, elevation, roughness, wet, ancestors):
     state = jax.ShapeDtypeStruct((2, ROWS, COLS), F32)
-    strip = jax.ShapeDtypeStruct((HALF, COLS), F32)
+    strip = jax.ShapeDtypeStruct((4, 2, COLS), F32)
     halves = jax.ShapeDtypeStruct((7, HALF, COLS), F32)
     ground = jax.ShapeDtypeStruct((3, HALF, COLS), F32)
     args = (depth, x_flow, y_flow, wet, elevation, roughness, ancestors)
@@ -327,7 +337,7 @@
         + [pltpu.SMEM((2,), jnp.int32), pltpu.SemaphoreType.DMA((7,))],
         compiler_params=params(),
     )(*[pltpu.with_memory_space_constraint(v, pltpu.HBM) for v in args])
-    mine = jnp.concatenate([keep, other_core(give)])
+    mine = jnp.concatenate([keep, other_core(give)[:3]])
     far = other_core(given)
     arrived = next_slab(mine)
     parts = pl.pallas_call(
@@ -341,7 +351,7 @@
     parts = [outer_step(v, k) for k, v in enumerate(parts)]
     names = (parts[0][4 * PER] + parts[1][4 * PER]) + (parts[2][4 * PER] + parts[3][4 * PER])
     parts = [jnp.concatenate([v, names[None]]) for v in regroup(parts, PER)]
-    parts = [inner_step(v, k, LATE_Z) for k, v in enumerate(parts)]
+    parts = [inner_step(v, k, LATE_Z, STEP_Y) for k, v in enumerate(parts)]
     names = sum(v[4 * PER, 0, :64] for v in parts).astype(jnp.int32)
     others = [other_core(v) for v in parts]
     parts = pl.pallas_call(
@@ -351,7 +361,7 @@
         out_specs=[VMEM] * 4,
         scratch_shapes=[pltpu.VMEM((2, 16 * PER, 8, 128), F32)],
         compiler_params=params(),
-    )(names, *parts, *others)
+    )(codes_of(names), *parts, *others)
     parts = [outer_step(v, k) for k, v in enumerate(parts)]
     parts = [inner_step(v, k) for k, v in enumerate(regroup(parts, PER))]
     return tuple(

time: 61.2 us -> 60.7 us (level)
  no operation moved by 1% of the time
where the time goes in v5:
time: 60.7 us; the launch traced here: 59.8 us
  waiting for transfers between devices  27.4 us (45%)
  starting transfers between devices  26.9 us (44%)
  Pallas kernels  4.42 us (7%)
  between operations  0.77 us (1%)
    ppermute x12, waiting for transfers between devices, swap(): return lax.ppermute(v, ('dom', 'rows'), pairs)  23 us
    ppermute x12, starting transfers between devices, swap(): return lax.ppermute(v, ('dom', 'rows'), pairs)  18.5 us
    ppermute x1, starting transfers between devices, next_slab(): return lax.ppermute(v, ('dom', 'rows'), low + [(b, a) for a, b in low])  7.31 us
    ppermute x1, waiting for transfers between devices, next_slab(): return lax.ppermute(v, ('dom', 'rows'), low + [(b, a) for a, b in low])  2.73 us
    pallas_call x1, Pallas kernels, shards(): pl.pallas_call(first_kernel, out_shape=[strip, strip, halves, halves, gro...  1.92 us
    ppermute x6, waiting for transfers between devices, other_core(): return lax.ppermute(v, 'dom', [(i, i ^ 1) for i in range(32)])  1.7 us
  transfers between devices with their start and end apart: 19, of which 13 were waited for; matrix products, arithmetic and copies ran while one was open for 0% of the time, Pallas kernels for 0%

profile of v5, /device:TPU:6, one launch (start us, length us, event | category | flops | bytes accessed | tf_op | source)
XLA Modules:
  0.0 59.8 jit_solution(16872190025828179997)
XLA Ops:
  0.6 1.9 %shard_map.94 = (f32[4,2,1536]{2,1,0:T(2,128)S(1)}, f32[4,2,1536]{2,1,0:T(2,128)S(1)}, f32[7,8,1536]{2,1,0:T(8,128)S(1)}, f32[7,8,1536]{2,1,0:T(8,128)S(1)}, f32[3,8,1536]{2,1,0:T(8,128)S(1)}) custom-call(f32[2,16,1536]{2,1,0:T(8,128)} %depth_in.1, f32[2,16,1536]{2,1,0:T(8,128)} %xf_in.1, f32[2,16,1536]{2,1,0:T(8,128)} %yf_in.1, s32[2,16,1536]{2,1,0:T(8,128)} %wet_in.1, ...), custom_call_target="tpu_custom_call" | custom-call | tf_op jit(solution)/shard_map/pallas_call | solution.py:331
  2.7 0.5 collective-permute-start
  3.2 0.7 %collective-permute-done.1 = f32[4,2,1536]{2,1,0:T(2,128)S(1)} collective-permute-done((f32[4,2,1536]{2,1,0:T(2,128)S(1)}, f32[4,2,1536]{2,1,0:T(2,128)S(1)}, u32[]{:S(2)}, u32[]{:S(2)}) %collective-permute-start.1) | collective-permute-done | bytes 49184 | tf_op jit(solution)/shard_map/ppermute | solution.py:313
  3.9 7.3 %collective-permute-start.2 = (f32[7,2,1536]{2,1,0:T(2,128)S(1)}, f32[7,2,1536]{2,1,0:T(2,128)S(1)}, u32[]{:S(2)}, u32[]{:S(2)}) collective-permute-start(f32[7,2,1536]{2,1,0:T(2,128)S(1)} %pad_maximum_fusion.4.mine), channel_id=1, source_target_pairs={{8,1},{9,2},{10,3},{11,4},{12,5},{13,6},{14,7},{15,0},{24,17},{25,... | collective-permute-start | bytes 258056 | tf_op jit(solution)/shard_map/ppermute | solution.py:318
  11.2 2.7 %collective-permute-done.2.next_slab = f32[7,2,1536]{2,1,0:T(2,128)S(1)} collective-permute-done((f32[7,2,1536]{2,1,0:T(2,128)S(1)}, f32[7,2,1536]{2,1,0:T(2,128)S(1)}, u32[]{:S(2)}, u32[]{:S(2)}) %collective-permute-start.2) | collective-permute-done | bytes 86048 | tf_op jit(solution)/shard_map/ppermute | solution.py:318
  14.0 0.7 %shard_map.95 = (f32[37,8,128]{2,1,0:T(8,128)S(1)}, f32[37,8,128]{2,1,0:T(8,128)S(1)}, f32[37,8,128]{2,1,0:T(8,128)S(1)}, f32[37,8,128]{2,1,0:T(8,128)S(1)}) custom-call(f32[7,8,1536]{2,1,0:T(8,128)S(1)} %get-tuple-element.16.own, f32[7,8,1536]{2,1,0:T(8,128)S(1)} %collective-permute-done.far, f32[3,8,1536]{2,1,0:T(8,128)S(1)} %get-tuple-element.18.terrain, ...), custom_call_target="tpu_custom_call" | custom-call | tf_op jit(solution)/shard_map/pallas_call | solution.py:343
  14.7 4.2 %collective-permute-start.3 = (f32[37,8,128]{2,1,0:T(8,128)S(1)}, f32[37,8,128]{2,1,0:T(8,128)S(1)}, u32[]{:S(2)}, u32[]{:S(2)}) collective-permute-start(f32[37,8,128]{2,1,0:T(8,128)S(1)} %get-tuple-element.22), channel_id=1, source_target_pairs={{0,32},{1,193},{2,34},{3,195},{4,36},{5,197},{6,38},{7,199},{8,200... | collective-permute-start | bytes 454664 | tf_op jit(solution)/shard_map/ppermute | solution.py:301
  18.9 0.7 %collective-permute-start.4 = (f32[37,8,128]{2,1,0:T(8,128)S(1)}, f32[37,8,128]{2,1,0:T(8,128)S(1)}, u32[]{:S(2)}, u32[]{:S(2)}) collective-permute-start(f32[37,8,128]{2,1,0:T(8,128)S(1)} %get-tuple-element.23), channel_id=1, source_target_pairs={{0,16},{1,129},{2,18},{3,131},{4,20},{5,133},{6,22},{7,135},{8,136... | collective-permute-start | bytes 454664 | tf_op jit(solution)/shard_map/ppermute | solution.py:301
  19.5 0.4 collective-permute-start.5
  19.9 2.1 %collective-permute-done.3 = f32[37,8,128]{2,1,0:T(8,128)S(1)} collective-permute-done((f32[37,8,128]{2,1,0:T(8,128)S(1)}, f32[37,8,128]{2,1,0:T(8,128)S(1)}, u32[]{:S(2)}, u32[]{:S(2)}) %collective-permute-start.3) | collective-permute-done | bytes 151584 | tf_op jit(solution)/shard_map/ppermute | solution.py:301
  22.0 2.3 %collective-permute-done.4 = f32[37,8,128]{2,1,0:T(8,128)S(1)} collective-permute-done((f32[37,8,128]{2,1,0:T(8,128)S(1)}, f32[37,8,128]{2,1,0:T(8,128)S(1)}, u32[]{:S(2)}, u32[]{:S(2)}) %collective-permute-start.4) | collective-permute-done | bytes 151584 | tf_op jit(solution)/shard_map/ppermute | solution.py:301
  24.3 1.6 %collective-permute-done.5 = f32[37,8,128]{2,1,0:T(8,128)S(1)} collective-permute-done((f32[37,8,128]{2,1,0:T(8,128)S(1)}, f32[37,8,128]{2,1,0:T(8,128)S(1)}, u32[]{:S(2)}, u32[]{:S(2)}) %collective-permute-start.5) | collective-permute-done | bytes 151584 | tf_op jit(solution)/shard_map/ppermute | solution.py:301
  26.0 3.2 %collective-permute-start.6 = (f32[37,8,128]{2,1,0:T(8,128)S(1)}, f32[37,8,128]{2,1,0:T(8,128)S(1)}, u32[]{:S(2)}, u32[]{:S(2)}) collective-permute-start(f32[37,8,128]{2,1,0:T(8,128)S(1)} %get-tuple-element.65), channel_id=1, source_target_pairs={{0,192},{1,33},{2,194},{3,35},{4,196},{5,37},{6,198},{7,39},{8,40}... | collective-permute-start | bytes 454664 | tf_op jit(solution)/shard_map/ppermute | solution.py:301
  29.2 0.7 %collective-permute-start.7 = (f32[37,8,128]{2,1,0:T(8,128)S(1)}, f32[37,8,128]{2,1,0:T(8,128)S(1)}, u32[]{:S(2)}, u32[]{:S(2)}) collective-permute-start(f32[37,8,128]{2,1,0:T(8,128)S(1)} %get-tuple-element.67), channel_id=1, source_target_pairs={{0,128},{1,17},{2,130},{3,19},{4,132},{5,21},{6,134},{7,23},{8,24}... | collective-permute-start | bytes 454664 | tf_op jit(solution)/shard_map/ppermute | solution.py:301
  29.9 0.5 collective-permute-start.8
  30.5 2.7 %collective-permute-done.6.m1 = f32[37,8,128]{2,1,0:T(8,128)S(1)} collective-permute-done((f32[37,8,128]{2,1,0:T(8,128)S(1)}, f32[37,8,128]{2,1,0:T(8,128)S(1)}, u32[]{:S(2)}, u32[]{:S(2)}) %collective-permute-start.6) | collective-permute-done | bytes 151584 | tf_op jit(solution)/shard_map/ppermute | solution.py:301
  33.2 4.7 %collective-permute-done.7.m2 = f32[37,8,128]{2,1,0:T(8,128)S(1)} collective-permute-done((f32[37,8,128]{2,1,0:T(8,128)S(1)}, f32[37,8,128]{2,1,0:T(8,128)S(1)}, u32[]{:S(2)}, u32[]{:S(2)}) %collective-permute-start.7) | collective-permute-done | bytes 151584 | tf_op jit(solution)/shard_map/ppermute | solution.py:301
  37.9 0.5 collective-permute-start.12
  38.5 0.8 %collective-permute-done.11.t2 = f32[37,8,128]{2,1,0:T(8,128)S(1)} collective-permute-done((f32[37,8,128]{2,1,0:T(8,128)S(1)}, f32[37,8,128]{2,1,0:T(8,128)S(1)}, u32[]{:S(2)}, u32[]{:S(2)}) %collective-permute-start.11) | collective-permute-done | bytes 151584 | tf_op jit(solution)/shard_map/ppermute | solution.py:313
  39.2 0.2 collective-permute-done.12.t3
  39.5 0.9 %shard_map.96 = (f32[36,8,128]{2,1,0:T(8,128)S(1)}, f32[36,8,128]{2,1,0:T(8,128)S(1)}, f32[36,8,128]{2,1,0:T(8,128)S(1)}, f32[36,8,128]{2,1,0:T(8,128)S(1)}) custom-call(s32[128]{0:T(128)S(1)} %pad_add_fusion.codes, f32[37,8,128]{2,1,0:T(8,128)S(1)} %get-tuple-element.29.m0, f32[37,8,128]{2,1,0:T(8,128)S(1)} %collective-permute-done.6.m1, ...), custom_call_target="tpu_custom_call" | custom-call | tf_op jit(solution)/shard_map/pallas_call | solution.py:357
  40.4 1.3 %collective-permute-start.13 = (f32[36,8,128]{2,1,0:T(8,128)S(1)}, f32[36,8,128]{2,1,0:T(8,128)S(1)}, u32[]{:S(2)}, u32[]{:S(2)}) collective-permute-start(f32[36,8,128]{2,1,0:T(8,128)S(1)} %get-tuple-element.26), channel_id=1, source_target_pairs={{0,32},{1,193},{2,34},{3,195},{4,36},{5,197},{6,38},{7,199},{8,200... | collective-permute-start | bytes 442376 | tf_op jit(solution)/shard_map/ppermute | solution.py:301
  41.7 0.7 %collective-permute-start.14 = (f32[36,8,128]{2,1,0:T(8,128)S(1)}, f32[36,8,128]{2,1,0:T(8,128)S(1)}, u32[]{:S(2)}, u32[]{:S(2)}) collective-permute-start(f32[36,8,128]{2,1,0:T(8,128)S(1)} %get-tuple-element.27), channel_id=1, source_target_pairs={{0,16},{1,129},{2,18},{3,131},{4,20},{5,133},{6,22},{7,135},{8,136... | collective-permute-start | bytes 442376 | tf_op jit(solution)/shard_map/ppermute | solution.py:301
  42.4 2.2 %collective-permute-start.15 = (f32[36,8,128]{2,1,0:T(8,128)S(1)}, f32[36,8,128]{2,1,0:T(8,128)S(1)}, u32[]{:S(2)}, u32[]{:S(2)}) collective-permute-start(f32[36,8,128]{2,1,0:T(8,128)S(1)} %get-tuple-element.28), channel_id=1, source_target_pairs={{0,48},{1,65},{2,50},{3,67},{4,52},{5,69},{6,54},{7,71},{8,72},{9,... | collective-permute-start | bytes 442376 | tf_op jit(solution)/shard_map/ppermute | solution.py:301
  44.6 2.5 %collective-permute-done.13 = f32[36,8,128]{2,1,0:T(8,128)S(1)} collective-permute-done((f32[36,8,128]{2,1,0:T(8,128)S(1)}, f32[36,8,128]{2,1,0:T(8,128)S(1)}, u32[]{:S(2)}, u32[]{:S(2)}) %collective-permute-start.13) | collective-permute-done | bytes 147488 | tf_op jit(solution)/shard_map/ppermute | solution.py:301
  47.1 1.6 %collective-permute-done.15 = f32[36,8,128]{2,1,0:T(8,128)S(1)} collective-permute-done((f32[36,8,128]{2,1,0:T(8,128)S(1)}, f32[36,8,128]{2,1,0:T(8,128)S(1)}, u32[]{:S(2)}, u32[]{:S(2)}) %collective-permute-start.15) | collective-permute-done | bytes 147488 | tf_op jit(solution)/shard_map/ppermute | solution.py:301
  48.8 3.0 %collective-permute-start.18 = (f32[36,8,128]{2,1,0:T(8,128)S(1)}, f32[36,8,128]{2,1,0:T(8,128)S(1)}, u32[]{:S(2)}, u32[]{:S(2)}) collective-permute-start(f32[36,8,128]{2,1,0:T(8,128)S(1)} %pad_maximum_fusion.3), channel_id=1, source_target_pairs={{0,192},{1,33},{2,194},{3,35},{4,196},{5,37},{6,198},{7,39},{8,40}... | collective-permute-start | bytes 442376 | tf_op jit(solution)/shard_map/ppermute | solution.py:301
  51.8 0.1 collective-permute-start.17
  51.9 1.5 %collective-permute-start.16 = (f32[36,8,128]{2,1,0:T(8,128)S(1)}, f32[36,8,128]{2,1,0:T(8,128)S(1)}, u32[]{:S(2)}, u32[]{:S(2)}) collective-permute-start(f32[36,8,128]{2,1,0:T(8,128)S(1)} %pad_maximum_fusion.1), channel_id=1, source_target_pairs={{0,64},{1,17},{2,66},{3,19},{4,68},{5,21},{6,70},{7,23},{8,24},{9,... | collective-permute-start | bytes 442376 | tf_op jit(solution)/shard_map/ppermute | solution.py:301
  53.4 2.4 %collective-permute-done.18.f3 = f32[36,8,128]{2,1,0:T(8,128)S(1)} collective-permute-done((f32[36,8,128]{2,1,0:T(8,128)S(1)}, f32[36,8,128]{2,1,0:T(8,128)S(1)}, u32[]{:S(2)}, u32[]{:S(2)}) %collective-permute-start.18) | collective-permute-done | bytes 147488 | tf_op jit(solution)/shard_map/ppermute | solution.py:301
  55.8 3.1 %collective-permute-done.17.f2 = f32[36,8,128]{2,1,0:T(8,128)S(1)} collective-permute-done((f32[36,8,128]{2,1,0:T(8,128)S(1)}, f32[36,8,128]{2,1,0:T(8,128)S(1)}, u32[]{:S(2)}, u32[]{:S(2)}) %collective-permute-start.17) | collective-permute-done | bytes 147488 | tf_op jit(solution)/shard_map/ppermute | solution.py:301
  59.0 0.9 %shard_map.97 = (f32[2,16,1536]{2,1,0:T(8,128)}, f32[2,16,1536]{2,1,0:T(8,128)}, f32[2,16,1536]{2,1,0:T(8,128)}) custom-call(f32[36,8,128]{2,1,0:T(8,128)S(1)} %pad_maximum_fusion.f0, f32[36,8,128]{2,1,0:T(8,128)S(1)} %collective-permute-done.16.f1, f32[36,8,128]{2,1,0:T(8,128)S(1)} %collective-permute-done.17.f2, f32[36,8,128]{2,1,0:T(8,128)S(1)} %collective-permute-done.18.f3), custom_call_target="tpu_custom_call" | custom-call | tf_op jit(solution)/shard_map/pallas_call | solution.py:368
  (28 shorter events, 0.4 us)
Async XLA Ops:
  2.6 1.3 %collective-permute-start.1 = (f32[4,2,1536]{2,1,0:T(2,128)S(1)}, f32[4,2,1536]{2,1,0:T(2,128)S(1)}, u32[]{:S(2)}, u32[]{:S(2)}) collective-permute-start(f32[4,2,1536]{2,1,0:T(2,128)S(1)} %get-tuple-element.20), channel_id=1, source_target_pairs={{0,8},{8,0},{16,24},{24,16},{32,40},{40,32},{48,56},{56,48},{64,72... | collective-permute-start | bytes 147464 | tf_op jit(solution)/shard_map/ppermute | solution.py:313
  2.7 11.3 %collective-permute-start = (f32[7,8,1536]{2,1,0:T(8,128)S(1)}, f32[7,8,1536]{2,1,0:T(8,128)S(1)}, u32[]{:S(2)}, u32[]{:S(2)}) collective-permute-start(f32[7,8,1536]{2,1,0:T(8,128)S(1)} %get-tuple-element.17), channel_id=1, source_target_pairs={{0,8},{8,0},{16,24},{24,16},{32,40},{40,32},{48,56},{56,48},{64,72... | collective-permute-start | bytes 1032200 | tf_op jit(solution)/shard_map/ppermute | solution.py:313
  3.9 10.0 %collective-permute-start.2 = (f32[7,2,1536]{2,1,0:T(2,128)S(1)}, f32[7,2,1536]{2,1,0:T(2,128)S(1)}, u32[]{:S(2)}, u32[]{:S(2)}) collective-permute-start(f32[7,2,1536]{2,1,0:T(2,128)S(1)} %pad_maximum_fusion.4.mine), channel_id=1, source_target_pairs={{8,1},{9,2},{10,3},{11,4},{12,5},{13,6},{14,7},{15,0},{24,17},{25,... | collective-permute-start | bytes 258056 | tf_op jit(solution)/shard_map/ppermute | solution.py:318
  14.7 7.3 %collective-permute-start.3 = (f32[37,8,128]{2,1,0:T(8,128)S(1)}, f32[37,8,128]{2,1,0:T(8,128)S(1)}, u32[]{:S(2)}, u32[]{:S(2)}) collective-permute-start(f32[37,8,128]{2,1,0:T(8,128)S(1)} %get-tuple-element.22), channel_id=1, source_target_pairs={{0,32},{1,193},{2,34},{3,195},{4,36},{5,197},{6,38},{7,199},{8,200... | collective-permute-start | bytes 454664 | tf_op jit(solution)/shard_map/ppermute | solution.py:301
  18.9 5.5 %collective-permute-start.4 = (f32[37,8,128]{2,1,0:T(8,128)S(1)}, f32[37,8,128]{2,1,0:T(8,128)S(1)}, u32[]{:S(2)}, u32[]{:S(2)}) collective-permute-start(f32[37,8,128]{2,1,0:T(8,128)S(1)} %get-tuple-element.23), channel_id=1, source_target_pairs={{0,16},{1,129},{2,18},{3,131},{4,20},{5,133},{6,22},{7,135},{8,136... | collective-permute-start | bytes 454664 | tf_op jit(solution)/shard_map/ppermute | solution.py:301
  19.5 6.4 %collective-permute-start.5 = (f32[37,8,128]{2,1,0:T(8,128)S(1)}, f32[37,8,128]{2,1,0:T(8,128)S(1)}, u32[]{:S(2)}, u32[]{:S(2)}) collective-permute-start(f32[37,8,128]{2,1,0:T(8,128)S(1)} %get-tuple-element.24), channel_id=1, source_target_pairs={{0,48},{1,65},{2,50},{3,67},{4,52},{5,69},{6,54},{7,71},{8,72},{9,... | collective-permute-start | bytes 454664 | tf_op jit(solution)/shard_map/ppermute | solution.py:301
  26.0 7.2 %collective-permute-start.6 = (f32[37,8,128]{2,1,0:T(8,128)S(1)}, f32[37,8,128]{2,1,0:T(8,128)S(1)}, u32[]{:S(2)}, u32[]{:S(2)}) collective-permute-start(f32[37,8,128]{2,1,0:T(8,128)S(1)} %get-tuple-element.65), channel_id=1, source_target_pairs={{0,192},{1,33},{2,194},{3,35},{4,196},{5,37},{6,198},{7,39},{8,40}... | collective-permute-start | bytes 454664 | tf_op jit(solution)/shard_map/ppermute | solution.py:301
  29.2 8.7 %collective-permute-start.7 = (f32[37,8,128]{2,1,0:T(8,128)S(1)}, f32[37,8,128]{2,1,0:T(8,128)S(1)}, u32[]{:S(2)}, u32[]{:S(2)}) collective-permute-start(f32[37,8,128]{2,1,0:T(8,128)S(1)} %get-tuple-element.67), channel_id=1, source_target_pairs={{0,128},{1,17},{2,130},{3,19},{4,132},{5,21},{6,134},{7,23},{8,24}... | collective-permute-start | bytes 454664 | tf_op jit(solution)/shard_map/ppermute | solution.py:301
  29.9 7.9 %collective-permute-start.8 = (f32[37,8,128]{2,1,0:T(8,128)S(1)}, f32[37,8,128]{2,1,0:T(8,128)S(1)}, u32[]{:S(2)}, u32[]{:S(2)}) collective-permute-start(f32[37,8,128]{2,1,0:T(8,128)S(1)} %get-tuple-element.66), channel_id=1, source_target_pairs={{0,64},{1,49},{2,66},{3,51},{4,68},{5,53},{6,70},{7,55},{8,56},{9,... | collective-permute-start | bytes 454664 | tf_op jit(solution)/shard_map/ppermute | solution.py:301
  30.4 8.0 %collective-permute-start.9 = (f32[37,8,128]{2,1,0:T(8,128)S(1)}, f32[37,8,128]{2,1,0:T(8,128)S(1)}, u32[]{:S(2)}, u32[]{:S(2)}) collective-permute-start(f32[37,8,128]{2,1,0:T(8,128)S(1)} %get-tuple-element.29.m0), channel_id=1, source_target_pairs={{0,8},{8,0},{16,24},{24,16},{32,40},{40,32},{48,56},{56,48},{64,72... | collective-permute-start | bytes 454664 | tf_op jit(solution)/shard_map/ppermute | solution.py:313
  33.1 5.3 %collective-permute-start.10 = (f32[37,8,128]{2,1,0:T(8,128)S(1)}, f32[37,8,128]{2,1,0:T(8,128)S(1)}, u32[]{:S(2)}, u32[]{:S(2)}) collective-permute-start(f32[37,8,128]{2,1,0:T(8,128)S(1)} %collective-permute-done.6.m1), channel_id=1, source_target_pairs={{0,8},{8,0},{16,24},{24,16},{32,40},{40,32},{48,56},{56,48},{64,72... | collective-permute-start | bytes 454664 | tf_op jit(solution)/shard_map/ppermute | solution.py:313
  37.9 1.4 %collective-permute-start.11 = (f32[37,8,128]{2,1,0:T(8,128)S(1)}, f32[37,8,128]{2,1,0:T(8,128)S(1)}, u32[]{:S(2)}, u32[]{:S(2)}) collective-permute-start(f32[37,8,128]{2,1,0:T(8,128)S(1)} %collective-permute-done.7.m2), channel_id=1, source_target_pairs={{0,8},{8,0},{16,24},{24,16},{32,40},{40,32},{48,56},{56,48},{64,72... | collective-permute-start | bytes 454664 | tf_op jit(solution)/shard_map/ppermute | solution.py:313
  37.9 1.6 %collective-permute-start.12 = (f32[37,8,128]{2,1,0:T(8,128)S(1)}, f32[37,8,128]{2,1,0:T(8,128)S(1)}, u32[]{:S(2)}, u32[]{:S(2)}) collective-permute-start(f32[37,8,128]{2,1,0:T(8,128)S(1)} %collective-permute-done.8.m3), channel_id=1, source_target_pairs={{0,8},{8,0},{16,24},{24,16},{32,40},{40,32},{48,56},{56,48},{64,72... | collective-permute-start | bytes 454664 | tf_op jit(solution)/shard_map/ppermute | solution.py:313
  40.4 6.7 %collective-permute-start.13 = (f32[36,8,128]{2,1,0:T(8,128)S(1)}, f32[36,8,128]{2,1,0:T(8,128)S(1)}, u32[]{:S(2)}, u32[]{:S(2)}) collective-permute-start(f32[36,8,128]{2,1,0:T(8,128)S(1)} %get-tuple-element.26), channel_id=1, source_target_pairs={{0,32},{1,193},{2,34},{3,195},{4,36},{5,197},{6,38},{7,199},{8,200... | collective-permute-start | bytes 442376 | tf_op jit(solution)/shard_map/ppermute | solution.py:301
  41.7 5.4 %collective-permute-start.14 = (f32[36,8,128]{2,1,0:T(8,128)S(1)}, f32[36,8,128]{2,1,0:T(8,128)S(1)}, u32[]{:S(2)}, u32[]{:S(2)}) collective-permute-start(f32[36,8,128]{2,1,0:T(8,128)S(1)} %get-tuple-element.27), channel_id=1, source_target_pairs={{0,16},{1,129},{2,18},{3,131},{4,20},{5,133},{6,22},{7,135},{8,136... | collective-permute-start | bytes 442376 | tf_op jit(solution)/shard_map/ppermute | solution.py:301
  42.4 6.4 %collective-permute-start.15 = (f32[36,8,128]{2,1,0:T(8,128)S(1)}, f32[36,8,128]{2,1,0:T(8,128)S(1)}, u32[]{:S(2)}, u32[]{:S(2)}) collective-permute-start(f32[36,8,128]{2,1,0:T(8,128)S(1)} %get-tuple-element.28), channel_id=1, source_target_pairs={{0,48},{1,65},{2,50},{3,67},{4,52},{5,69},{6,54},{7,71},{8,72},{9,... | collective-permute-start | bytes 442376 | tf_op jit(solution)/shard_map/ppermute | solution.py:301
  48.8 7.1 %collective-permute-start.18 = (f32[36,8,128]{2,1,0:T(8,128)S(1)}, f32[36,8,128]{2,1,0:T(8,128)S(1)}, u32[]{:S(2)}, u32[]{:S(2)}) collective-permute-start(f32[36,8,128]{2,1,0:T(8,128)S(1)} %pad_maximum_fusion.3), channel_id=1, source_target_pairs={{0,192},{1,33},{2,194},{3,35},{4,196},{5,37},{6,198},{7,39},{8,40}... | collective-permute-start | bytes 442376 | tf_op jit(solution)/shard_map/ppermute | solution.py:301
  51.8 7.2 %collective-permute-start.17 = (f32[36,8,128]{2,1,0:T(8,128)S(1)}, f32[36,8,128]{2,1,0:T(8,128)S(1)}, u32[]{:S(2)}, u32[]{:S(2)}) collective-permute-start(f32[36,8,128]{2,1,0:T(8,128)S(1)} %pad_maximum_fusion.2), channel_id=1, source_target_pairs={{0,128},{1,49},{2,130},{3,51},{4,132},{5,53},{6,134},{7,55},{8,56}... | collective-permute-start | bytes 442376 | tf_op jit(solution)/shard_map/ppermute | solution.py:301
  51.9 7.1 %collective-permute-start.16 = (f32[36,8,128]{2,1,0:T(8,128)S(1)}, f32[36,8,128]{2,1,0:T(8,128)S(1)}, u32[]{:S(2)}, u32[]{:S(2)}) collective-permute-start(f32[36,8,128]{2,1,0:T(8,128)S(1)} %pad_maximum_fusion.1), channel_id=1, source_target_pairs={{0,64},{1,17},{2,66},{3,19},{4,68},{5,21},{6,70},{7,23},{8,24},{9,... | collective-permute-start | bytes 442376 | tf_op jit(solution)/shard_map/ppermute | solution.py:301

commit v6 on v5

--- a/solution.py
+++ b/solution.py
@@ -91,13 +91,14 @@
     depth_in, xf_in, yf_in, wet_in, elev_in, rough_in, anc_in, keep, give, kept, given, terrain,
     depth, xf, yf, wet, elev, rough, anc, sems,
 ):
-    pairs = zip(
-        (elev_in, rough_in, depth_in, wet_in, xf_in, yf_in, anc_in), (elev, rough, depth, wet, xf, yf, anc)
-    )
+    pairs = [(elev_in, elev), (rough_in, rough), (anc_in, anc)]
+    for p in range(2):
+        fields = ((depth_in, depth), (wet_in, wet), (xf_in, xf), (yf_in, yf))
+        pairs += [(src.at[p], dst.at[p]) for src, dst in fields]
     copies = [pltpu.make_async_copy(src, dst, sems.at[n]) for n, (src, dst) in enumerate(pairs)]
     for copy in copies:
         copy.start()
-    for copy in copies:
+    for copy in copies[:3]:
         copy.wait()
     _, _, c = place()
     top = c == 0
@@ -128,6 +129,8 @@
     edge(6, bed[:1], bed[end:])
     edge(7, fric[:1], fric[end:])
     for p in range(2):
+        for copy in copies[3 + 4 * p : 7 + 4 * p]:
+            copy.wait()
         h0 = depth[p] * wet[p].astype(F32)
         qx, qy = xf[p], yf[p]
         edge(p, h0[:1], h0[end:])
@@ -266,13 +269,15 @@
     return jnp.concatenate(codes)
 
 
-def last_kernel(f0, f1, f2, f3, ho, xo, yo, packed):
+def last_kernel(f0, f1, f2, f3, ho, xo, yo, packed, done, sems):
     z, y, c = place()
     low, even = masks()
     for j, ref in enumerate((f0, f1, f2, f3)):
         for k in range(4):
             packed[pl.ds(chunk_at(z, y, role_of(c), k, j) * PER, PER)] = ref[PER * k : PER * k + PER]
-    for f, out in enumerate((ho, xo, yo)):
+    copies = []
+    for f, target in enumerate((ho, xo, yo)):
+        out = done.at[f]
         for t in range(NT):
             cols = slice(128 * t, 128 * t + 128)
             pair = [packed[AT[(d, f, t)]] for d in range(4)]
@@ -286,6 +291,10 @@
                     b1 = jnp.where(low, pltpu.roll(pair[1], 4, 0), pair[3])
                 out[0, rows, cols] = jnp.where(even, b0, pltpu.roll(b1, 2, 0))
                 out[1, rows, cols] = jnp.where(even, pltpu.roll(b0, 6, 0), b1)
+        copies.append(pltpu.make_async_copy(out, target, sems.at[f]))
+        copies[f].start()
+    for copy in copies:
+        copy.wait()
 
 
 def tiles(n):
@@ -334,7 +343,7 @@
         in_specs=[HBM] * 7,
         out_specs=[VMEM] * 5,
         scratch_shapes=[pltpu.VMEM(v.shape, v.dtype) for v in args[:6]]
-        + [pltpu.SMEM((2,), jnp.int32), pltpu.SemaphoreType.DMA((7,))],
+        + [pltpu.SMEM((2,), jnp.int32), pltpu.SemaphoreType.DMA((11,))],
         compiler_params=params(),
     )(*[pltpu.with_memory_space_constraint(v, pltpu.HBM) for v in args])
     mine = jnp.concatenate([keep, other_core(give)[:3]])
@@ -369,8 +378,12 @@
             last_kernel,
             out_shape=[state] * 3,
             in_specs=[VMEM] * 4,
-            out_specs=[VMEM] * 3,
-            scratch_shapes=[pltpu.VMEM((16 * PER, 8, 128), F32)],
+            out_specs=[HBM] * 3,
+            scratch_shapes=[
+                pltpu.VMEM((16 * PER, 8, 128), F32),
+                pltpu.VMEM((3, 2, ROWS, COLS), F32),
+                pltpu.SemaphoreType.DMA((3,)),
+            ],
             compiler_params=params(),
         )(*parts)
     )

time: 60.7 us -> 60.6 us (level)
  no operation moved by 1% of the time
where the time goes in v6:
time: 60.6 us; the launch traced here: 59.7 us
  waiting for transfers between devices  27.4 us (45%)
  starting transfers between devices  26.9 us (44%)
  Pallas kernels  4.31 us (7%)
  between operations  0.77 us (1%)
    ppermute x12, waiting for transfers between devices, swap(): return lax.ppermute(v, ('dom', 'rows'), pairs)  23 us
    ppermute x12, starting transfers between devices, swap(): return lax.ppermute(v, ('dom', 'rows'), pairs)  18.5 us
    ppermute x1, starting transfers between devices, next_slab(): return lax.ppermute(v, ('dom', 'rows'), low + [(b, a) for a, b in low])  7.31 us
    ppermute x1, waiting for transfers between devices, next_slab(): return lax.ppermute(v, ('dom', 'rows'), low + [(b, a) for a, b in low])  2.73 us
    pallas_call x1, Pallas kernels, shards(): pl.pallas_call(first_kernel, out_shape=[strip, strip, halves, halves, gro...  1.79 us
    ppermute x6, waiting for transfers between devices, other_core(): return lax.ppermute(v, 'dom', [(i, i ^ 1) for i in range(32)])  1.7 us
  transfers between devices with their start and end apart: 19, of which 13 were waited for; matrix products, arithmetic and copies ran while one was open for 0% of the time, Pallas kernels for 0%

profile of v6, /device:TPU:6, one launch (start us, length us, event | category | flops | bytes accessed | tf_op | source)
XLA Modules:
  0.0 59.7 jit_solution(11230335098953130797)
XLA Ops:
  0.6 1.8 %shard_map.94 = (f32[4,2,1536]{2,1,0:T(2,128)S(1)}, f32[4,2,1536]{2,1,0:T(2,128)S(1)}, f32[7,8,1536]{2,1,0:T(8,128)S(1)}, f32[7,8,1536]{2,1,0:T(8,128)S(1)}, f32[3,8,1536]{2,1,0:T(8,128)S(1)}) custom-call(f32[2,16,1536]{2,1,0:T(8,128)} %depth_in.1, f32[2,16,1536]{2,1,0:T(8,128)} %xf_in.1, f32[2,16,1536]{2,1,0:T(8,128)} %yf_in.1, s32[2,16,1536]{2,1,0:T(8,128)} %wet_in.1, ...), custom_call_target="tpu_custom_call" | custom-call | tf_op jit(solution)/shard_map/pallas_call | solution.py:340
  2.5 0.5 collective-permute-start
  3.0 0.7 %collective-permute-done.1 = f32[4,2,1536]{2,1,0:T(2,128)S(1)} collective-permute-done((f32[4,2,1536]{2,1,0:T(2,128)S(1)}, f32[4,2,1536]{2,1,0:T(2,128)S(1)}, u32[]{:S(2)}, u32[]{:S(2)}) %collective-permute-start.1) | collective-permute-done | bytes 49184 | tf_op jit(solution)/shard_map/ppermute | solution.py:322
  3.8 7.3 %collective-permute-start.2 = (f32[7,2,1536]{2,1,0:T(2,128)S(1)}, f32[7,2,1536]{2,1,0:T(2,128)S(1)}, u32[]{:S(2)}, u32[]{:S(2)}) collective-permute-start(f32[7,2,1536]{2,1,0:T(2,128)S(1)} %pad_maximum_fusion.4.mine), channel_id=1, source_target_pairs={{8,1},{9,2},{10,3},{11,4},{12,5},{13,6},{14,7},{15,0},{24,17},{25,... | collective-permute-start | bytes 258056 | tf_op jit(solution)/shard_map/ppermute | solution.py:327
  11.1 2.7 %collective-permute-done.2.next_slab = f32[7,2,1536]{2,1,0:T(2,128)S(1)} collective-permute-done((f32[7,2,1536]{2,1,0:T(2,128)S(1)}, f32[7,2,1536]{2,1,0:T(2,128)S(1)}, u32[]{:S(2)}, u32[]{:S(2)}) %collective-permute-start.2) | collective-permute-done | bytes 86048 | tf_op jit(solution)/shard_map/ppermute | solution.py:327
  13.8 0.7 %shard_map.95 = (f32[37,8,128]{2,1,0:T(8,128)S(1)}, f32[37,8,128]{2,1,0:T(8,128)S(1)}, f32[37,8,128]{2,1,0:T(8,128)S(1)}, f32[37,8,128]{2,1,0:T(8,128)S(1)}) custom-call(f32[7,8,1536]{2,1,0:T(8,128)S(1)} %get-tuple-element.16.own, f32[7,8,1536]{2,1,0:T(8,128)S(1)} %collective-permute-done.far, f32[3,8,1536]{2,1,0:T(8,128)S(1)} %get-tuple-element.18.terrain, ...), custom_call_target="tpu_custom_call" | custom-call | tf_op jit(solution)/shard_map/pallas_call | solution.py:352
  14.6 4.2 %collective-permute-start.3 = (f32[37,8,128]{2,1,0:T(8,128)S(1)}, f32[37,8,128]{2,1,0:T(8,128)S(1)}, u32[]{:S(2)}, u32[]{:S(2)}) collective-permute-start(f32[37,8,128]{2,1,0:T(8,128)S(1)} %get-tuple-element.22), channel_id=1, source_target_pairs={{0,32},{1,193},{2,34},{3,195},{4,36},{5,197},{6,38},{7,199},{8,200... | collective-permute-start | bytes 454664 | tf_op jit(solution)/shard_map/ppermute | solution.py:310
  18.7 0.7 %collective-permute-start.4 = (f32[37,8,128]{2,1,0:T(8,128)S(1)}, f32[37,8,128]{2,1,0:T(8,128)S(1)}, u32[]{:S(2)}, u32[]{:S(2)}) collective-permute-start(f32[37,8,128]{2,1,0:T(8,128)S(1)} %get-tuple-element.23), channel_id=1, source_target_pairs={{0,16},{1,129},{2,18},{3,131},{4,20},{5,133},{6,22},{7,135},{8,136... | collective-permute-start | bytes 454664 | tf_op jit(solution)/shard_map/ppermute | solution.py:310
  19.4 0.4 collective-permute-start.5
  19.8 2.1 %collective-permute-done.3 = f32[37,8,128]{2,1,0:T(8,128)S(1)} collective-permute-done((f32[37,8,128]{2,1,0:T(8,128)S(1)}, f32[37,8,128]{2,1,0:T(8,128)S(1)}, u32[]{:S(2)}, u32[]{:S(2)}) %collective-permute-start.3) | collective-permute-done | bytes 151584 | tf_op jit(solution)/shard_map/ppermute | solution.py:310
  21.9 2.3 %collective-permute-done.4 = f32[37,8,128]{2,1,0:T(8,128)S(1)} collective-permute-done((f32[37,8,128]{2,1,0:T(8,128)S(1)}, f32[37,8,128]{2,1,0:T(8,128)S(1)}, u32[]{:S(2)}, u32[]{:S(2)}) %collective-permute-start.4) | collective-permute-done | bytes 151584 | tf_op jit(solution)/shard_map/ppermute | solution.py:310
  24.2 1.6 %collective-permute-done.5 = f32[37,8,128]{2,1,0:T(8,128)S(1)} collective-permute-done((f32[37,8,128]{2,1,0:T(8,128)S(1)}, f32[37,8,128]{2,1,0:T(8,128)S(1)}, u32[]{:S(2)}, u32[]{:S(2)}) %collective-permute-start.5) | collective-permute-done | bytes 151584 | tf_op jit(solution)/shard_map/ppermute | solution.py:310
  25.8 3.2 %collective-permute-start.6 = (f32[37,8,128]{2,1,0:T(8,128)S(1)}, f32[37,8,128]{2,1,0:T(8,128)S(1)}, u32[]{:S(2)}, u32[]{:S(2)}) collective-permute-start(f32[37,8,128]{2,1,0:T(8,128)S(1)} %get-tuple-element.65), channel_id=1, source_target_pairs={{0,192},{1,33},{2,194},{3,35},{4,196},{5,37},{6,198},{7,39},{8,40}... | collective-permute-start | bytes 454664 | tf_op jit(solution)/shard_map/ppermute | solution.py:310
  29.1 0.7 %collective-permute-start.7 = (f32[37,8,128]{2,1,0:T(8,128)S(1)}, f32[37,8,128]{2,1,0:T(8,128)S(1)}, u32[]{:S(2)}, u32[]{:S(2)}) collective-permute-start(f32[37,8,128]{2,1,0:T(8,128)S(1)} %get-tuple-element.67), channel_id=1, source_target_pairs={{0,128},{1,17},{2,130},{3,19},{4,132},{5,21},{6,134},{7,23},{8,24}... | collective-permute-start | bytes 454664 | tf_op jit(solution)/shard_map/ppermute | solution.py:310
  29.8 0.5 collective-permute-start.8
  30.3 2.7 %collective-permute-done.6.m1 = f32[37,8,128]{2,1,0:T(8,128)S(1)} collective-permute-done((f32[37,8,128]{2,1,0:T(8,128)S(1)}, f32[37,8,128]{2,1,0:T(8,128)S(1)}, u32[]{:S(2)}, u32[]{:S(2)}) %collective-permute-start.6) | collective-permute-done | bytes 151584 | tf_op jit(solution)/shard_map/ppermute | solution.py:310
  33.0 4.7 %collective-permute-done.7.m2 = f32[37,8,128]{2,1,0:T(8,128)S(1)} collective-permute-done((f32[37,8,128]{2,1,0:T(8,128)S(1)}, f32[37,8,128]{2,1,0:T(8,128)S(1)}, u32[]{:S(2)}, u32[]{:S(2)}) %collective-permute-start.7) | collective-permute-done | bytes 151584 | tf_op jit(solution)/shard_map/ppermute | solution.py:310
  37.7 0.5 collective-permute-start.12
  38.4 0.8 %collective-permute-done.11.t2 = f32[37,8,128]{2,1,0:T(8,128)S(1)} collective-permute-done((f32[37,8,128]{2,1,0:T(8,128)S(1)}, f32[37,8,128]{2,1,0:T(8,128)S(1)}, u32[]{:S(2)}, u32[]{:S(2)}) %collective-permute-start.11) | collective-permute-done | bytes 151584 | tf_op jit(solution)/shard_map/ppermute | solution.py:322
  39.1 0.2 collective-permute-done.12.t3
  39.3 0.9 %shard_map.96 = (f32[36,8,128]{2,1,0:T(8,128)S(1)}, f32[36,8,128]{2,1,0:T(8,128)S(1)}, f32[36,8,128]{2,1,0:T(8,128)S(1)}, f32[36,8,128]{2,1,0:T(8,128)S(1)}) custom-call(s32[128]{0:T(128)S(1)} %pad_add_fusion.codes, f32[37,8,128]{2,1,0:T(8,128)S(1)} %get-tuple-element.29.m0, f32[37,8,128]{2,1,0:T(8,128)S(1)} %collective-permute-done.6.m1, ...), custom_call_target="tpu_custom_call" | custom-call | tf_op jit(solution)/shard_map/pallas_call | solution.py:366
  40.2 1.3 %collective-permute-start.13 = (f32[36,8,128]{2,1,0:T(8,128)S(1)}, f32[36,8,128]{2,1,0:T(8,128)S(1)}, u32[]{:S(2)}, u32[]{:S(2)}) collective-permute-start(f32[36,8,128]{2,1,0:T(8,128)S(1)} %get-tuple-element.26), channel_id=1, source_target_pairs={{0,32},{1,193},{2,34},{3,195},{4,36},{5,197},{6,38},{7,199},{8,200... | collective-permute-start | bytes 442376 | tf_op jit(solution)/shard_map/ppermute | solution.py:310
  41.6 0.7 %collective-permute-start.14 = (f32[36,8,128]{2,1,0:T(8,128)S(1)}, f32[36,8,128]{2,1,0:T(8,128)S(1)}, u32[]{:S(2)}, u32[]{:S(2)}) collective-permute-start(f32[36,8,128]{2,1,0:T(8,128)S(1)} %get-tuple-element.27), channel_id=1, source_target_pairs={{0,16},{1,129},{2,18},{3,131},{4,20},{5,133},{6,22},{7,135},{8,136... | collective-permute-start | bytes 442376 | tf_op jit(solution)/shard_map/ppermute | solution.py:310
  42.2 2.2 %collective-permute-start.15 = (f32[36,8,128]{2,1,0:T(8,128)S(1)}, f32[36,8,128]{2,1,0:T(8,128)S(1)}, u32[]{:S(2)}, u32[]{:S(2)}) collective-permute-start(f32[36,8,128]{2,1,0:T(8,128)S(1)} %get-tuple-element.28), channel_id=1, source_target_pairs={{0,48},{1,65},{2,50},{3,67},{4,52},{5,69},{6,54},{7,71},{8,72},{9,... | collective-permute-start | bytes 442376 | tf_op jit(solution)/shard_map/ppermute | solution.py:310
  44.4 2.5 %collective-permute-done.13 = f32[36,8,128]{2,1,0:T(8,128)S(1)} collective-permute-done((f32[36,8,128]{2,1,0:T(8,128)S(1)}, f32[36,8,128]{2,1,0:T(8,128)S(1)}, u32[]{:S(2)}, u32[]{:S(2)}) %collective-permute-start.13) | collective-permute-done | bytes 147488 | tf_op jit(solution)/shard_map/ppermute | solution.py:310
  47.0 1.6 %collective-permute-done.15 = f32[36,8,128]{2,1,0:T(8,128)S(1)} collective-permute-done((f32[36,8,128]{2,1,0:T(8,128)S(1)}, f32[36,8,128]{2,1,0:T(8,128)S(1)}, u32[]{:S(2)}, u32[]{:S(2)}) %collective-permute-start.15) | collective-permute-done | bytes 147488 | tf_op jit(solution)/shard_map/ppermute | solution.py:310
  48.6 3.0 %collective-permute-start.18 = (f32[36,8,128]{2,1,0:T(8,128)S(1)}, f32[36,8,128]{2,1,0:T(8,128)S(1)}, u32[]{:S(2)}, u32[]{:S(2)}) collective-permute-start(f32[36,8,128]{2,1,0:T(8,128)S(1)} %pad_maximum_fusion.3), channel_id=1, source_target_pairs={{0,192},{1,33},{2,194},{3,35},{4,196},{5,37},{6,198},{7,39},{8,40}... | collective-permute-start | bytes 442376 | tf_op jit(solution)/shard_map/ppermute | solution.py:310
  51.6 0.1 collective-permute-start.17
  51.8 1.5 %collective-permute-start.16 = (f32[36,8,128]{2,1,0:T(8,128)S(1)}, f32[36,8,128]{2,1,0:T(8,128)S(1)}, u32[]{:S(2)}, u32[]{:S(2)}) collective-permute-start(f32[36,8,128]{2,1,0:T(8,128)S(1)} %pad_maximum_fusion.1), channel_id=1, source_target_pairs={{0,64},{1,17},{2,66},{3,19},{4,68},{5,21},{6,70},{7,23},{8,24},{9,... | collective-permute-start | bytes 442376 | tf_op jit(solution)/shard_map/ppermute | solution.py:310
  53.3 2.4 %collective-permute-done.18.f3 = f32[36,8,128]{2,1,0:T(8,128)S(1)} collective-permute-done((f32[36,8,128]{2,1,0:T(8,128)S(1)}, f32[36,8,128]{2,1,0:T(8,128)S(1)}, u32[]{:S(2)}, u32[]{:S(2)}) %collective-permute-start.18) | collective-permute-done | bytes 147488 | tf_op jit(solution)/shard_map/ppermute | solution.py:310
  55.7 3.1 %collective-permute-done.17.f2 = f32[36,8,128]{2,1,0:T(8,128)S(1)} collective-permute-done((f32[36,8,128]{2,1,0:T(8,128)S(1)}, f32[36,8,128]{2,1,0:T(8,128)S(1)}, u32[]{:S(2)}, u32[]{:S(2)}) %collective-permute-start.17) | collective-permute-done | bytes 147488 | tf_op jit(solution)/shard_map/ppermute | solution.py:310
  58.8 0.9 %shard_map.97 = (f32[2,16,1536]{2,1,0:T(8,128)}, f32[2,16,1536]{2,1,0:T(8,128)}, f32[2,16,1536]{2,1,0:T(8,128)}) custom-call(f32[36,8,128]{2,1,0:T(8,128)S(1)} %pad_maximum_fusion.f0, f32[36,8,128]{2,1,0:T(8,128)S(1)} %collective-permute-done.16.f1, f32[36,8,128]{2,1,0:T(8,128)S(1)} %collective-permute-done.17.f2, f32[36,8,128]{2,1,0:T(8,128)S(1)} %collective-permute-done.18.f3), custom_call_target="tpu_custom_call" | custom-call | tf_op jit(solution)/shard_map/pallas_call | solution.py:377
  (28 shorter events, 0.4 us)
Async XLA Ops:
  2.4 1.3 %collective-permute-start.1 = (f32[4,2,1536]{2,1,0:T(2,128)S(1)}, f32[4,2,1536]{2,1,0:T(2,128)S(1)}, u32[]{:S(2)}, u32[]{:S(2)}) collective-permute-start(f32[4,2,1536]{2,1,0:T(2,128)S(1)} %get-tuple-element.20), channel_id=1, source_target_pairs={{0,8},{8,0},{16,24},{24,16},{32,40},{40,32},{48,56},{56,48},{64,72... | collective-permute-start | bytes 147464 | tf_op jit(solution)/shard_map/ppermute | solution.py:322
  2.5 11.3 %collective-permute-start = (f32[7,8,1536]{2,1,0:T(8,128)S(1)}, f32[7,8,1536]{2,1,0:T(8,128)S(1)}, u32[]{:S(2)}, u32[]{:S(2)}) collective-permute-start(f32[7,8,1536]{2,1,0:T(8,128)S(1)} %get-tuple-element.17), channel_id=1, source_target_pairs={{0,8},{8,0},{16,24},{24,16},{32,40},{40,32},{48,56},{56,48},{64,72... | collective-permute-start | bytes 1032200 | tf_op jit(solution)/shard_map/ppermute | solution.py:322
  3.8 10.0 %collective-permute-start.2 = (f32[7,2,1536]{2,1,0:T(2,128)S(1)}, f32[7,2,1536]{2,1,0:T(2,128)S(1)}, u32[]{:S(2)}, u32[]{:S(2)}) collective-permute-start(f32[7,2,1536]{2,1,0:T(2,128)S(1)} %pad_maximum_fusion.4.mine), channel_id=1, source_target_pairs={{8,1},{9,2},{10,3},{11,4},{12,5},{13,6},{14,7},{15,0},{24,17},{25,... | collective-permute-start | bytes 258056 | tf_op jit(solution)/shard_map/ppermute | solution.py:327
  14.6 7.3 %collective-permute-start.3 = (f32[37,8,128]{2,1,0:T(8,128)S(1)}, f32[37,8,128]{2,1,0:T(8,128)S(1)}, u32[]{:S(2)}, u32[]{:S(2)}) collective-permute-start(f32[37,8,128]{2,1,0:T(8,128)S(1)} %get-tuple-element.22), channel_id=1, source_target_pairs={{0,32},{1,193},{2,34},{3,195},{4,36},{5,197},{6,38},{7,199},{8,200... | collective-permute-start | bytes 454664 | tf_op jit(solution)/shard_map/ppermute | solution.py:310
  18.7 5.5 %collective-permute-start.4 = (f32[37,8,128]{2,1,0:T(8,128)S(1)}, f32[37,8,128]{2,1,0:T(8,128)S(1)}, u32[]{:S(2)}, u32[]{:S(2)}) collective-permute-start(f32[37,8,128]{2,1,0:T(8,128)S(1)} %get-tuple-element.23), channel_id=1, source_target_pairs={{0,16},{1,129},{2,18},{3,131},{4,20},{5,133},{6,22},{7,135},{8,136... | collective-permute-start | bytes 454664 | tf_op jit(solution)/shard_map/ppermute | solution.py:310
  19.4 6.4 %collective-permute-start.5 = (f32[37,8,128]{2,1,0:T(8,128)S(1)}, f32[37,8,128]{2,1,0:T(8,128)S(1)}, u32[]{:S(2)}, u32[]{:S(2)}) collective-permute-start(f32[37,8,128]{2,1,0:T(8,128)S(1)} %get-tuple-element.24), channel_id=1, source_target_pairs={{0,48},{1,65},{2,50},{3,67},{4,52},{5,69},{6,54},{7,71},{8,72},{9,... | collective-permute-start | bytes 454664 | tf_op jit(solution)/shard_map/ppermute | solution.py:310
  25.8 7.2 %collective-permute-start.6 = (f32[37,8,128]{2,1,0:T(8,128)S(1)}, f32[37,8,128]{2,1,0:T(8,128)S(1)}, u32[]{:S(2)}, u32[]{:S(2)}) collective-permute-start(f32[37,8,128]{2,1,0:T(8,128)S(1)} %get-tuple-element.65), channel_id=1, source_target_pairs={{0,192},{1,33},{2,194},{3,35},{4,196},{5,37},{6,198},{7,39},{8,40}... | collective-permute-start | bytes 454664 | tf_op jit(solution)/shard_map/ppermute | solution.py:310
  29.1 8.7 %collective-permute-start.7 = (f32[37,8,128]{2,1,0:T(8,128)S(1)}, f32[37,8,128]{2,1,0:T(8,128)S(1)}, u32[]{:S(2)}, u32[]{:S(2)}) collective-permute-start(f32[37,8,128]{2,1,0:T(8,128)S(1)} %get-tuple-element.67), channel_id=1, source_target_pairs={{0,128},{1,17},{2,130},{3,19},{4,132},{5,21},{6,134},{7,23},{8,24}... | collective-permute-start | bytes 454664 | tf_op jit(solution)/shard_map/ppermute | solution.py:310
  29.8 7.9 %collective-permute-start.8 = (f32[37,8,128]{2,1,0:T(8,128)S(1)}, f32[37,8,128]{2,1,0:T(8,128)S(1)}, u32[]{:S(2)}, u32[]{:S(2)}) collective-permute-start(f32[37,8,128]{2,1,0:T(8,128)S(1)} %get-tuple-element.66), channel_id=1, source_target_pairs={{0,64},{1,49},{2,66},{3,51},{4,68},{5,53},{6,70},{7,55},{8,56},{9,... | collective-permute-start | bytes 454664 | tf_op jit(solution)/shard_map/ppermute | solution.py:310
  30.3 8.0 %collective-permute-start.9 = (f32[37,8,128]{2,1,0:T(8,128)S(1)}, f32[37,8,128]{2,1,0:T(8,128)S(1)}, u32[]{:S(2)}, u32[]{:S(2)}) collective-permute-start(f32[37,8,128]{2,1,0:T(8,128)S(1)} %get-tuple-element.29.m0), channel_id=1, source_target_pairs={{0,8},{8,0},{16,24},{24,16},{32,40},{40,32},{48,56},{56,48},{64,72... | collective-permute-start | bytes 454664 | tf_op jit(solution)/shard_map/ppermute | solution.py:322
  33.0 5.3 %collective-permute-start.10 = (f32[37,8,128]{2,1,0:T(8,128)S(1)}, f32[37,8,128]{2,1,0:T(8,128)S(1)}, u32[]{:S(2)}, u32[]{:S(2)}) collective-permute-start(f32[37,8,128]{2,1,0:T(8,128)S(1)} %collective-permute-done.6.m1), channel_id=1, source_target_pairs={{0,8},{8,0},{16,24},{24,16},{32,40},{40,32},{48,56},{56,48},{64,72... | collective-permute-start | bytes 454664 | tf_op jit(solution)/shard_map/ppermute | solution.py:322
  37.7 1.4 %collective-permute-start.11 = (f32[37,8,128]{2,1,0:T(8,128)S(1)}, f32[37,8,128]{2,1,0:T(8,128)S(1)}, u32[]{:S(2)}, u32[]{:S(2)}) collective-permute-start(f32[37,8,128]{2,1,0:T(8,128)S(1)} %collective-permute-done.7.m2), channel_id=1, source_target_pairs={{0,8},{8,0},{16,24},{24,16},{32,40},{40,32},{48,56},{56,48},{64,72... | collective-permute-start | bytes 454664 | tf_op jit(solution)/shard_map/ppermute | solution.py:322
  37.7 1.6 %collective-permute-start.12 = (f32[37,8,128]{2,1,0:T(8,128)S(1)}, f32[37,8,128]{2,1,0:T(8,128)S(1)}, u32[]{:S(2)}, u32[]{:S(2)}) collective-permute-start(f32[37,8,128]{2,1,0:T(8,128)S(1)} %collective-permute-done.8.m3), channel_id=1, source_target_pairs={{0,8},{8,0},{16,24},{24,16},{32,40},{40,32},{48,56},{56,48},{64,72... | collective-permute-start | bytes 454664 | tf_op jit(solution)/shard_map/ppermute | solution.py:322
  40.2 6.7 %collective-permute-start.13 = (f32[36,8,128]{2,1,0:T(8,128)S(1)}, f32[36,8,128]{2,1,0:T(8,128)S(1)}, u32[]{:S(2)}, u32[]{:S(2)}) collective-permute-start(f32[36,8,128]{2,1,0:T(8,128)S(1)} %get-tuple-element.26), channel_id=1, source_target_pairs={{0,32},{1,193},{2,34},{3,195},{4,36},{5,197},{6,38},{7,199},{8,200... | collective-permute-start | bytes 442376 | tf_op jit(solution)/shard_map/ppermute | solution.py:310
  41.6 5.4 %collective-permute-start.14 = (f32[36,8,128]{2,1,0:T(8,128)S(1)}, f32[36,8,128]{2,1,0:T(8,128)S(1)}, u32[]{:S(2)}, u32[]{:S(2)}) collective-permute-start(f32[36,8,128]{2,1,0:T(8,128)S(1)} %get-tuple-element.27), channel_id=1, source_target_pairs={{0,16},{1,129},{2,18},{3,131},{4,20},{5,133},{6,22},{7,135},{8,136... | collective-permute-start | bytes 442376 | tf_op jit(solution)/shard_map/ppermute | solution.py:310
  42.2 6.4 %collective-permute-start.15 = (f32[36,8,128]{2,1,0:T(8,128)S(1)}, f32[36,8,128]{2,1,0:T(8,128)S(1)}, u32[]{:S(2)}, u32[]{:S(2)}) collective-permute-start(f32[36,8,128]{2,1,0:T(8,128)S(1)} %get-tuple-element.28), channel_id=1, source_target_pairs={{0,48},{1,65},{2,50},{3,67},{4,52},{5,69},{6,54},{7,71},{8,72},{9,... | collective-permute-start | bytes 442376 | tf_op jit(solution)/shard_map/ppermute | solution.py:310
  48.6 7.1 %collective-permute-start.18 = (f32[36,8,128]{2,1,0:T(8,128)S(1)}, f32[36,8,128]{2,1,0:T(8,128)S(1)}, u32[]{:S(2)}, u32[]{:S(2)}) collective-permute-start(f32[36,8,128]{2,1,0:T(8,128)S(1)} %pad_maximum_fusion.3), channel_id=1, source_target_pairs={{0,192},{1,33},{2,194},{3,35},{4,196},{5,37},{6,198},{7,39},{8,40}... | collective-permute-start | bytes 442376 | tf_op jit(solution)/shard_map/ppermute | solution.py:310
  51.6 7.2 %collective-permute-start.17 = (f32[36,8,128]{2,1,0:T(8,128)S(1)}, f32[36,8,128]{2,1,0:T(8,128)S(1)}, u32[]{:S(2)}, u32[]{:S(2)}) collective-permute-start(f32[36,8,128]{2,1,0:T(8,128)S(1)} %pad_maximum_fusion.2), channel_id=1, source_target_pairs={{0,128},{1,49},{2,130},{3,51},{4,132},{5,53},{6,134},{7,55},{8,56}... | collective-permute-start | bytes 442376 | tf_op jit(solution)/shard_map/ppermute | solution.py:310
  51.8 7.1 %collective-permute-start.16 = (f32[36,8,128]{2,1,0:T(8,128)S(1)}, f32[36,8,128]{2,1,0:T(8,128)S(1)}, u32[]{:S(2)}, u32[]{:S(2)}) collective-permute-start(f32[36,8,128]{2,1,0:T(8,128)S(1)} %pad_maximum_fusion.1), channel_id=1, source_target_pairs={{0,64},{1,17},{2,66},{3,19},{4,68},{5,21},{6,70},{7,23},{8,24},{9,... | collective-permute-start | bytes 442376 | tf_op jit(solution)/shard_map/ppermute | solution.py:310

commit v7 on v6

--- a/solution.py
+++ b/solution.py
@@ -123,7 +123,8 @@
 
     def edge(row, upper, lower):
         keep[row // 2, row % 2 : row % 2 + 1, :] = jnp.where(top, upper, lower)
-        give[row // 2, row % 2 : row % 2 + 1, :] = jnp.where(top, lower, upper)
+        if row < 6:
+            give[row // 2, row % 2 : row % 2 + 1, :] = jnp.where(top, lower, upper)
 
     zero = jnp.zeros((1, COLS), F32)
     edge(6, bed[:1], bed[end:])
@@ -339,14 +340,14 @@
     args = (depth, x_flow, y_flow, wet, elevation, roughness, ancestors)
     keep, give, kept, given, terrain = pl.pallas_call(
         first_kernel,
-        out_shape=[strip, strip, halves, halves, ground],
+        out_shape=[strip, jax.ShapeDtypeStruct((3, 2, COLS), F32), halves, halves, ground],
         in_specs=[HBM] * 7,
         out_specs=[VMEM] * 5,
         scratch_shapes=[pltpu.VMEM(v.shape, v.dtype) for v in args[:6]]
         + [pltpu.SMEM((2,), jnp.int32), pltpu.SemaphoreType.DMA((11,))],
         compiler_params=params(),
     )(*[pltpu.with_memory_space_constraint(v, pltpu.HBM) for v in args])
-    mine = jnp.concatenate([keep, other_core(give)[:3]])
+    mine = jnp.concatenate([keep, other_core(give)])
     far = other_core(given)
     arrived = next_slab(mine)
     parts = pl.pallas_call(

time: 60.6 us -> 60.6 us (level)
  no operation moved by 1% of the time
where the time goes in v7:
time: 60.6 us; the launch traced here: 59.6 us
  waiting for transfers between devices  27.2 us (45%)
  starting transfers between devices  27.1 us (45%)
  Pallas kernels  4.31 us (7%)
  between operations  0.77 us (1%)
    ppermute x12, waiting for transfers between devices, swap(): return lax.ppermute(v, ('dom', 'rows'), pairs)  22.9 us
    ppermute x12, starting transfers between devices, swap(): return lax.ppermute(v, ('dom', 'rows'), pairs)  18.8 us
    ppermute x1, starting transfers between devices, next_slab(): return lax.ppermute(v, ('dom', 'rows'), low + [(b, a) for a, b in low])  7.22 us
    ppermute x1, waiting for transfers between devices, next_slab(): return lax.ppermute(v, ('dom', 'rows'), low + [(b, a) for a, b in low])  2.63 us
    pallas_call x1, Pallas kernels, shards(): pl.pallas_call(first_kernel, out_shape=[strip, jax.ShapeDtypeStruct((3, 2...  1.79 us
    ppermute x6, waiting for transfers between devices, other_core(): return lax.ppermute(v, 'dom', [(i, i ^ 1) for i in range(32)])  1.68 us
  transfers between devices with their start and end apart: 19, of which 13 were waited for; matrix products, arithmetic and copies ran while one was open for 0% of the time, Pallas kernels for 0%

profile of v7, /device:TPU:6, one launch (start us, length us, event | category | flops | bytes accessed | tf_op | source)
XLA Modules:
  0.0 59.6 jit_solution(10706739538197791797)
XLA Ops:
  0.6 1.8 %shard_map.94 = (f32[4,2,1536]{2,1,0:T(2,128)S(1)}, f32[3,2,1536]{2,1,0:T(2,128)S(1)}, f32[7,8,1536]{2,1,0:T(8,128)S(1)}, f32[7,8,1536]{2,1,0:T(8,128)S(1)}, f32[3,8,1536]{2,1,0:T(8,128)S(1)}) custom-call(f32[2,16,1536]{2,1,0:T(8,128)} %depth_in.1, f32[2,16,1536]{2,1,0:T(8,128)} %xf_in.1, f32[2,16,1536]{2,1,0:T(8,128)} %yf_in.1, s32[2,16,1536]{2,1,0:T(8,128)} %wet_in.1, ...), custom_call_target="tpu_custom_call" | custom-call | tf_op jit(solution)/shard_map/pallas_call | solution.py:341
  2.5 0.5 collective-permute-start
  3.0 0.7 %collective-permute-done.1 = f32[3,2,1536]{2,1,0:T(2,128)S(1)} collective-permute-done((f32[3,2,1536]{2,1,0:T(2,128)S(1)}, f32[3,2,1536]{2,1,0:T(2,128)S(1)}, u32[]{:S(2)}, u32[]{:S(2)}) %collective-permute-start.1) | collective-permute-done | bytes 36896 | tf_op jit(solution)/shard_map/ppermute | solution.py:323
  3.7 7.2 %collective-permute-start.2 = (f32[7,2,1536]{2,1,0:T(2,128)S(1)}, f32[7,2,1536]{2,1,0:T(2,128)S(1)}, u32[]{:S(2)}, u32[]{:S(2)}) collective-permute-start(f32[7,2,1536]{2,1,0:T(2,128)S(1)} %constant_dynamic-update-slice_fusion.mine), channel_id=1, source_target_pairs={{8,1},{9,2},{10,3},{11,4},{12,5},{13,6},{14,7},{15,0},{24,17},{25,... | collective-permute-start | bytes 258056 | tf_op jit(solution)/shard_map/ppermute | solution.py:328
  11.0 2.6 %collective-permute-done.2.next_slab = f32[7,2,1536]{2,1,0:T(2,128)S(1)} collective-permute-done((f32[7,2,1536]{2,1,0:T(2,128)S(1)}, f32[7,2,1536]{2,1,0:T(2,128)S(1)}, u32[]{:S(2)}, u32[]{:S(2)}) %collective-permute-start.2) | collective-permute-done | bytes 86048 | tf_op jit(solution)/shard_map/ppermute | solution.py:328
  13.6 0.7 %shard_map.95 = (f32[37,8,128]{2,1,0:T(8,128)S(1)}, f32[37,8,128]{2,1,0:T(8,128)S(1)}, f32[37,8,128]{2,1,0:T(8,128)S(1)}, f32[37,8,128]{2,1,0:T(8,128)S(1)}) custom-call(f32[7,8,1536]{2,1,0:T(8,128)S(1)} %get-tuple-element.16.own, f32[7,8,1536]{2,1,0:T(8,128)S(1)} %collective-permute-done.far, f32[3,8,1536]{2,1,0:T(8,128)S(1)} %get-tuple-element.18.terrain, ...), custom_call_target="tpu_custom_call" | custom-call | tf_op jit(solution)/shard_map/pallas_call | solution.py:353
  14.3 4.4 %collective-permute-start.3 = (f32[37,8,128]{2,1,0:T(8,128)S(1)}, f32[37,8,128]{2,1,0:T(8,128)S(1)}, u32[]{:S(2)}, u32[]{:S(2)}) collective-permute-start(f32[37,8,128]{2,1,0:T(8,128)S(1)} %get-tuple-element.22), channel_id=1, source_target_pairs={{0,32},{1,193},{2,34},{3,195},{4,36},{5,197},{6,38},{7,199},{8,200... | collective-permute-start | bytes 454664 | tf_op jit(solution)/shard_map/ppermute | solution.py:311
  18.7 0.7 %collective-permute-start.4 = (f32[37,8,128]{2,1,0:T(8,128)S(1)}, f32[37,8,128]{2,1,0:T(8,128)S(1)}, u32[]{:S(2)}, u32[]{:S(2)}) collective-permute-start(f32[37,8,128]{2,1,0:T(8,128)S(1)} %get-tuple-element.23), channel_id=1, source_target_pairs={{0,16},{1,129},{2,18},{3,131},{4,20},{5,133},{6,22},{7,135},{8,136... | collective-permute-start | bytes 454664 | tf_op jit(solution)/shard_map/ppermute | solution.py:311
  19.4 0.4 collective-permute-start.5
  19.8 2.1 %collective-permute-done.3 = f32[37,8,128]{2,1,0:T(8,128)S(1)} collective-permute-done((f32[37,8,128]{2,1,0:T(8,128)S(1)}, f32[37,8,128]{2,1,0:T(8,128)S(1)}, u32[]{:S(2)}, u32[]{:S(2)}) %collective-permute-start.3) | collective-permute-done | bytes 151584 | tf_op jit(solution)/shard_map/ppermute | solution.py:311
  21.9 2.3 %collective-permute-done.4 = f32[37,8,128]{2,1,0:T(8,128)S(1)} collective-permute-done((f32[37,8,128]{2,1,0:T(8,128)S(1)}, f32[37,8,128]{2,1,0:T(8,128)S(1)}, u32[]{:S(2)}, u32[]{:S(2)}) %collective-permute-start.4) | collective-permute-done | bytes 151584 | tf_op jit(solution)/shard_map/ppermute | solution.py:311
  24.2 1.6 %collective-permute-done.5 = f32[37,8,128]{2,1,0:T(8,128)S(1)} collective-permute-done((f32[37,8,128]{2,1,0:T(8,128)S(1)}, f32[37,8,128]{2,1,0:T(8,128)S(1)}, u32[]{:S(2)}, u32[]{:S(2)}) %collective-permute-start.5) | collective-permute-done | bytes 151584 | tf_op jit(solution)/shard_map/ppermute | solution.py:311
  25.9 3.1 %collective-permute-start.6 = (f32[37,8,128]{2,1,0:T(8,128)S(1)}, f32[37,8,128]{2,1,0:T(8,128)S(1)}, u32[]{:S(2)}, u32[]{:S(2)}) collective-permute-start(f32[37,8,128]{2,1,0:T(8,128)S(1)} %get-tuple-element.65), channel_id=1, source_target_pairs={{0,192},{1,33},{2,194},{3,35},{4,196},{5,37},{6,198},{7,39},{8,40}... | collective-permute-start | bytes 454664 | tf_op jit(solution)/shard_map/ppermute | solution.py:311
  28.9 0.7 %collective-permute-start.7 = (f32[37,8,128]{2,1,0:T(8,128)S(1)}, f32[37,8,128]{2,1,0:T(8,128)S(1)}, u32[]{:S(2)}, u32[]{:S(2)}) collective-permute-start(f32[37,8,128]{2,1,0:T(8,128)S(1)} %get-tuple-element.67), channel_id=1, source_target_pairs={{0,128},{1,17},{2,130},{3,19},{4,132},{5,21},{6,134},{7,23},{8,24}... | collective-permute-start | bytes 454664 | tf_op jit(solution)/shard_map/ppermute | solution.py:311
  29.7 0.7 %collective-permute-start.8 = (f32[37,8,128]{2,1,0:T(8,128)S(1)}, f32[37,8,128]{2,1,0:T(8,128)S(1)}, u32[]{:S(2)}, u32[]{:S(2)}) collective-permute-start(f32[37,8,128]{2,1,0:T(8,128)S(1)} %get-tuple-element.66), channel_id=1, source_target_pairs={{0,64},{1,49},{2,66},{3,51},{4,68},{5,53},{6,70},{7,55},{8,56},{9,... | collective-permute-start | bytes 454664 | tf_op jit(solution)/shard_map/ppermute | solution.py:311
  30.3 2.7 %collective-permute-done.6.m1 = f32[37,8,128]{2,1,0:T(8,128)S(1)} collective-permute-done((f32[37,8,128]{2,1,0:T(8,128)S(1)}, f32[37,8,128]{2,1,0:T(8,128)S(1)}, u32[]{:S(2)}, u32[]{:S(2)}) %collective-permute-start.6) | collective-permute-done | bytes 151584 | tf_op jit(solution)/shard_map/ppermute | solution.py:311
  33.0 4.6 %collective-permute-done.7.m2 = f32[37,8,128]{2,1,0:T(8,128)S(1)} collective-permute-done((f32[37,8,128]{2,1,0:T(8,128)S(1)}, f32[37,8,128]{2,1,0:T(8,128)S(1)}, u32[]{:S(2)}, u32[]{:S(2)}) %collective-permute-start.7) | collective-permute-done | bytes 151584 | tf_op jit(solution)/shard_map/ppermute | solution.py:311
  37.6 0.5 collective-permute-start.12
  38.2 0.8 %collective-permute-done.11.t2 = f32[37,8,128]{2,1,0:T(8,128)S(1)} collective-permute-done((f32[37,8,128]{2,1,0:T(8,128)S(1)}, f32[37,8,128]{2,1,0:T(8,128)S(1)}, u32[]{:S(2)}, u32[]{:S(2)}) %collective-permute-start.11) | collective-permute-done | bytes 151584 | tf_op jit(solution)/shard_map/ppermute | solution.py:323
  39.0 0.2 collective-permute-done.12.t3
  39.2 0.9 %shard_map.96 = (f32[36,8,128]{2,1,0:T(8,128)S(1)}, f32[36,8,128]{2,1,0:T(8,128)S(1)}, f32[36,8,128]{2,1,0:T(8,128)S(1)}, f32[36,8,128]{2,1,0:T(8,128)S(1)}) custom-call(s32[128]{0:T(128)S(1)} %pad_add_fusion.codes, f32[37,8,128]{2,1,0:T(8,128)S(1)} %get-tuple-element.29.m0, f32[37,8,128]{2,1,0:T(8,128)S(1)} %collective-permute-done.6.m1, ...), custom_call_target="tpu_custom_call" | custom-call | tf_op jit(solution)/shard_map/pallas_call | solution.py:367
  40.1 1.3 %collective-permute-start.13 = (f32[36,8,128]{2,1,0:T(8,128)S(1)}, f32[36,8,128]{2,1,0:T(8,128)S(1)}, u32[]{:S(2)}, u32[]{:S(2)}) collective-permute-start(f32[36,8,128]{2,1,0:T(8,128)S(1)} %get-tuple-element.26), channel_id=1, source_target_pairs={{0,32},{1,193},{2,34},{3,195},{4,36},{5,197},{6,38},{7,199},{8,200... | collective-permute-start | bytes 442376 | tf_op jit(solution)/shard_map/ppermute | solution.py:311
  41.4 0.7 %collective-permute-start.14 = (f32[36,8,128]{2,1,0:T(8,128)S(1)}, f32[36,8,128]{2,1,0:T(8,128)S(1)}, u32[]{:S(2)}, u32[]{:S(2)}) collective-permute-start(f32[36,8,128]{2,1,0:T(8,128)S(1)} %get-tuple-element.27), channel_id=1, source_target_pairs={{0,16},{1,129},{2,18},{3,131},{4,20},{5,133},{6,22},{7,135},{8,136... | collective-permute-start | bytes 442376 | tf_op jit(solution)/shard_map/ppermute | solution.py:311
  42.1 2.2 %collective-permute-start.15 = (f32[36,8,128]{2,1,0:T(8,128)S(1)}, f32[36,8,128]{2,1,0:T(8,128)S(1)}, u32[]{:S(2)}, u32[]{:S(2)}) collective-permute-start(f32[36,8,128]{2,1,0:T(8,128)S(1)} %get-tuple-element.28), channel_id=1, source_target_pairs={{0,48},{1,65},{2,50},{3,67},{4,52},{5,69},{6,54},{7,71},{8,72},{9,... | collective-permute-start | bytes 442376 | tf_op jit(solution)/shard_map/ppermute | solution.py:311
  44.3 2.5 %collective-permute-done.13 = f32[36,8,128]{2,1,0:T(8,128)S(1)} collective-permute-done((f32[36,8,128]{2,1,0:T(8,128)S(1)}, f32[36,8,128]{2,1,0:T(8,128)S(1)}, u32[]{:S(2)}, u32[]{:S(2)}) %collective-permute-start.13) | collective-permute-done | bytes 147488 | tf_op jit(solution)/shard_map/ppermute | solution.py:311
  46.9 1.6 %collective-permute-done.15 = f32[36,8,128]{2,1,0:T(8,128)S(1)} collective-permute-done((f32[36,8,128]{2,1,0:T(8,128)S(1)}, f32[36,8,128]{2,1,0:T(8,128)S(1)}, u32[]{:S(2)}, u32[]{:S(2)}) %collective-permute-start.15) | collective-permute-done | bytes 147488 | tf_op jit(solution)/shard_map/ppermute | solution.py:311
  48.5 3.0 %collective-permute-start.18 = (f32[36,8,128]{2,1,0:T(8,128)S(1)}, f32[36,8,128]{2,1,0:T(8,128)S(1)}, u32[]{:S(2)}, u32[]{:S(2)}) collective-permute-start(f32[36,8,128]{2,1,0:T(8,128)S(1)} %pad_maximum_fusion.3), channel_id=1, source_target_pairs={{0,192},{1,33},{2,194},{3,35},{4,196},{5,37},{6,198},{7,39},{8,40}... | collective-permute-start | bytes 442376 | tf_op jit(solution)/shard_map/ppermute | solution.py:311
  51.5 0.1 collective-permute-start.17
  51.6 1.5 %collective-permute-start.16 = (f32[36,8,128]{2,1,0:T(8,128)S(1)}, f32[36,8,128]{2,1,0:T(8,128)S(1)}, u32[]{:S(2)}, u32[]{:S(2)}) collective-permute-start(f32[36,8,128]{2,1,0:T(8,128)S(1)} %pad_maximum_fusion.1), channel_id=1, source_target_pairs={{0,64},{1,17},{2,66},{3,19},{4,68},{5,21},{6,70},{7,23},{8,24},{9,... | collective-permute-start | bytes 442376 | tf_op jit(solution)/shard_map/ppermute | solution.py:311
  53.2 2.4 %collective-permute-done.18.f3 = f32[36,8,128]{2,1,0:T(8,128)S(1)} collective-permute-done((f32[36,8,128]{2,1,0:T(8,128)S(1)}, f32[36,8,128]{2,1,0:T(8,128)S(1)}, u32[]{:S(2)}, u32[]{:S(2)}) %collective-permute-start.18) | collective-permute-done | bytes 147488 | tf_op jit(solution)/shard_map/ppermute | solution.py:311
  55.5 3.1 %collective-permute-done.17.f2 = f32[36,8,128]{2,1,0:T(8,128)S(1)} collective-permute-done((f32[36,8,128]{2,1,0:T(8,128)S(1)}, f32[36,8,128]{2,1,0:T(8,128)S(1)}, u32[]{:S(2)}, u32[]{:S(2)}) %collective-permute-start.17) | collective-permute-done | bytes 147488 | tf_op jit(solution)/shard_map/ppermute | solution.py:311
  58.7 0.9 %shard_map.97 = (f32[2,16,1536]{2,1,0:T(8,128)}, f32[2,16,1536]{2,1,0:T(8,128)}, f32[2,16,1536]{2,1,0:T(8,128)}) custom-call(f32[36,8,128]{2,1,0:T(8,128)S(1)} %pad_maximum_fusion.f0, f32[36,8,128]{2,1,0:T(8,128)S(1)} %collective-permute-done.16.f1, f32[36,8,128]{2,1,0:T(8,128)S(1)} %collective-permute-done.17.f2, f32[36,8,128]{2,1,0:T(8,128)S(1)} %collective-permute-done.18.f3), custom_call_target="tpu_custom_call" | custom-call | tf_op jit(solution)/shard_map/pallas_call | solution.py:378
  (28 shorter events, 0.4 us)
Async XLA Ops:
  2.4 1.3 %collective-permute-start.1 = (f32[3,2,1536]{2,1,0:T(2,128)S(1)}, f32[3,2,1536]{2,1,0:T(2,128)S(1)}, u32[]{:S(2)}, u32[]{:S(2)}) collective-permute-start(f32[3,2,1536]{2,1,0:T(2,128)S(1)} %get-tuple-element.20), channel_id=1, source_target_pairs={{0,8},{8,0},{16,24},{24,16},{32,40},{40,32},{48,56},{56,48},{64,72... | collective-permute-start | bytes 110600 | tf_op jit(solution)/shard_map/ppermute | solution.py:323
  2.5 11.1 %collective-permute-start = (f32[7,8,1536]{2,1,0:T(8,128)S(1)}, f32[7,8,1536]{2,1,0:T(8,128)S(1)}, u32[]{:S(2)}, u32[]{:S(2)}) collective-permute-start(f32[7,8,1536]{2,1,0:T(8,128)S(1)} %get-tuple-element.17), channel_id=1, source_target_pairs={{0,8},{8,0},{16,24},{24,16},{32,40},{40,32},{48,56},{56,48},{64,72... | collective-permute-start | bytes 1032200 | tf_op jit(solution)/shard_map/ppermute | solution.py:323
  3.7 9.9 %collective-permute-start.2 = (f32[7,2,1536]{2,1,0:T(2,128)S(1)}, f32[7,2,1536]{2,1,0:T(2,128)S(1)}, u32[]{:S(2)}, u32[]{:S(2)}) collective-permute-start(f32[7,2,1536]{2,1,0:T(2,128)S(1)} %constant_dynamic-update-slice_fusion.mine), channel_id=1, source_target_pairs={{8,1},{9,2},{10,3},{11,4},{12,5},{13,6},{14,7},{15,0},{24,17},{25,... | collective-permute-start | bytes 258056 | tf_op jit(solution)/shard_map/ppermute | solution.py:328
  14.3 7.6 %collective-permute-start.3 = (f32[37,8,128]{2,1,0:T(8,128)S(1)}, f32[37,8,128]{2,1,0:T(8,128)S(1)}, u32[]{:S(2)}, u32[]{:S(2)}) collective-permute-start(f32[37,8,128]{2,1,0:T(8,128)S(1)} %get-tuple-element.22), channel_id=1, source_target_pairs={{0,32},{1,193},{2,34},{3,195},{4,36},{5,197},{6,38},{7,199},{8,200... | collective-permute-start | bytes 454664 | tf_op jit(solution)/shard_map/ppermute | solution.py:311
  18.7 5.5 %collective-permute-start.4 = (f32[37,8,128]{2,1,0:T(8,128)S(1)}, f32[37,8,128]{2,1,0:T(8,128)S(1)}, u32[]{:S(2)}, u32[]{:S(2)}) collective-permute-start(f32[37,8,128]{2,1,0:T(8,128)S(1)} %get-tuple-element.23), channel_id=1, source_target_pairs={{0,16},{1,129},{2,18},{3,131},{4,20},{5,133},{6,22},{7,135},{8,136... | collective-permute-start | bytes 454664 | tf_op jit(solution)/shard_map/ppermute | solution.py:311
  19.4 6.4 %collective-permute-start.5 = (f32[37,8,128]{2,1,0:T(8,128)S(1)}, f32[37,8,128]{2,1,0:T(8,128)S(1)}, u32[]{:S(2)}, u32[]{:S(2)}) collective-permute-start(f32[37,8,128]{2,1,0:T(8,128)S(1)} %get-tuple-element.24), channel_id=1, source_target_pairs={{0,48},{1,65},{2,50},{3,67},{4,52},{5,69},{6,54},{7,71},{8,72},{9,... | collective-permute-start | bytes 454664 | tf_op jit(solution)/shard_map/ppermute | solution.py:311
  25.9 7.2 %collective-permute-start.6 = (f32[37,8,128]{2,1,0:T(8,128)S(1)}, f32[37,8,128]{2,1,0:T(8,128)S(1)}, u32[]{:S(2)}, u32[]{:S(2)}) collective-permute-start(f32[37,8,128]{2,1,0:T(8,128)S(1)} %get-tuple-element.65), channel_id=1, source_target_pairs={{0,192},{1,33},{2,194},{3,35},{4,196},{5,37},{6,198},{7,39},{8,40}... | collective-permute-start | bytes 454664 | tf_op jit(solution)/shard_map/ppermute | solution.py:311
  28.9 8.7 %collective-permute-start.7 = (f32[37,8,128]{2,1,0:T(8,128)S(1)}, f32[37,8,128]{2,1,0:T(8,128)S(1)}, u32[]{:S(2)}, u32[]{:S(2)}) collective-permute-start(f32[37,8,128]{2,1,0:T(8,128)S(1)} %get-tuple-element.67), channel_id=1, source_target_pairs={{0,128},{1,17},{2,130},{3,19},{4,132},{5,21},{6,134},{7,23},{8,24}... | collective-permute-start | bytes 454664 | tf_op jit(solution)/shard_map/ppermute | solution.py:311
  29.7 7.9 %collective-permute-start.8 = (f32[37,8,128]{2,1,0:T(8,128)S(1)}, f32[37,8,128]{2,1,0:T(8,128)S(1)}, u32[]{:S(2)}, u32[]{:S(2)}) collective-permute-start(f32[37,8,128]{2,1,0:T(8,128)S(1)} %get-tuple-element.66), channel_id=1, source_target_pairs={{0,64},{1,49},{2,66},{3,51},{4,68},{5,53},{6,70},{7,55},{8,56},{9,... | collective-permute-start | bytes 454664 | tf_op jit(solution)/shard_map/ppermute | solution.py:311
  30.3 7.9 %collective-permute-start.9 = (f32[37,8,128]{2,1,0:T(8,128)S(1)}, f32[37,8,128]{2,1,0:T(8,128)S(1)}, u32[]{:S(2)}, u32[]{:S(2)}) collective-permute-start(f32[37,8,128]{2,1,0:T(8,128)S(1)} %get-tuple-element.29.m0), channel_id=1, source_target_pairs={{0,8},{8,0},{16,24},{24,16},{32,40},{40,32},{48,56},{56,48},{64,72... | collective-permute-start | bytes 454664 | tf_op jit(solution)/shard_map/ppermute | solution.py:323
  33.0 5.2 %collective-permute-start.10 = (f32[37,8,128]{2,1,0:T(8,128)S(1)}, f32[37,8,128]{2,1,0:T(8,128)S(1)}, u32[]{:S(2)}, u32[]{:S(2)}) collective-permute-start(f32[37,8,128]{2,1,0:T(8,128)S(1)} %collective-permute-done.6.m1), channel_id=1, source_target_pairs={{0,8},{8,0},{16,24},{24,16},{32,40},{40,32},{48,56},{56,48},{64,72... | collective-permute-start | bytes 454664 | tf_op jit(solution)/shard_map/ppermute | solution.py:323
  37.6 1.4 %collective-permute-start.11 = (f32[37,8,128]{2,1,0:T(8,128)S(1)}, f32[37,8,128]{2,1,0:T(8,128)S(1)}, u32[]{:S(2)}, u32[]{:S(2)}) collective-permute-start(f32[37,8,128]{2,1,0:T(8,128)S(1)} %collective-permute-done.7.m2), channel_id=1, source_target_pairs={{0,8},{8,0},{16,24},{24,16},{32,40},{40,32},{48,56},{56,48},{64,72... | collective-permute-start | bytes 454664 | tf_op jit(solution)/shard_map/ppermute | solution.py:323
  37.6 1.6 %collective-permute-start.12 = (f32[37,8,128]{2,1,0:T(8,128)S(1)}, f32[37,8,128]{2,1,0:T(8,128)S(1)}, u32[]{:S(2)}, u32[]{:S(2)}) collective-permute-start(f32[37,8,128]{2,1,0:T(8,128)S(1)} %collective-permute-done.8.m3), channel_id=1, source_target_pairs={{0,8},{8,0},{16,24},{24,16},{32,40},{40,32},{48,56},{56,48},{64,72... | collective-permute-start | bytes 454664 | tf_op jit(solution)/shard_map/ppermute | solution.py:323
  40.1 6.7 %collective-permute-start.13 = (f32[36,8,128]{2,1,0:T(8,128)S(1)}, f32[36,8,128]{2,1,0:T(8,128)S(1)}, u32[]{:S(2)}, u32[]{:S(2)}) collective-permute-start(f32[36,8,128]{2,1,0:T(8,128)S(1)} %get-tuple-element.26), channel_id=1, source_target_pairs={{0,32},{1,193},{2,34},{3,195},{4,36},{5,197},{6,38},{7,199},{8,200... | collective-permute-start | bytes 442376 | tf_op jit(solution)/shard_map/ppermute | solution.py:311
  41.4 5.4 %collective-permute-start.14 = (f32[36,8,128]{2,1,0:T(8,128)S(1)}, f32[36,8,128]{2,1,0:T(8,128)S(1)}, u32[]{:S(2)}, u32[]{:S(2)}) collective-permute-start(f32[36,8,128]{2,1,0:T(8,128)S(1)} %get-tuple-element.27), channel_id=1, source_target_pairs={{0,16},{1,129},{2,18},{3,131},{4,20},{5,133},{6,22},{7,135},{8,136... | collective-permute-start | bytes 442376 | tf_op jit(solution)/shard_map/ppermute | solution.py:311
  42.1 6.4 %collective-permute-start.15 = (f32[36,8,128]{2,1,0:T(8,128)S(1)}, f32[36,8,128]{2,1,0:T(8,128)S(1)}, u32[]{:S(2)}, u32[]{:S(2)}) collective-permute-start(f32[36,8,128]{2,1,0:T(8,128)S(1)} %get-tuple-element.28), channel_id=1, source_target_pairs={{0,48},{1,65},{2,50},{3,67},{4,52},{5,69},{6,54},{7,71},{8,72},{9,... | collective-permute-start | bytes 442376 | tf_op jit(solution)/shard_map/ppermute | solution.py:311
  48.5 7.1 %collective-permute-start.18 = (f32[36,8,128]{2,1,0:T(8,128)S(1)}, f32[36,8,128]{2,1,0:T(8,128)S(1)}, u32[]{:S(2)}, u32[]{:S(2)}) collective-permute-start(f32[36,8,128]{2,1,0:T(8,128)S(1)} %pad_maximum_fusion.3), channel_id=1, source_target_pairs={{0,192},{1,33},{2,194},{3,35},{4,196},{5,37},{6,198},{7,39},{8,40}... | collective-permute-start | bytes 442376 | tf_op jit(solution)/shard_map/ppermute | solution.py:311
  51.5 7.2 %collective-permute-start.17 = (f32[36,8,128]{2,1,0:T(8,128)S(1)}, f32[36,8,128]{2,1,0:T(8,128)S(1)}, u32[]{:S(2)}, u32[]{:S(2)}) collective-permute-start(f32[36,8,128]{2,1,0:T(8,128)S(1)} %pad_maximum_fusion.2), channel_id=1, source_target_pairs={{0,128},{1,49},{2,130},{3,51},{4,132},{5,53},{6,134},{7,55},{8,56}... | collective-permute-start | bytes 442376 | tf_op jit(solution)/shard_map/ppermute | solution.py:311
  51.6 7.1 %collective-permute-start.16 = (f32[36,8,128]{2,1,0:T(8,128)S(1)}, f32[36,8,128]{2,1,0:T(8,128)S(1)}, u32[]{:S(2)}, u32[]{:S(2)}) collective-permute-start(f32[36,8,128]{2,1,0:T(8,128)S(1)} %pad_maximum_fusion.1), channel_id=1, source_target_pairs={{0,64},{1,17},{2,66},{3,19},{4,68},{5,21},{6,70},{7,23},{8,24},{9,... | collective-permute-start | bytes 442376 | tf_op jit(solution)/shard_map/ppermute | solution.py:311
